TPU v7x, 32 devices: a whole 2x2x4 slice. The times are simulated.
32 devices in a mesh: groups: 2 (over x), dom: 16 (over z, y, core).
Axes of the slice: x: 2, y: 2, z: 4, core: 2. Of those that a mesh axis runs over, the one named last changes fastest.
Arguments:
- nodes: bfloat16 [4096, 256], P(('groups', 'dom')), parts along dimension 0, may hold values from -6 to 6
- cotangent: bfloat16 [4096, 256], P(('groups', 'dom')), parts along dimension 0, may hold values from -6 to 6
- fine_weights: bfloat16 [3, 256, 256], replicated, may hold values from -0.375 to 0.375
- coarse_weights: bfloat16 [3, 256, 256], replicated, may hold values from -0.375 to 0.375
- biases: float32 [2, 256], replicated, may hold values from -4 to 4
- send_lists: int32 [4, 256], P('groups', 'dom'), parts along dimension 0, may hold values from 0 to 127
- edge_ends: int32 [4, 24576], P('groups', 'dom'), parts along dimension 0, may hold values from 0 to 159, as said below
- live_blocks: int32 [32], P(('groups', 'dom')), parts along dimension 0, may hold values from 4 to 12, as said below
- pool_members: int32 [16, 256], P('groups', 'dom'), parts along dimension 0, may hold values from 0 to 127
- parents: int32 [4096], P(('groups', 'dom')), parts along dimension 0, may hold values from 0 to 15
- coarse_ends: int32 [4, 768], P('groups', 'dom'), parts along dimension 0, may hold values from 0 to 255
Outputs:
- moved_nodes: float32 [4096, 256], P(('groups', 'dom')), parts along dimension 0
- node_grads: float32 [4096, 256], P(('groups', 'dom')), parts along dimension 0
- fine_grads: float32 [6, 256, 256], P('groups'), parts along dimension 0
- coarse_grads: float32 [6, 256, 256], P('groups'), parts along dimension 0
- bias_grads: float32 [4, 256], P('groups'), parts along dimension 0
There are 2 independent parts, one for each index of `groups`. A program takes and returns all parts, laid end to end along the dimension named above; an argument that names none is the same for every part. Nothing has to cross between parts.
Inputs may be any that keep to these rules, and one draw needn't show every extreme that they name: `edge_ends`: row 0 indexes the partition's extended table and never a row that is zeros; row 1 indexes a local node. `live_blocks`: some partition has all 12 blocks live.
All inputs are finite; a program needn't handle non-finite values.
Results may differ from a plain program's by a relative error of at most 0.0061.
Values may be sent and summed in bfloat16 or wider, within the bound.
No kernel may reach another device: no remote copies, remote signals or barrier semaphores. Data moves between devices by JAX's collectives and lax.ppermute only.
A program may use at most 64 MiB of HBM per device.

v0:
```python
import jax
import jax.numpy as jnp
from jax import lax
from jax.sharding import PartitionSpec as P


def padded(block, sides, width):
    for axis, dim in sides:
        count = lax.axis_size(axis)
        forward = [(i, i + 1) for i in range(count - 1)]
        backward = [(target, source) for source, target in forward]
        low = lax.ppermute(
            lax.slice_in_dim(block, block.shape[dim] - width, None, axis=dim), axis, forward
        )
        high = lax.ppermute(lax.slice_in_dim(block, 0, width, axis=dim), axis, backward)
        block = jnp.concatenate([low, block, high], axis=dim)
    return block


def silu_slope(value):
    sig = jax.nn.sigmoid(value)
    return sig * (1.0 + value * (1.0 - sig))


def precise_dot(left, right):
    return jnp.dot(left, right, precision=lax.Precision.HIGHEST)


def segment_rows(values, index, count):
    return jax.ops.segment_sum(values, index, count)


def shards(
    nodes,
    cotangent,
    fine_weights,
    coarse_weights,
    biases,
    send_lists,
    edge_ends,
    live_blocks,
    pool_members,
    parents,
    coarse_ends,
):
    node_count, width = nodes.shape
    rim_rows = send_lists.shape[1]
    member_count = pool_members.shape[0]
    coarse_count = pool_members.shape[1]
    edge_slots = edge_ends.shape[1]
    fine_src, fine_dst, fine_out = (fine_weights[0], fine_weights[1], fine_weights[2])
    coarse_src, coarse_dst, coarse_out = (coarse_weights[0], coarse_weights[1], coarse_weights[2])
    outgoing = jnp.concatenate([nodes[send_lists[0]], nodes[send_lists[1]]], 0)
    widened = padded(outgoing, (("dom", 0),), rim_rows)
    extended = jnp.concatenate([widened[:rim_rows], nodes, widened[3 * rim_rows :]], 0)
    src_proj = jnp.dot(extended, fine_src, preferred_element_type=jnp.float32).astype(jnp.bfloat16)
    dst_proj = jnp.dot(nodes, fine_dst, preferred_element_type=jnp.float32).astype(jnp.bfloat16)
    senders, receivers = (edge_ends[0], edge_ends[1])
    live_mask = (jnp.arange(edge_slots) // 128 < live_blocks[0]).astype(jnp.float32)[:, None]
    pre_act = (
        src_proj[senders].astype(jnp.float32) + dst_proj[receivers].astype(jnp.float32) + biases[0]
    )
    messages = jax.nn.silu(pre_act) * live_mask
    summed = segment_rows(messages, receivers, node_count).astype(jnp.bfloat16)
    updated = nodes.astype(jnp.float32) + jnp.dot(
        summed, fine_out, preferred_element_type=jnp.float32
    )
    pooled = jnp.sum(updated[pool_members], 0)
    coarse_own = (pooled / member_count).astype(jnp.bfloat16)
    links = lax.all_gather(coarse_ends, "dom", axis=1, tiled=True)
    senders2, receivers2 = (links[0], links[1])
    own_start = lax.axis_index("dom") * coarse_count
    coarse_all = lax.all_gather(coarse_own, "dom", axis=0, tiled=True)
    src2 = jnp.dot(coarse_all, coarse_src, preferred_element_type=jnp.float32).astype(jnp.bfloat16)
    dst2 = jnp.dot(coarse_all, coarse_dst, preferred_element_type=jnp.float32).astype(jnp.bfloat16)
    total = src2.shape[0]
    pre2 = src2[senders2].astype(jnp.float32) + dst2[receivers2].astype(jnp.float32) + biases[1]
    part_sum = segment_rows(jax.nn.silu(pre2), receivers2, total)
    coarse_sum = part_sum.astype(jnp.bfloat16)
    coarse_whole = coarse_all.astype(jnp.float32) + jnp.dot(
        coarse_sum, coarse_out, preferred_element_type=jnp.float32
    )
    coarse_new = lax.dynamic_slice_in_dim(coarse_whole, own_start, coarse_count, 0)
    moved = updated + coarse_new[parents]
    upstream = cotangent.astype(jnp.float32)
    parent_grad = segment_rows(upstream, parents, coarse_count).astype(jnp.bfloat16)
    parent_own = parent_grad.astype(jnp.float32)
    parent_all = lax.all_gather(parent_grad, "dom", axis=0, tiled=True).astype(jnp.float32)
    grad_agg2 = precise_dot(parent_all, coarse_out.astype(jnp.float32).T)
    slope2 = grad_agg2[receivers2] * silu_slope(pre2)
    bias2 = jnp.sum(slope2, 0)
    grad_src2 = segment_rows(slope2, senders2, total)
    grad_dst2 = segment_rows(slope2, receivers2, total)
    coarse_f32 = coarse_all.astype(jnp.float32)
    grad_s2 = precise_dot(coarse_f32.T, grad_src2)
    grad_r2 = precise_dot(coarse_f32.T, grad_dst2)
    back_terms = precise_dot(grad_src2, coarse_src.astype(jnp.float32).T) + precise_dot(
        grad_dst2, coarse_dst.astype(jnp.float32).T
    )
    grad_out2 = precise_dot(coarse_sum.astype(jnp.float32).T, parent_all)
    coarse_grad = parent_own + lax.dynamic_slice_in_dim(back_terms, own_start, coarse_count, 0)
    spread = jnp.broadcast_to(
        (coarse_grad / member_count)[None], (member_count, coarse_count, width)
    ).reshape(-1, width)
    grad_updated = upstream + segment_rows(spread, pool_members.reshape(-1), node_count)
    grad_u = precise_dot(summed.astype(jnp.float32).T, grad_updated)
    grad_summed = precise_dot(grad_updated, fine_out.astype(jnp.float32).T)
    slope = grad_summed[receivers] * live_mask * silu_slope(pre_act)
    bias1 = jnp.sum(slope, 0)
    grad_src = segment_rows(slope, senders, node_count + 2 * rim_rows)
    grad_dst = segment_rows(slope, receivers, node_count)
    grad_s = precise_dot(extended.astype(jnp.float32).T, grad_src)
    grad_r = precise_dot(nodes.astype(jnp.float32).T, grad_dst)
    grad_ext = precise_dot(grad_src, fine_src.astype(jnp.float32).T)
    returning = jnp.concatenate([grad_ext[:rim_rows], grad_ext[node_count + rim_rows :]], 0)
    arrived = padded(returning.astype(jnp.bfloat16), (("dom", 0),), rim_rows).astype(
        returning.dtype
    )
    node_grads = (
        grad_updated
        + grad_ext[rim_rows : rim_rows + node_count]
        + precise_dot(grad_dst, fine_dst.astype(jnp.float32).T)
    )
    node_grads = node_grads + segment_rows(arrived[:rim_rows], send_lists[0], node_count)
    node_grads = node_grads + segment_rows(arrived[3 * rim_rows :], send_lists[1], node_count)
    grad_s, grad_r, grad_u, bias1 = lax.psum((grad_s, grad_r, grad_u, bias1), "dom")
    return (
        moved,
        node_grads,
        jnp.stack([grad_s, grad_r, grad_u]),
        jnp.stack([grad_s2, grad_r2, grad_out2]),
        jnp.stack([bias1, bias2]),
    )


def solution(mesh):
    return jax.shard_map(
        shards,
        mesh=mesh,
        in_specs=(
            P(("groups", "dom"), None),
            P(("groups", "dom"), None),
            P(),
            P(),
            P(),
            P("groups", "dom"),
            P("groups", "dom"),
            P(("groups", "dom")),
            P("groups", "dom"),
            P(("groups", "dom")),
            P("groups", "dom"),
        ),
        out_specs=(
            P(("groups", "dom"), None),
            P(("groups", "dom"), None),
            P("groups", None, None),
            P("groups", None, None),
            P("groups", None),
        ),
        check_vma=False,
    )
```

profile of v0, /device:TPU:0, one launch (start us, length us, event | category | flops | bytes accessed | tf_op | source)
XLA Modules:
  0.0 280.7 jit_solution(1800031173504668396)
XLA Ops:
  8.0 1.4 gather_fusion
  9.4 2.4 collective-permute-start
  11.8 1.4 gather_fusion.1
  13.2 1.3 collective-permute-start.1
  15.3 25.2 %all-gather = s32[16,48,2]{1,2,0:T(2,128)S(1)} all-gather(s32[1,48,2]{1,2,0:T(2,128)} %bitcast.112), channel_id=1, replica_groups=mesh['groups'=2,'dom'=16] {'dom'}, dimensions={0}, use_global_device_ids=true | all-gather | bytes 6528 | tf_op jit(solution)/shard_map/all_gather | solution.py:70
  41.3 0.8 fusion.69
  42.1 1.4 slice_reduce_fusion
  44.8 1.3 fusion.78
  46.9 1.6 scatter_custom_fusion.2
  49.1 1.1 convolution_convert_fusion.3
  50.2 17.8 %all_gather.11 = bf16[256,256]{1,0:T(8,128)(2,1)S(1)} all-gather(bf16[16,256]{1,0:T(8,128)(2,1)S(1)} %convert_element_type.86), channel_id=1, replica_groups=mesh['groups'=2,'dom'=16] {'dom'}, dimensions={0}, use_global_device_ids=true | all-gather | bytes 139264 | tf_op jit(solution)/shard_map/all_gather | solution.py:88
  68.6 1.1 fusion.10
  70.3 1.4 reshape.320
  71.7 0.8 convert_element_type.85
  72.6 2.9 %gather_fusion.8 = f32[768,256]{1,0:T(8,128)} fusion(f32[256,256]{1,0:T(8,128)S(1)} %fusion.10, s32[1024]{0:T(1024)S(1)} %get-tuple-element.35), kind=kCustom, calls=%fused_computation.8 | custom fusion | bytes 1575936 | tf_op jit(solution)/shard_map/gather | solution.py:90
  75.5 4.8 %gather_fusion.3 = bf16[1536,256]{1,0:T(8,128)(2,1)S(1)} fusion(bf16[128,256]{1,0:T(8,128)(2,1)S(1)} %convolution_convert_fusion.3, s32[2048]{0:T(1024)S(1)} %get-tuple-element.32), kind=kCustom, calls=%fused_computation.3 | custom fusion | bytes 1579008 | tf_op jit(solution)/shard_map/gather | solution.py:61
  81.0 4.8 %gather_fusion.2 = bf16[1536,256]{1,0:T(8,128)(2,1)S(1)} fusion(bf16[160,256]{1,0:T(8,128)(2,1)S(1)} %convolution_convert_fusion.2, s32[2048]{0:T(1024)S(1)} %get-tuple-element.33), kind=kCustom, calls=%fused_computation.2 | custom fusion | bytes 1579008 | tf_op jit(solution)/shard_map/gather | solution.py:61
  85.8 10.0 %scatter_custom_fusion = f32[128,256]{1,0:T(8,128)S(1)} fusion(s32[1536]{0:T(1024)S(1)} %get-tuple-element.6, bf16[1536,256]{1,0:T(8,128)(2,1)S(1)} %gather_fusion.3, bf16[1536,256]{1,0:T(8,128)(2,1)S(1)} %gather_fusion.2, f32[1536]{0:T(1024)S(1)} %fusion.68, f32[]{:T(128)} %constant.19.clone.1, f32[256]{0:T(256)S(1)} %bitcast.106, f32[]{:T(128)} %constant.15.clone.1), kind=kCustom, calls=%fused_computation.20 | custom fusion | flops 3932160 | bytes 1713160 | tf_op jit(solution)/shard_map/scatter-add | solution.py:30
  96.7 19.1 %all_gather.9 = bf16[256,256]{1,0:T(8,128)(2,1)S(1)} all-gather(bf16[16,256]{1,0:T(8,128)(2,1)S(1)} %multiply_convert_fusion), channel_id=1, replica_groups=mesh['groups'=2,'dom'=16] {'dom'}, dimensions={0}, use_global_device_ids=true | all-gather | bytes 139264 | tf_op jit(solution)/shard_map/all_gather | solution.py:73
  116.3 2.7 gather_fusion.6
  118.9 2.8 gather_fusion.5
  121.7 6.3 %scatter_custom_fusion.1 = f32[256,256]{1,0:T(8,128)S(1)} fusion(s32[768]{0:T(1024)} %get-tuple-element.10, bf16[768,256]{1,0:T(8,128)(2,1)S(1)} %gather_fusion.6, bf16[768,256]{1,0:T(8,128)(2,1)S(1)} %gather_fusion.5, f32[]{:T(128)} %constant.19.clone.1, f32[256]{0:T(256)} %bitcast.108, f32[]{:T(128)} %constant.15.clone.1), kind=kCustom, calls=%fused_computation.40 | custom fusion | flops 1769472 | bytes 1050624 | tf_op jit(solution)/shard_map/scatter-add | solution.py:30
  128.0 0.9 convolution_bitcast_fusion.2
  129.0 0.9 fusion.12
  129.9 2.5 fusion.76
  132.3 6.1 %scatter_custom_fusion.4 = f32[256,256]{1,0:T(8,128)S(1)} fusion(s32[768]{0:T(1024)} %get-tuple-element.10, f32[768,256]{1,0:T(8,128)} %get-tuple-element.19, f32[]{:T(128)} %constant.15.clone.1), kind=kCustom, calls=%fused_computation.68 | custom fusion | flops 196608 | bytes 262656 | tf_op jit(solution)/shard_map/scatter-add | solution.py:30
  138.4 6.1 %scatter_custom_fusion.3 = f32[256,256]{1,0:T(8,128)S(1)} fusion(s32[768]{0:T(1024)} %get-tuple-element.9, f32[768,256]{1,0:T(8,128)} %get-tuple-element.19, f32[]{:T(128)} %constant.15.clone.1), kind=kCustom, calls=%fused_computation.70 | custom fusion | flops 196608 | bytes 262656 | tf_op jit(solution)/shard_map/scatter-add | solution.py:30
  144.5 1.0 convolution_bitcast_fusion.1
  145.9 1.0 convolution_bitcast_fusion
  147.4 1.6 scatter_fusion
  149.0 1.0 convolution_bitcast_fusion.3
  150.0 1.2 fusion.20
  151.2 3.7 %gather_fusion.9 = f32[1536,256]{1,0:T(8,128)S(1)} fusion(f32[128,256]{1,0:T(8,128)S(1)} %fusion.20, s32[2048]{0:T(1024)S(1)} %copy-done.16), kind=kCustom, calls=%fused_computation.9 | custom fusion | bytes 3151872 | tf_op jit(solution)/shard_map/gather | solution.py:108
  154.9 2.6 fusion.75
  157.6 9.3 %scatter_custom_fusion.7 = f32[128,256]{1,0:T(8,128)S(1)} fusion(s32[1536]{0:T(1024)} %copy-done.18, f32[1536,256]{1,0:T(8,128)} %get-tuple-element.17, f32[]{:T(128)} %constant.15.clone.1), kind=kCustom, calls=%fused_computation.89 | custom fusion | flops 393216 | bytes 131584 | tf_op jit(solution)/shard_map/scatter-add | solution.py:30
  166.9 9.4 %scatter_custom_fusion.6 = f32[160,256]{1,0:T(8,128)S(1)} fusion(s32[1536]{0:T(1024)} %get-tuple-element.5, f32[1536,256]{1,0:T(8,128)} %get-tuple-element.17, f32[]{:T(128)} %constant.15.clone.1), kind=kCustom, calls=%fused_computation.85 | custom fusion | flops 393216 | bytes 164352 | tf_op jit(solution)/shard_map/scatter-add | solution.py:30
  176.2 1.9 convolution_bitcast_fusion.5
  178.1 1.2 fusion.79
  179.4 1.0 convolution_bitcast_fusion.4
  180.4 1.2 convolution_add_fusion.1
  182.4 2.2 collective-permute-start.2
  184.6 1.3 collective-permute-start.3
  185.9 30.7 %psum.31 = f32[1,256]{1,0:T(1,128)S(1)} all-reduce(f32[1,256]{1,0:T(1,128)S(1)} %bitcast.110), channel_id=1, replica_groups=mesh['groups'=2,'dom'=16] {'dom'}, use_global_device_ids=true, to_apply=%region_14.15 | all-reduce | flops 256 | bytes 2048 | tf_op jit(solution)/shard_map/psum | solution.py:126
  216.6 0.9 pad_maximum_fusion.1
  218.2 0.9 gather_fusion.7
  219.7 1.0 scatter_custom_fusion.8
  220.7 51.1 %all-reduce.3.cloned.1.call-done = (f32[1,256,256]{2,1,0:T(8,128)}, f32[1,256,256]{2,1,0:T(8,128)}, f32[1,256,256]{2,1,0:T(8,128)}) async-done(((f32[1,256,256]{2,1,0:T(8,128)}, f32[1,256,256]{2,1,0:T(8,128)}, f32[1,256,256]{2,1,0:T(8,128)}), (f32[1,256,256]{2,1,0:T(8,128)}, f32[1,256,256]{2,1,0:T(8,128)}, f32[1,256,256]{2,1,0:T(8,128)})) %all-reduce.3.cloned.1.call-update) | async-done | bytes 786448 | tf_op jit(solution)/shard_map/psum | solution.py:126
  271.8 2.0 pad_maximum_fusion
  (85 shorter events, 10.3 us)
Async XLA Ops:
  7.2 264.6 %all-reduce.3.cloned.1.call-start = ((), (), s32[]{:S(2)}) async-start(), calls=%async_computation | async-start | bytes 1572864 | tf_op jit(solution)/shard_map/psum | solution.py:126
  9.4 70.8 %collective-permute-start = (bf16[16,256]{1,0:T(8,128)(2,1)S(1)}, bf16[16,256]{1,0:T(8,128)(2,1)S(1)}, u32[]{:S(2)}, u32[]{:S(2)}) collective-permute-start(bf16[16,256]{1,0:T(8,128)(2,1)S(1)} %gather_fusion), channel_id=1, source_target_pairs={{0,1},{1,2},{2,3},{3,4},{4,5},{5,6},{6,7},{7,8},{8,9},{9,10},{10,1... | collective-permute-start | bytes 24584 | tf_op jit(solution)/shard_map/ppermute | solution.py:12
  13.2 67.1 %collective-permute-start.1 = (bf16[16,256]{1,0:T(8,128)(2,1)S(1)}, bf16[16,256]{1,0:T(8,128)(2,1)S(1)}, u32[]{:S(2)}, u32[]{:S(2)}) collective-permute-start(bf16[16,256]{1,0:T(8,128)(2,1)S(1)} %gather_fusion.1), channel_id=1, source_target_pairs={{1,0},{2,1},{3,2},{4,3},{5,4},{6,5},{7,6},{8,7},{9,8},{10,9},{11,1... | collective-permute-start | bytes 24584 | tf_op jit(solution)/shard_map/ppermute | solution.py:15
  43.5 42.2 %copy-start.18 = (s32[1536]{0:T(1024)}, s32[1536]{0:T(1024)S(1)}, u32[]{:S(2)}) copy-start(s32[1536]{0:T(1024)S(1)} %get-tuple-element.6) | copy-start | bytes 18436
  46.1 39.6 %copy-start.17 = (f32[1,256]{1,0:T(1,128)}, f32[1,256]{1,0:T(1,128)S(1)}, u32[]{:S(2)}) copy-start(f32[1,256]{1,0:T(1,128)S(1)} %get-tuple-element.25) | copy-start | bytes 3076
  46.9 38.8 %copy-start.13 = (f32[1536]{0:T(1024)}, f32[1536]{0:T(1024)S(1)}, u32[]{:S(2)}) copy-start(f32[1536]{0:T(1024)S(1)} %fusion.68) | copy-start | bytes 18436
  68.6 6.9 %copy-start.15 = (s32[2048]{0:T(1024)}, s32[2048]{0:T(1024)S(1)}, u32[]{:S(2)}) copy-start(s32[2048]{0:T(1024)S(1)} %get-tuple-element.32) | copy-start | bytes 24580
  75.5 4.8 %copy-start.2 = (bf16[128,256]{1,0:T(8,128)(2,1)S(1)}, bf16[128,256]{1,0:T(8,128)(2,1)}, u32[]{:S(2)}) copy-start(bf16[128,256]{1,0:T(8,128)(2,1)} %param.11) | copy-start | bytes 196612
  75.5 4.8 %copy-start.5 = (bf16[3,256,256]{2,1,0:T(8,128)(2,1)S(1)}, bf16[3,256,256]{2,1,0:T(8,128)(2,1)}, u32[]{:S(2)}) copy-start(bf16[3,256,256]{2,1,0:T(8,128)(2,1)} %param.13) | copy-start | bytes 1179652
  80.3 0.6 copy-start.11
  85.7 30.1 %copy-start.4 = (bf16[3,256,256]{2,1,0:T(8,128)(2,1)S(1)}, bf16[3,256,256]{2,1,0:T(8,128)(2,1)}, u32[]{:S(2)}) copy-start(bf16[3,256,256]{2,1,0:T(8,128)(2,1)} %param.14) | copy-start | bytes 1179652
  95.8 20.3 %copy-start.6 = (f32[128,256]{1,0:T(8,128)}, f32[128,256]{1,0:T(8,128)S(1)}, u32[]{:S(2)}) copy-start(f32[128,256]{1,0:T(8,128)S(1)} %scatter_custom_fusion) | copy-start | bytes 393220
  115.9 30.0 %copy-start = (bf16[256,256]{1,0:T(8,128)(2,1)}, bf16[256,256]{1,0:T(8,128)(2,1)S(1)}, u32[]{:S(2)}) copy-start(bf16[256,256]{1,0:T(8,128)(2,1)S(1)} %all_gather.9) | copy-start | bytes 393220
  128.0 1.8 copy-start.1
  138.4 8.9 %copy-start.20 = (s32[128]{0:T(128)S(1)}, s32[128]{0:T(128)}, u32[]{:S(2)}) copy-start(s32[128]{0:T(128)} %reshape.320) | copy-start | bytes 1540
  146.9 2.0 copy-start.7
  147.4 3.8 %copy-start.16 = (s32[2048]{0:T(1024)S(1)}, s32[2048]{0:T(1024)}, u32[]{:S(2)}) copy-start(s32[2048]{0:T(1024)} %copy-done.15) | copy-start | bytes 24580
  151.2 3.7 %copy-start.14 = (f32[1536]{0:T(1024)S(1)}, f32[1536]{0:T(1024)}, u32[]{:S(2)}) copy-start(f32[1536]{0:T(1024)} %copy-done.13) | copy-start | bytes 18436
  154.9 24.5 %copy-start.3 = (bf16[128,256]{1,0:T(8,128)(2,1)S(1)}, bf16[128,256]{1,0:T(8,128)(2,1)}, u32[]{:S(2)}) copy-start(bf16[128,256]{1,0:T(8,128)(2,1)} %param.11) | copy-start | bytes 196612
  166.8 49.8 %copy-start.8 = (f32[1,256,256]{2,1,0:T(8,128)S(1)}, f32[1,256,256]{2,1,0:T(8,128)}, u32[]{:S(2)}) copy-start(f32[1,256,256]{2,1,0:T(8,128)} %convolution_bitcast_fusion.2) | copy-start | bytes 786436
  166.8 49.8 %copy-start.9 = (f32[1,256,256]{2,1,0:T(8,128)S(1)}, f32[1,256,256]{2,1,0:T(8,128)}, u32[]{:S(2)}) copy-start(f32[1,256,256]{2,1,0:T(8,128)} %convolution_bitcast_fusion.1) | copy-start | bytes 786436
  166.9 49.8 %copy-start.10 = (f32[1,256,256]{2,1,0:T(8,128)S(1)}, f32[1,256,256]{2,1,0:T(8,128)}, u32[]{:S(2)}) copy-start(f32[1,256,256]{2,1,0:T(8,128)} %convolution_bitcast_fusion) | copy-start | bytes 786436
  180.4 37.2 %copy-start.19 = (f32[256]{0:T(256)S(1)}, f32[256]{0:T(256)}, u32[]{:S(2)}) copy-start(f32[256]{0:T(256)} %get-tuple-element.18) | copy-start | bytes 3076
  182.4 37.3 %collective-permute-start.2 = (bf16[16,256]{1,0:T(8,128)(2,1)S(1)}, bf16[16,256]{1,0:T(8,128)(2,1)S(1)}, u32[]{:S(2)}, u32[]{:S(2)}) collective-permute-start(bf16[16,256]{1,0:T(8,128)(2,1)S(1)} %get-tuple-element.20), channel_id=1, source_target_pairs={{0,1},{1,2},{2,3},{3,4},{4,5},{5,6},{6,7},{7,8},{8,9},{9,10},{10,1... | collective-permute-start | bytes 24584 | tf_op jit(solution)/shard_map/ppermute | solution.py:12
  184.6 35.1 %collective-permute-start.3 = (bf16[16,256]{1,0:T(8,128)(2,1)S(1)}, bf16[16,256]{1,0:T(8,128)(2,1)S(1)}, u32[]{:S(2)}, u32[]{:S(2)}) collective-permute-start(bf16[16,256]{1,0:T(8,128)(2,1)S(1)} %get-tuple-element.21), channel_id=1, source_target_pairs={{1,0},{2,1},{3,2},{4,3},{5,4},{6,5},{7,6},{8,7},{9,8},{10,9},{11,1... | collective-permute-start | bytes 24584 | tf_op jit(solution)/shard_map/ppermute | solution.py:15
  220.7 53.1 %copy-start.12 = (f32[128,256]{1,0:T(8,128)}, f32[128,256]{1,0:T(8,128)S(1)}, u32[]{:S(2)}) copy-start(f32[128,256]{1,0:T(8,128)S(1)} %scatter_custom_fusion.8) | copy-start | bytes 393220
Sparse Core Ops, SparseCore 0:
  181.8 89.9 all-reduce.2
where the time goes:
time: 282 us; the launch traced here: 281 us
  blocking collectives  92.9 us (33%)
  other arithmetic  67 us (24%)
  waiting for transfers between devices  51.1 us (18%)
  local copies, waits for them, and re-layouts  32.2 us (11%)
  between operations  15.3 us (5%)
  matrix products  15 us (5%)
  starting transfers between devices  7.22 us (3%)
    psum x1, waiting for transfers between devices, shards(): lax.psum((grad_s, grad_r, grad_u, bias1), 'dom')  51.1 us
    scatter-add x8, other arithmetic, segment_rows(): return jax.ops.segment_sum(values, index, count)  50.2 us
    psum x1, blocking collectives, shards(): lax.psum((grad_s, grad_r, grad_u, bias1), 'dom')  30.7 us
    all_gather x1, blocking collectives, shards(): links = lax.all_gather(coarse_ends, 'dom', axis=1, tiled=True)  25.2 us
    all_gather x1, blocking collectives, shards(): coarse_all = lax.all_gather(coarse_own, 'dom', axis=0, tiled=True)  19.1 us
    all_gather x1, blocking collectives, shards(): lax.all_gather(parent_grad, 'dom', axis=0, tiled=True).astype(jnp.float32)  17.8 us
    dot_general x12, matrix products, precise_dot(): return jnp.dot(left, right, precision=lax.Precision.HIGHEST)  12.4 us
  transfers between devices with their start and end apart: 5, of which 1 were waited for; matrix products, arithmetic and copies ran while one was open for 10% of the time, Pallas kernels for 0%

commit v1 on v0

v1 whole, which is shorter than its diff:
```python
import functools

import jax
import jax.numpy as jnp
from jax import lax
from jax.experimental import pallas as pl
from jax.experimental.pallas import tpu as pltpu
from jax.sharding import PartitionSpec as P

BF16 = jnp.bfloat16
F32 = jnp.float32
EDGE_BLOCK = 128
ROW_TILE = 16
VMEM_LIMIT = 56 * 1024 * 1024


def dot(left, right):
    return jnp.dot(left, right, preferred_element_type=F32)


def dot_tn(left, right):
    return lax.dot_general(left, right, (((0,), (0,)), ((), ())), preferred_element_type=F32)


def dot_nt(left, right):
    return lax.dot_general(left, right, (((1,), (1,)), ((), ())), preferred_element_type=F32)


def split(value):
    high = value.astype(BF16)
    return high, (value - high.astype(F32)).astype(BF16)


def one_hot_rows(index_row, count):
    spots = lax.broadcasted_iota(jnp.int32, (count, index_row.shape[1]), 0)
    return jnp.where(spots == index_row, 1.0, 0.0).astype(BF16)


def one_hot_cols(index_col, count):
    spots = lax.broadcasted_iota(jnp.int32, (index_col.shape[0], count), 1)
    return jnp.where(spots == index_col, 1.0, 0.0).astype(BF16)


def to_column(index_row):
    return jnp.transpose(jnp.broadcast_to(index_row, (8, index_row.shape[1])))[:, :1]


def silu_and_slope(value):
    sig = 0.5 * jnp.tanh(0.5 * value) + 0.5
    message = value * sig
    return message, sig + message * (1.0 - sig)


def membership(members, node_count):
    spots = lax.broadcasted_iota(jnp.int32, (node_count, members.shape[1]), 0)
    total = jnp.zeros(spots.shape, F32)
    for row in range(members.shape[0]):
        total = total + jnp.where(spots == members[row : row + 1], 1.0, 0.0)
    return total.astype(BF16)


def place():
    me = lax.axis_index("dom")
    return me, lax.rem(me, 2), lax.div(me, 2)


def live_rows(ends_ref, live_ref, row):
    index = ends_ref[row : row + 1, :]
    slot = lax.broadcasted_iota(jnp.int32, index.shape, 1)
    return jnp.where(slot < live_ref[0] * EDGE_BLOCK, index, -1)


def pick_kernel(nodes_ref, lists_ref, near_ref, far_ref):
    _, odd, _ = place()
    lists = lists_ref[...]
    near = jnp.where(odd == 1, lists[0:1], lists[1:2])
    far = jnp.where(odd == 1, lists[1:2], lists[0:1])
    nodes = nodes_ref[...]
    near_ref[...] = dot_tn(one_hot_rows(near, nodes.shape[0]), nodes).astype(BF16)
    far_ref[...] = dot_tn(one_hot_rows(far, nodes.shape[0]), nodes).astype(BF16)


def extend(nodes, near, far, odd):
    low = jnp.where(odd == 1, near, far)
    high = jnp.where(odd == 1, far, near)
    return jnp.concatenate([low, nodes, high], 0)


def forward_kernel(
    ndom,
    nodes_ref,
    near_ref,
    far_ref,
    weights_ref,
    biases_ref,
    ends_ref,
    live_ref,
    members_ref,
    parents_ref,
    cotangent_ref,
    links_ref,
    updated_ref,
    summed_ref,
    slopes_sum_ref,
    slopes_ref,
    packet_ref,
    message_ref,
    link_ref,
):
    me, odd, _ = place()
    nodes = nodes_ref[...]
    node_count, width = nodes.shape
    coarse_count = members_ref.shape[1]
    extended = extend(nodes, near_ref[...], far_ref[...], odd)
    src_proj = dot(extended, weights_ref[0]).astype(BF16)
    dst_proj = dot(nodes, weights_ref[1]).astype(BF16)
    slots = ends_ref.shape[1]
    chunk = 2 * EDGE_BLOCK
    bias = biases_ref[0:1, :]
    for start in range(0, slots, chunk):
        senders = to_column(ends_ref[0:1, start : start + chunk])
        receivers = to_column(ends_ref[1:2, start : start + chunk])
        pre = (
            dot(one_hot_cols(senders, extended.shape[0]), src_proj)
            + dot(one_hot_cols(receivers, node_count), dst_proj)
            + bias
        )
        message, slope = silu_and_slope(pre)
        message_ref[start : start + chunk, :] = message.astype(BF16)
        slopes_ref[start : start + chunk, :] = slope.astype(BF16)
    into = one_hot_rows(live_rows(ends_ref, live_ref, 1), node_count)
    summed = dot(into, message_ref[...]).astype(BF16)
    slopes_sum_ref[...] = dot(into, slopes_ref[...])
    summed_ref[...] = summed
    updated = nodes.astype(F32) + dot(summed, weights_ref[2])
    updated_ref[...] = updated

    share = membership(members_ref[...], node_count)
    high, low = split(updated)
    pooled = dot_tn(share, high) + dot_tn(share, low)
    coarse = (pooled / members_ref.shape[0]).astype(BF16)
    family = one_hot_rows(parents_ref[...], coarse_count)
    parent_grad = dot(family, cotangent_ref[...]).astype(BF16)

    links = links_ref[...]
    own = links.shape[1]
    rows = link_ref.shape[0]
    pieces = -(-own * ndom // width)
    spot = lax.broadcasted_iota(jnp.int32, (own, pieces * width), 1)
    source = lax.broadcasted_iota(jnp.int32, (own, pieces * width), 0)
    spread = jnp.where(spot == source + me * own, 1.0, 0.0).astype(BF16)
    coded = (
        dot((links >> 8).astype(F32).astype(BF16), spread),
        dot((links & 255).astype(F32).astype(BF16), spread),
    )
    link_ref[...] = jnp.zeros(link_ref.shape, F32)
    for part in range(2):
        for end in range(2):
            for piece in range(pieces):
                row = (part * 2 + end) * pieces + piece
                link_ref[row : row + 1, :] = coded[part][
                    end : end + 1, piece * width : (piece + 1) * width
                ]
    coded_links = link_ref[...].astype(BF16)
    for chip in range(packet_ref.shape[0]):
        packet_ref[chip, :coarse_count, :] = coarse
        packet_ref[chip, coarse_count : 2 * coarse_count, :] = parent_grad
        packet_ref[chip, 2 * coarse_count : 2 * coarse_count + rows, :] = coded_links


def ordered(mine_ref, theirs_ref, odd, start, count):
    blocks = []
    for chip in range(mine_ref.shape[0]):
        mine = mine_ref[chip, start : start + count, :]
        theirs = theirs_ref[chip, start : start + count, :]
        blocks.append(jnp.where(odd == 1, theirs, mine))
        blocks.append(jnp.where(odd == 1, mine, theirs))
    return blocks


def backward_kernel(
    ndom,
    edge_count2,
    mine_ref,
    theirs_ref,
    coarse_weights_ref,
    biases_ref,
    nodes_ref,
    near_ref,
    far_ref,
    weights_ref,
    ends_ref,
    live_ref,
    members_ref,
    parents_ref,
    cotangent_ref,
    updated_ref,
    summed_ref,
    slopes_sum_ref,
    slopes_ref,
    moved_ref,
    node_part_ref,
    coarse_grads_ref,
    bias2_ref,
    send_ref,
    keep_ref,
    link_ref,
    message2_ref,
    slope2_ref,
    edge2_ref,
    own_ref,
    grads_ref,
    edge_ref,
):
    me, odd, _ = place()
    nodes = nodes_ref[...]
    node_count, width = nodes.shape
    coarse_count = members_ref.shape[1]
    member_count = members_ref.shape[0]
    total = ndom * coarse_count

    coarse = jnp.concatenate(ordered(mine_ref, theirs_ref, odd, 0, coarse_count), 0)
    parent_all = jnp.concatenate(
        ordered(mine_ref, theirs_ref, odd, coarse_count, coarse_count), 0
    )
    link_rows = link_ref.shape[0]
    gathered = jnp.zeros(link_ref.shape, F32)
    for chip in range(mine_ref.shape[0]):
        for ref in (mine_ref, theirs_ref):
            gathered = gathered + ref[
                chip, 2 * coarse_count : 2 * coarse_count + link_rows, :
            ].astype(F32)
    link_ref[...] = gathered
    pieces = -(-edge_count2 // width)
    ends2 = []
    for end in range(2):
        rows = []
        for piece in range(pieces):
            top = end * pieces + piece
            bottom = (2 + end) * pieces + piece
            code = 256.0 * link_ref[top : top + 1, :] + link_ref[bottom : bottom + 1, :]
            spot = lax.broadcasted_iota(jnp.int32, code.shape, 1) + piece * width
            rows.append(jnp.where(spot < edge_count2, code.astype(jnp.int32), -1))
        ends2.append(rows)
    src2 = dot(coarse, coarse_weights_ref[0]).astype(BF16)
    dst2 = dot(coarse, coarse_weights_ref[1]).astype(BF16)
    grad_agg2 = dot_nt(parent_all, coarse_weights_ref[2])
    grad_agg2_near = grad_agg2.astype(BF16)
    bias = biases_ref[1:2, :]
    for piece in range(pieces):
        span = slice(piece * width, (piece + 1) * width)
        from_nodes = one_hot_cols(to_column(ends2[0][piece]), total)
        to_nodes = one_hot_cols(to_column(ends2[1][piece]), total)
        pre = dot(from_nodes, src2) + dot(to_nodes, dst2) + bias
        message, slope = silu_and_slope(pre)
        message2_ref[span, :] = message.astype(BF16)
        slope2_ref[span, :] = slope.astype(BF16)
        edge2_ref[span, :] = (dot(to_nodes, grad_agg2_near) * slope).astype(BF16)
    into = jnp.concatenate([one_hot_rows(row, total) for row in ends2[1]], 1)
    coarse_sum = dot(into, message2_ref[...]).astype(BF16)
    grad_dst2 = dot(into, slope2_ref[...]) * grad_agg2
    back = jnp.concatenate([one_hot_rows(row, total) for row in ends2[0]], 1)
    grad_src2 = dot(back, edge2_ref[...])
    bias2_ref[...] = jnp.sum(grad_dst2, 0, keepdims=True)
    grad_src2 = grad_src2.astype(BF16)
    grad_dst2 = grad_dst2.astype(BF16)
    coarse_grads_ref[0] = dot_tn(coarse, grad_src2)
    coarse_grads_ref[1] = dot_tn(coarse, grad_dst2)
    coarse_grads_ref[2] = dot_tn(coarse_sum, parent_all)

    own_ref[0] = coarse
    own_ref[1] = parent_all
    own_ref[2] = coarse_sum
    own_ref[3] = grad_src2
    own_ref[4] = grad_dst2
    rows = pl.ds(pl.multiple_of(me * coarse_count, coarse_count), coarse_count)
    coarse_new = own_ref[0, rows, :].astype(F32) + dot(own_ref[2, rows, :], coarse_weights_ref[2])
    coarse_grad = (
        own_ref[1, rows, :].astype(F32)
        + dot_nt(own_ref[3, rows, :], coarse_weights_ref[0])
        + dot_nt(own_ref[4, rows, :], coarse_weights_ref[1])
    )
    family = one_hot_rows(parents_ref[...], coarse_count)
    high, low = split(coarse_new)
    moved_ref[...] = updated_ref[...] + dot_tn(family, high) + dot_tn(family, low)
    share = membership(members_ref[...], node_count)
    high, low = split(coarse_grad / member_count)
    grad_updated = cotangent_ref[...].astype(F32) + dot(share, high) + dot(share, low)

    extended = extend(nodes, near_ref[...], far_ref[...], odd)
    rim = near_ref.shape[0]
    slots = ends_ref.shape[1]
    grad_updated_near = grad_updated.astype(BF16)
    grad_summed = dot_nt(grad_updated_near, weights_ref[2])
    grad_summed_near = grad_summed.astype(BF16)
    grad_dst = slopes_sum_ref[...] * grad_summed
    chunk = 2 * EDGE_BLOCK
    for start in range(0, slots, chunk):
        receivers = to_column(ends_ref[1:2, start : start + chunk])
        slope = slopes_ref[start : start + chunk, :].astype(F32)
        edge = dot(one_hot_cols(receivers, node_count), grad_summed_near) * slope
        edge_ref[start : start + chunk, :] = edge.astype(BF16)
    back = one_hot_rows(live_rows(ends_ref, live_ref, 0), extended.shape[0])
    grad_src = dot(back, edge_ref[...]).astype(BF16)
    bias1 = jnp.sum(grad_dst, 0, keepdims=True)
    grad_dst = grad_dst.astype(BF16)
    both = jnp.concatenate([grad_src[rim : rim + node_count], grad_dst], 1)
    node_part_ref[...] = grad_updated + dot_nt(
        both, jnp.concatenate([weights_ref[0], weights_ref[1]], 1)
    )
    low = dot_nt(grad_src[:rim], weights_ref[0]).astype(BF16)
    high = dot_nt(grad_src[rim + node_count :], weights_ref[0]).astype(BF16)
    grads_ref[0:width, :] = dot_tn(extended, grad_src).astype(BF16)
    grads_ref[width : 2 * width, :] = dot_tn(nodes, grad_dst).astype(BF16)
    grads_ref[2 * width : 3 * width, :] = dot_tn(summed_ref[...], grad_updated_near).astype(BF16)
    if grads_ref.shape[0] > 3 * width:
        grads_ref[3 * width :, :] = jnp.zeros((grads_ref.shape[0] - 3 * width, width), BF16)
    half = grads_ref.shape[0] // 2
    keep_ref[:half, :] = grads_ref[pl.ds(pl.multiple_of(odd * half, ROW_TILE), half), :]
    send_ref[:half, :] = grads_ref[pl.ds(pl.multiple_of((1 - odd) * half, ROW_TILE), half), :]
    bias_rows = two_rows(bias1)
    keep_ref[half : half + ROW_TILE, :] = bias_rows
    send_ref[half : half + ROW_TILE, :] = bias_rows
    base = half + ROW_TILE
    send_ref[base : base + rim, :] = jnp.where(odd == 1, low, high)
    send_ref[base + rim : base + 2 * rim, :] = jnp.where(odd == 1, high, low)


def two_rows(value):
    high = value.astype(BF16).astype(F32)
    row = lax.broadcasted_iota(jnp.int32, (ROW_TILE, value.shape[1]), 0)
    return jnp.where(row == 0, high, jnp.where(row == 1, value - high, 0.0)).astype(BF16)


def pair_kernel(keep_ref, came_ref, blocks_ref):
    half = keep_ref.shape[0] - ROW_TILE
    chips, depth, _ = blocks_ref.shape
    rim = came_ref.shape[0] - half - ROW_TILE
    rim = rim // 2
    rows = half // chips
    bias = keep_ref[half:, :].astype(F32) + came_ref[half : half + ROW_TILE, :].astype(F32)
    bias = two_rows(jnp.sum(bias, 0, keepdims=True))
    far = came_ref[half + ROW_TILE + rim :, :]
    for chip in range(chips):
        span = slice(chip * rows, (chip + 1) * rows)
        blocks_ref[chip, :rows, :] = (
            keep_ref[span, :].astype(F32) + came_ref[span, :].astype(F32)
        ).astype(BF16)
        blocks_ref[chip, rows : rows + ROW_TILE, :] = bias
        blocks_ref[chip, rows + ROW_TILE :, :] = far


def sum_kernel(
    blocks_ref, came_ref, node_part_ref, lists_ref, bias2_ref, part_ref, node_grads_ref, bias_ref
):
    _, odd, chip = place()
    chips, rows, _ = part_ref.shape
    rim = lists_ref.shape[1]
    half = chips * rows
    total = blocks_ref[0, : rows + ROW_TILE, :].astype(F32)
    for other in range(1, chips):
        total = total + blocks_ref[other, : rows + ROW_TILE, :].astype(F32)
    part = total[:rows].astype(BF16)
    for other in range(chips):
        part_ref[other] = part
    bias_ref[0:1, :] = jnp.sum(total[rows:], 0, keepdims=True)
    bias_ref[1:2, :] = bias2_ref[...]
    lists = lists_ref[...]
    near_list = jnp.where(odd == 1, lists[0:1], lists[1:2])
    far_list = jnp.where(odd == 1, lists[1:2], lists[0:1])
    origin = jnp.where(odd == 1, chip + 1, chip - 1)
    inside = jnp.logical_and(origin >= 0, origin < chips)
    far_list = jnp.where(inside, far_list, -1)
    origin = jnp.clip(origin, 0, chips - 1)
    near = came_ref[half + ROW_TILE : half + ROW_TILE + rim, :]
    far = blocks_ref[origin, rows + ROW_TILE : rows + ROW_TILE + rim, :]
    node_count = node_part_ref.shape[0]
    node_grads_ref[...] = (
        node_part_ref[...]
        + dot(one_hot_rows(near_list, node_count), near)
        + dot(one_hot_rows(far_list, node_count), far)
    )


def join_kernel(mine_ref, theirs_ref, out_ref):
    _, odd, _ = place()
    chips, rows, _ = mine_ref.shape
    limit = out_ref.shape[0]
    for side in range(2):
        for chip in range(chips):
            start = (side * chips + chip) * rows
            count = min(rows, limit - start)
            if count <= 0:
                continue
            mine = mine_ref[chip, :count, :]
            theirs = theirs_ref[chip, :count, :]
            out_ref[start : start + count, :] = jnp.where(odd == side, mine, theirs).astype(F32)


def call(kernel, outs, args, scratch=(), scalars=()):
    whole = pl.BlockSpec(memory_space=pltpu.VMEM)
    scalar = pl.BlockSpec(memory_space=pltpu.SMEM)
    return pl.pallas_call(
        kernel,
        out_shape=[jax.ShapeDtypeStruct(shape, kind) for shape, kind in outs],
        in_specs=[scalar if spot in scalars else whole for spot in range(len(args))],
        out_specs=[whole] * len(outs),
        scratch_shapes=[pltpu.VMEM(shape, kind) for shape, kind in scratch],
        compiler_params=pltpu.CompilerParams(vmem_limit_bytes=VMEM_LIMIT),
    )(*args)


def round_up(value, unit):
    return -(-value // unit) * unit


def shards(
    nodes,
    cotangent,
    fine_weights,
    coarse_weights,
    biases,
    send_lists,
    edge_ends,
    live_blocks,
    pool_members,
    parents,
    coarse_ends,
):
    ndom = lax.axis_size("dom")
    chips = ndom // 2
    node_count, width = nodes.shape
    rim = send_lists.shape[1]
    coarse_count = pool_members.shape[1]
    slots = edge_ends.shape[1]
    edge_count2 = coarse_ends.shape[1] * ndom
    total = coarse_count * ndom
    parents = parents.reshape(1, node_count)
    pairs = [(i, i ^ 1) for i in range(ndom)]
    across = [(i, i + 1) for i in range(1, ndom - 1, 2)]
    across = across + [(target, source) for source, target in across]
    same_core = [[2 * chip + core for chip in range(chips)] for core in range(2)]

    def swap(value):
        return lax.ppermute(value, "dom", pairs)

    def exchange(value):
        return lax.all_to_all(value, "dom", 0, 0, axis_index_groups=same_core)

    near, far = call(
        pick_kernel, [((rim, width), BF16), ((rim, width), BF16)], (nodes, send_lists)
    )
    far = lax.ppermute(far, "dom", across)
    near = swap(near)

    pieces = -(-edge_count2 // width)
    link_rows = round_up(4 * pieces, ROW_TILE)
    packet_rows = 2 * coarse_count + link_rows
    updated, summed, slopes_sum, slopes, packet = call(
        functools.partial(forward_kernel, ndom),
        [
            ((node_count, width), F32),
            ((node_count, width), BF16),
            ((node_count, width), F32),
            ((slots, width), BF16),
            ((chips, packet_rows, width), BF16),
        ],
        (
            nodes,
            near,
            far,
            fine_weights,
            biases,
            edge_ends,
            live_blocks,
            pool_members,
            parents,
            cotangent,
            coarse_ends,
        ),
        scratch=[((slots, width), BF16), ((link_rows, width), F32)],
        scalars=(6,),
    )
    mine = exchange(packet)
    theirs = swap(mine)

    rows = round_up(-(-3 * width // ndom), ROW_TILE)
    half = rows * chips
    edges2 = pieces * width
    moved, node_part, coarse_grads, bias2, send, keep = call(
        functools.partial(backward_kernel, ndom, edge_count2),
        [
            ((node_count, width), F32),
            ((node_count, width), F32),
            ((3, width, width), F32),
            ((1, width), F32),
            ((half + ROW_TILE + 2 * rim, width), BF16),
            ((half + ROW_TILE, width), BF16),
        ],
        (
            mine,
            theirs,
            coarse_weights,
            biases,
            nodes,
            near,
            far,
            fine_weights,
            edge_ends,
            live_blocks,
            pool_members,
            parents,
            cotangent,
            updated,
            summed,
            slopes_sum,
            slopes,
        ),
        scratch=[
            ((link_rows, width), F32),
            ((edges2, width), BF16),
            ((edges2, width), BF16),
            ((edges2, width), BF16),
            ((5, total, width), BF16),
            ((2 * half, width), BF16),
            ((slots, width), BF16),
        ],
        scalars=(9,),
    )
    came = swap(send)
    (blocks,) = call(
        pair_kernel, [((chips, rows + ROW_TILE + rim, width), BF16)], (keep, came)
    )
    blocks = exchange(blocks)
    part, node_grads, bias_grads = call(
        sum_kernel,
        [
            ((chips, rows, width), BF16),
            ((node_count, width), F32),
            ((2, width), F32),
        ],
        (blocks, came, node_part, send_lists, bias2),
    )
    mine = exchange(part)
    theirs = swap(mine)
    (fine_grads,) = call(join_kernel, [((3 * width, width), F32)], (mine, theirs))
    return moved, node_grads, fine_grads.reshape(3, width, width), coarse_grads, bias_grads


def solution(mesh):
    return jax.shard_map(
        shards,
        mesh=mesh,
        in_specs=(
            P(("groups", "dom"), None),
            P(("groups", "dom"), None),
            P(),
            P(),
            P(),
            P("groups", "dom"),
            P("groups", "dom"),
            P(("groups", "dom")),
            P("groups", "dom"),
            P(("groups", "dom")),
            P("groups", "dom"),
        ),
        out_specs=(
            P(("groups", "dom"), None),
            P(("groups", "dom"), None),
            P("groups", None, None),
            P("groups", None, None),
            P("groups", None),
        ),
        check_vma=False,
    )
```

time: 282 us -> 72.9 us (0.26)
  other arithmetic: 67 us -> 0 us
  blocking collectives: 92.9 us -> 45.8 us
  waiting for transfers between devices: 51.1 us -> 4.43 us
  local copies, waits for them, and re-layouts: 32.2 us -> 2.62 us
  Pallas kernels: 0 us -> 16.8 us
  matrix products: 15 us -> 0 us
  between operations: 15.3 us -> 1.33 us
  starting transfers between devices: 7.22 us -> 1.27 us
    all_gather x3 -> x0, blocking collectives: 62.2 us -> none  [the longest x1 25.2 us: shards(): links = lax.all_gather(coarse_ends, 'dom', axis=1, tiled=True)]
    psum x1 -> x0, waiting for transfers between devices: 51.1 us -> none  [shards(): lax.psum((grad_s, grad_r, grad_u, bias1), 'dom')]
    scatter-add x8 -> x0, other arithmetic: 50.2 us -> none  [segment_rows(): return jax.ops.segment_sum(values, index, count)]
    all_to_all x0 -> x3, blocking collectives: none -> 45.8 us  [exchange(): return lax.all_to_all(value, 'dom', 0, 0, axis_index_groups=same_core)]
    psum x1 -> x0, blocking collectives: 30.7 us -> none  [shards(): lax.psum((grad_s, grad_r, grad_u, bias1), 'dom')]
    gather x10 -> x0, local copies, waits for them, and re-layouts: 26 us -> none  [the longest x1 4.76 us: shards(): dst_proj[receivers].astype(jnp.float32)]
    pallas_call x0 -> x6, Pallas kernels: none -> 16.8 us  [call(): pl.pallas_call(kernel, out_shape=[jax.ShapeDtypeStruct(shape, kind) for s...]
    dot_general x18 -> x0, matrix products: 15 us -> none  [the longest x12 12.4 us: precise_dot(): return jnp.dot(left, right, precision=lax.Precision.HIGHEST)]
  transfers between devices with their start and end apart: 5 -> 5, of which waited for: 1 -> 3; matrix products, arithmetic and copies ran while one was open for 10% -> 0% of each run, Pallas kernels for 0% -> 0%
where the time goes in v1:
time: 72.9 us; the launch traced here: 72.3 us
  blocking collectives  45.8 us (63%)
  Pallas kernels  16.8 us (23%)
  waiting for transfers between devices  4.43 us (6%)
  local copies, waits for them, and re-layouts  2.62 us (4%)
  between operations  1.33 us (2%)
  starting transfers between devices  1.27 us (2%)
    all_to_all x3, blocking collectives, exchange(): return lax.all_to_all(value, 'dom', 0, 0, axis_index_groups=same_core)  45.8 us
    pallas_call x6, Pallas kernels, call(): pl.pallas_call(kernel, out_shape=[jax.ShapeDtypeStruct(shape, kind) for s...  16.8 us
    ppermute x4, waiting for transfers between devices, swap(): return lax.ppermute(value, 'dom', pairs)  4.43 us
    unnamed x14, local copies, waits for them, and re-layouts  2.62 us
  transfers between devices with their start and end apart: 5, of which 3 were waited for; matrix products, arithmetic and copies ran while one was open for 0% of the time, Pallas kernels for 0%

profile of v1, /device:TPU:0, one launch (start us, length us, event | category | flops | bytes accessed | tf_op | source)
XLA Modules:
  0.0 72.3 jit_solution(13984128417091148881)
XLA Ops:
  0.6 1.6 %shard_map.146 = (bf16[16,256]{1,0:T(8,128)(2,1)}, bf16[16,256]{1,0:T(8,128)(2,1)}) custom-call(bf16[128,256]{1,0:T(8,128)(2,1)} %nodes_ref.5, s32[2,16]{1,0:T(2,128)} %lists_ref.3), custom_call_target="tpu_custom_call" | custom-call | tf_op jit(solution)/shard_map/pallas_call | solution.py:403
  2.3 0.5 collective-permute-start
  2.7 0.6 collective-permute-start.1
  4.0 0.0 collective-permute-done.near_ref
  4.0 0.0 copy-start.5
  4.0 0.0 collective-permute-done.1.far_ref
  4.1 0.0 copy-start.6
  4.1 0.6 copy-done.5
  4.6 0.0 copy-done.6
  4.6 3.7 %shard_map.147 = (f32[128,256]{1,0:T(8,128)}, bf16[128,256]{1,0:T(8,128)(2,1)}, f32[128,256]{1,0:T(8,128)}, bf16[1536,256]{1,0:T(8,128)(2,1)}, bf16[8,48,256]{2,1,0:T(8,128)(2,1)}) custom-call(bf16[128,256]{1,0:T(8,128)(2,1)} %nodes_ref.5, bf16[16,256]{1,0:T(8,128)(2,1)} %copy-done.5, bf16[16,256]{1,0:T(8,128)(2,1)} %copy-done.6, ...), custom_call_target="tpu_custom_call" | custom-call | tf_op jit(solution)/shard_map/pallas_call | solution.py:403
  8.3 19.2 %all_to_all.15.mine_ref = bf16[8,48,256]{2,1,0:T(8,128)(2,1)S(1)} all-to-all(bf16[8,48,256]{2,1,0:T(8,128)(2,1)} %get-tuple-element.23), channel_id=1, replica_groups={{0,2,4,6,8,10,12,14},{1,3,5,7,9,11,13,15},{16,18,20,22,24,26,28,30},{17..., dimensions={0} | all-to-all | bytes 393216 | tf_op jit(solution)/shard_map/all_to_all | solution.py:448
  27.5 0.0 copy-start.2
  27.5 0.0 collective-permute-start.2
  27.5 1.4 %collective-permute-done.2.theirs_ref = bf16[8,48,256]{2,1,0:T(8,128)(2,1)S(1)} collective-permute-done((bf16[8,48,256]{2,1,0:T(8,128)(2,1)S(1)}, bf16[8,48,256]{2,1,0:T(8,128)(2,1)S(1)}, u32[]{:S(2)}, u32[]{:S(2)}) %collective-permute-start.2) | collective-permute-done | bytes 196640 | tf_op jit(solution)/shard_map/ppermute | solution.py:445
  28.9 0.0 copy-start.4
  28.9 0.0 copy-done.2
  28.9 0.7 copy-done.4
  29.6 5.8 %shard_map.148 = (f32[128,256]{1,0:T(8,128)}, f32[128,256]{1,0:T(8,128)}, f32[3,256,256]{2,1,0:T(8,128)}, f32[1,256]{1,0:T(1,128)}, bf16[432,256]{1,0:T(8,128)(2,1)}, /*index=5*/bf16[400,256]{1,0:T(8,128)(2,1)}) custom-call(bf16[8,48,256]{2,1,0:T(8,128)(2,1)} %copy-done.2, bf16[8,48,256]{2,1,0:T(8,128)(2,1)} %copy-done.4, ...), custom_call_target="tpu_custom_call" | custom-call | tf_op jit(solution)/shard_map/pallas_call | solution.py:403
  35.4 0.2 collective-permute-start.3
  35.6 1.5 %collective-permute-done.3.came_ref = bf16[432,256]{1,0:T(8,128)(2,1)S(1)} collective-permute-done((bf16[432,256]{1,0:T(8,128)(2,1)}, bf16[432,256]{1,0:T(8,128)(2,1)S(1)}, u32[]{:S(2)}, u32[]{:S(2)}) %collective-permute-start.3) | collective-permute-done | bytes 221216 | tf_op jit(solution)/shard_map/ppermute | solution.py:445
  37.1 0.0 copy-start
  37.1 0.7 copy-done
  37.8 1.8 %shard_map.149 = bf16[8,80,256]{2,1,0:T(8,128)(2,1)} custom-call(bf16[400,256]{1,0:T(8,128)(2,1)} %get-tuple-element.29.keep_ref, bf16[432,256]{1,0:T(8,128)(2,1)} %copy-done), custom_call_target="tpu_custom_call" | custom-call | tf_op jit(solution)/shard_map/pallas_call | solution.py:403
  39.6 15.6 %all_to_all.16.blocks_ref = bf16[8,80,256]{2,1,0:T(8,128)(2,1)} all-to-all(bf16[8,80,256]{2,1,0:T(8,128)(2,1)} %shard_map.149), channel_id=1, replica_groups={{0,2,4,6,8,10,12,14},{1,3,5,7,9,11,13,15},{16,18,20,22,24,26,28,30},{17..., dimensions={0} | all-to-all | bytes 655360 | tf_op jit(solution)/shard_map/all_to_all | solution.py:448
  55.2 2.0 %shard_map.150 = (bf16[8,48,256]{2,1,0:T(8,128)(2,1)}, f32[128,256]{1,0:T(8,128)}, f32[2,256]{1,0:T(2,128)}) custom-call(bf16[8,80,256]{2,1,0:T(8,128)(2,1)} %all_to_all.16.blocks_ref, bf16[432,256]{1,0:T(8,128)(2,1)} %copy-done, f32[128,256]{1,0:T(8,128)} %get-tuple-element.31.node_part_ref, s32[2,16]{1,0:T(2,128)} %lists_ref.3, ...), custom_call_target="tpu_custom_call" | custom-call | tf_op jit(solution)/shard_map/pallas_call | solution.py:403
  57.1 11.1 %all_to_all.17.mine_ref = bf16[8,48,256]{2,1,0:T(8,128)(2,1)S(1)} all-to-all(bf16[8,48,256]{2,1,0:T(8,128)(2,1)} %get-tuple-element.34), channel_id=1, replica_groups={{0,2,4,6,8,10,12,14},{1,3,5,7,9,11,13,15},{16,18,20,22,24,26,28,30},{17..., dimensions={0} | all-to-all | bytes 393216 | tf_op jit(solution)/shard_map/all_to_all | solution.py:448
  68.2 0.0 copy-start.1
  68.2 0.0 collective-permute-start.4
  68.2 1.4 %collective-permute-done.4.theirs_ref = bf16[8,48,256]{2,1,0:T(8,128)(2,1)S(1)} collective-permute-done((bf16[8,48,256]{2,1,0:T(8,128)(2,1)S(1)}, bf16[8,48,256]{2,1,0:T(8,128)(2,1)S(1)}, u32[]{:S(2)}, u32[]{:S(2)}) %collective-permute-start.4) | collective-permute-done | bytes 196640 | tf_op jit(solution)/shard_map/ppermute | solution.py:445
  69.6 0.0 copy-done.1
  69.6 0.0 copy-start.3
  69.7 0.7 copy-done.3
  70.3 2.0 %shard_map.151 = f32[768,256]{1,0:T(8,128)} custom-call(bf16[8,48,256]{2,1,0:T(8,128)(2,1)} %copy-done.1, bf16[8,48,256]{2,1,0:T(8,128)(2,1)} %copy-done.3), custom_call_target="tpu_custom_call" | custom-call | tf_op jit(solution)/shard_map/pallas_call | solution.py:403
Async XLA Ops:
  2.3 1.8 %collective-permute-start = (bf16[16,256]{1,0:T(8,128)(2,1)}, bf16[16,256]{1,0:T(8,128)(2,1)S(1)}, u32[]{:S(2)}, u32[]{:S(2)}) collective-permute-start(bf16[16,256]{1,0:T(8,128)(2,1)} %get-tuple-element.21), channel_id=1, source_target_pairs={{0,1},{1,0},{2,3},{3,2},{4,5},{5,4},{6,7},{7,6},{8,9},{9,8},{10,11... | collective-permute-start | bytes 24584 | tf_op jit(solution)/shard_map/ppermute | solution.py:445
  2.7 1.3 %collective-permute-start.1 = (bf16[16,256]{1,0:T(8,128)(2,1)}, bf16[16,256]{1,0:T(8,128)(2,1)S(1)}, u32[]{:S(2)}, u32[]{:S(2)}) collective-permute-start(bf16[16,256]{1,0:T(8,128)(2,1)} %get-tuple-element.22), channel_id=1, source_target_pairs={{1,2},{3,4},{5,6},{7,8},{9,10},{11,12},{13,14},{2,1},{4,3},{6,5},{... | collective-permute-start | bytes 24584 | tf_op jit(solution)/shard_map/ppermute | solution.py:453
  4.0 0.6 copy-start.5
  4.1 0.6 copy-start.6
  27.5 1.4 %copy-start.2 = (bf16[8,48,256]{2,1,0:T(8,128)(2,1)}, bf16[8,48,256]{2,1,0:T(8,128)(2,1)S(1)}, u32[]{:S(2)}) copy-start(bf16[8,48,256]{2,1,0:T(8,128)(2,1)S(1)} %all_to_all.15.mine_ref) | copy-start | bytes 589828
  27.5 1.4 %collective-permute-start.2 = (bf16[8,48,256]{2,1,0:T(8,128)(2,1)S(1)}, bf16[8,48,256]{2,1,0:T(8,128)(2,1)S(1)}, u32[]{:S(2)}, u32[]{:S(2)}) collective-permute-start(bf16[8,48,256]{2,1,0:T(8,128)(2,1)S(1)} %all_to_all.15.mine_ref), channel_id=1, source_target_pairs={{0,1},{1,0},{2,3},{3,2},{4,5},{5,4},{6,7},{7,6},{8,9},{9,8},{10,11... | collective-permute-start | bytes 589832 | tf_op jit(solution)/shard_map/ppermute | solution.py:445
  28.9 0.7 copy-start.4
  35.4 1.7 %collective-permute-start.3 = (bf16[432,256]{1,0:T(8,128)(2,1)}, bf16[432,256]{1,0:T(8,128)(2,1)S(1)}, u32[]{:S(2)}, u32[]{:S(2)}) collective-permute-start(bf16[432,256]{1,0:T(8,128)(2,1)} %get-tuple-element.30), channel_id=1, source_target_pairs={{0,1},{1,0},{2,3},{3,2},{4,5},{5,4},{6,7},{7,6},{8,9},{9,8},{10,11... | collective-permute-start | bytes 663560 | tf_op jit(solution)/shard_map/ppermute | solution.py:445
  37.1 0.7 copy-start
  68.2 1.4 %copy-start.1 = (bf16[8,48,256]{2,1,0:T(8,128)(2,1)}, bf16[8,48,256]{2,1,0:T(8,128)(2,1)S(1)}, u32[]{:S(2)}) copy-start(bf16[8,48,256]{2,1,0:T(8,128)(2,1)S(1)} %all_to_all.17.mine_ref) | copy-start | bytes 589828
  68.2 1.4 %collective-permute-start.4 = (bf16[8,48,256]{2,1,0:T(8,128)(2,1)S(1)}, bf16[8,48,256]{2,1,0:T(8,128)(2,1)S(1)}, u32[]{:S(2)}, u32[]{:S(2)}) collective-permute-start(bf16[8,48,256]{2,1,0:T(8,128)(2,1)S(1)} %all_to_all.17.mine_ref), channel_id=1, source_target_pairs={{0,1},{1,0},{2,3},{3,2},{4,5},{5,4},{6,7},{7,6},{8,9},{9,8},{10,11... | collective-permute-start | bytes 589832 | tf_op jit(solution)/shard_map/ppermute | solution.py:445
  69.6 0.7 copy-start.3

commit v2 on v1

--- a/solution.py
+++ b/solution.py
@@ -11,7 +11,7 @@
 F32 = jnp.float32
 EDGE_BLOCK = 128
 ROW_TILE = 16
-VMEM_LIMIT = 56 * 1024 * 1024
+MIB = 1024 * 1024
 
 
 def dot(left, right):
@@ -397,7 +397,7 @@
             out_ref[start : start + count, :] = jnp.where(odd == side, mine, theirs).astype(F32)
 
 
-def call(kernel, outs, args, scratch=(), scalars=()):
+def call(kernel, outs, args, room, scratch=(), scalars=()):
     whole = pl.BlockSpec(memory_space=pltpu.VMEM)
     scalar = pl.BlockSpec(memory_space=pltpu.SMEM)
     return pl.pallas_call(
@@ -406,7 +406,7 @@
         in_specs=[scalar if spot in scalars else whole for spot in range(len(args))],
         out_specs=[whole] * len(outs),
         scratch_shapes=[pltpu.VMEM(shape, kind) for shape, kind in scratch],
-        compiler_params=pltpu.CompilerParams(vmem_limit_bytes=VMEM_LIMIT),
+        compiler_params=pltpu.CompilerParams(vmem_limit_bytes=room * MIB),
     )(*args)
 
 
@@ -448,7 +448,7 @@
         return lax.all_to_all(value, "dom", 0, 0, axis_index_groups=same_core)
 
     near, far = call(
-        pick_kernel, [((rim, width), BF16), ((rim, width), BF16)], (nodes, send_lists)
+        pick_kernel, [((rim, width), BF16), ((rim, width), BF16)], (nodes, send_lists), 2
     )
     far = lax.ppermute(far, "dom", across)
     near = swap(near)
@@ -478,6 +478,7 @@
             cotangent,
             coarse_ends,
         ),
+        16,
         scratch=[((slots, width), BF16), ((link_rows, width), F32)],
         scalars=(6,),
     )
@@ -516,6 +517,7 @@
             slopes_sum,
             slopes,
         ),
+        20 if total <= 256 else 56,
         scratch=[
             ((link_rows, width), F32),
             ((edges2, width), BF16),
@@ -529,7 +531,7 @@
     )
     came = swap(send)
     (blocks,) = call(
-        pair_kernel, [((chips, rows + ROW_TILE + rim, width), BF16)], (keep, came)
+        pair_kernel, [((chips, rows + ROW_TILE + rim, width), BF16)], (keep, came), 4
     )
     blocks = exchange(blocks)
     part, node_grads, bias_grads = call(
@@ -540,10 +542,11 @@
             ((2, width), F32),
         ],
         (blocks, came, node_part, send_lists, bias2),
+        4,
     )
     mine = exchange(part)
     theirs = swap(mine)
-    (fine_grads,) = call(join_kernel, [((3 * width, width), F32)], (mine, theirs))
+    (fine_grads,) = call(join_kernel, [((3 * width, width), F32)], (mine, theirs), 4)
     return moved, node_grads, fine_grads.reshape(3, width, width), coarse_grads, bias_grads
 
 

time: 72.9 us -> 63.3 us (0.87)
  Pallas kernels: 16.8 us -> 7.3 us
  local copies, waits for them, and re-layouts: 2.62 us -> 5.39 us
  blocking collectives: 45.8 us -> 43.1 us
    pallas_call x6, Pallas kernels: 16.8 us -> 7.3 us  [call(): pl.pallas_call(kernel, out_shape=[jax.ShapeDtypeStruct(shape, kind) for s...]
    unnamed x14 -> x30, local copies, waits for them, and re-layouts: 2.62 us -> 5.39 us
    all_to_all x3, blocking collectives: 45.8 us -> 43.1 us  [exchange(): return lax.all_to_all(value, 'dom', 0, 0, axis_index_groups=same_core)]
where the time goes in v2:
time: 63.3 us; the launch traced here: 62.8 us
  blocking collectives  43.1 us (68%)
  Pallas kernels  7.3 us (12%)
  local copies, waits for them, and re-layouts  5.39 us (9%)
  waiting for transfers between devices  4.22 us (7%)
  starting transfers between devices  1.43 us (2%)
  between operations  1.4 us (2%)
    all_to_all x3, blocking collectives, exchange(): return lax.all_to_all(value, 'dom', 0, 0, axis_index_groups=same_core)  43.1 us
    pallas_call x6, Pallas kernels, call(): pl.pallas_call(kernel, out_shape=[jax.ShapeDtypeStruct(shape, kind) for s...  7.3 us
    unnamed x30, local copies, waits for them, and re-layouts  5.39 us
    ppermute x4, waiting for transfers between devices, swap(): return lax.ppermute(value, 'dom', pairs)  4.22 us
  transfers between devices with their start and end apart: 5, of which 3 were waited for; matrix products, arithmetic and copies ran while one was open for 0% of the time, Pallas kernels for 0%

profile of v2, /device:TPU:0, one launch (start us, length us, event | category | flops | bytes accessed | tf_op | source)
XLA Modules:
  0.0 62.8 jit_solution(2573715575788315731)
XLA Ops:
  0.6 0.0 copy-start.2
  0.6 0.8 %copy-done.2 = bf16[128,256]{1,0:T(8,128)(2,1)S(1)} copy-done((bf16[128,256]{1,0:T(8,128)(2,1)S(1)}, bf16[128,256]{1,0:T(8,128)(2,1)}, u32[]{:S(2)}) %copy-start.2) | copy-done | bytes 65560
  1.5 0.0 copy-start.11
  1.5 0.7 %copy-done.11 = s32[2,16]{1,0:T(2,128)S(1)} copy-done((s32[2,16]{1,0:T(2,128)S(1)}, s32[2,16]{1,0:T(2,128)}, u32[]{:S(2)}) %copy-start.11) | copy-done | bytes 152
  2.2 0.0 copy-start.3
  2.2 0.2 shard_map.146
  2.3 0.0 copy-start.9
  2.3 0.5 collective-permute-start
  2.8 0.0 copy-start.10
  2.8 0.8 %collective-permute-start.1 = (bf16[16,256]{1,0:T(8,128)(2,1)S(1)}, bf16[16,256]{1,0:T(8,128)(2,1)S(1)}, u32[]{:S(2)}, u32[]{:S(2)}) collective-permute-start(bf16[16,256]{1,0:T(8,128)(2,1)S(1)} %get-tuple-element.22), channel_id=1, source_target_pairs={{1,2},{3,4},{5,6},{7,8},{9,10},{11,12},{13,14},{2,1},{4,3},{6,5},{... | collective-permute-start | bytes 24584 | tf_op jit(solution)/shard_map/ppermute | solution.py:453
  4.2 0.0 copy-start.13
  4.2 0.0 copy-start.14
  4.3 0.0 collective-permute-done.near_ref
  4.3 0.0 collective-permute-done.1.far_ref
  4.3 0.0 copy-done.3
  4.3 0.0 copy-done.9
  4.3 0.0 copy-done.10
  4.3 0.6 copy-done.13
  4.9 0.0 copy-done.14
  4.9 0.0 copy-start
  4.9 1.0 %copy-done = bf16[3,256,256]{2,1,0:T(8,128)(2,1)S(1)} copy-done((bf16[3,256,256]{2,1,0:T(8,128)(2,1)S(1)}, bf16[3,256,256]{2,1,0:T(8,128)(2,1)}, u32[]{:S(2)}) %copy-start) | copy-done | bytes 393240
  5.9 0.0 copy-start.5
  5.9 0.8 %copy-done.5 = bf16[128,256]{1,0:T(8,128)(2,1)S(1)} copy-done((bf16[128,256]{1,0:T(8,128)(2,1)S(1)}, bf16[128,256]{1,0:T(8,128)(2,1)}, u32[]{:S(2)}) %copy-start.5) | copy-done | bytes 65560
  6.8 0.0 copy-start.7
  6.8 0.7 %copy-done.7 = s32[2,1536]{1,0:T(2,128)S(1)} copy-done((s32[2,1536]{1,0:T(2,128)S(1)}, s32[2,1536]{1,0:T(2,128)}, u32[]{:S(2)}) %copy-start.7) | copy-done | bytes 12312
  7.5 0.0 copy-start.1
  7.5 0.0 copy-start.4
  7.5 1.9 %shard_map.147 = (f32[128,256]{1,0:T(8,128)S(1)}, bf16[128,256]{1,0:T(8,128)(2,1)S(1)}, f32[128,256]{1,0:T(8,128)S(1)}, bf16[1536,256]{1,0:T(8,128)(2,1)S(1)}, bf16[8,48,256]{2,1,0:T(8,128)(2,1)S(1)}) custom-call(bf16[128,256]{1,0:T(8,128)(2,1)S(1)} %copy-done.3, bf16[16,256]{1,0:T(8,128)(2,1)S(1)} %collective-permute-done.near_ref, ...), custom_call_target="tpu_custom_call" | custom-call | tf_op jit(solution)/shard_map/pallas_call | solution.py:403
  9.4 0.0 copy-start.6
  9.4 0.0 copy-start.8
  9.4 18.3 %all_to_all.15.mine_ref = bf16[8,48,256]{2,1,0:T(8,128)(2,1)S(1)} all-to-all(bf16[8,48,256]{2,1,0:T(8,128)(2,1)S(1)} %get-tuple-element.23), channel_id=1, replica_groups={{0,2,4,6,8,10,12,14},{1,3,5,7,9,11,13,15},{16,18,20,22,24,26,28,30},{17..., dimensions={0} | all-to-all | bytes 393216 | tf_op jit(solution)/shard_map/all_to_all | solution.py:448
  27.7 0.0 collective-permute-start.2
  27.7 1.4 %collective-permute-done.2.theirs_ref = bf16[8,48,256]{2,1,0:T(8,128)(2,1)S(1)} collective-permute-done((bf16[8,48,256]{2,1,0:T(8,128)(2,1)S(1)}, bf16[8,48,256]{2,1,0:T(8,128)(2,1)S(1)}, u32[]{:S(2)}, u32[]{:S(2)}) %collective-permute-start.2) | collective-permute-done | bytes 196640 | tf_op jit(solution)/shard_map/ppermute | solution.py:445
  29.1 0.0 copy-done.1
  29.1 0.0 copy-done.4
  29.1 0.0 copy-done.6
  29.2 0.0 copy-done.8
  29.2 3.3 %shard_map.148 = (f32[128,256]{1,0:T(8,128)}, f32[128,256]{1,0:T(8,128)S(1)}, f32[3,256,256]{2,1,0:T(8,128)}, f32[1,256]{1,0:T(1,128)S(1)}, bf16[432,256]{1,0:T(8,128)(2,1)S(1)}, /*index=5*/bf16[400,256]{1,0:T(8,128)(2,1)S(1)}) custom-call(bf16[8,48,256]{2,1,0:T(8,128)(2,1)S(1)} %all_to_all.15.mine_ref, ...), custom_call_target="tpu_custom_call" | custom-call | tf_op jit(solution)/shard_map/pallas_call | solution.py:403
  32.5 0.2 collective-permute-start.3
  32.7 1.3 %collective-permute-done.3.came_ref = bf16[432,256]{1,0:T(8,128)(2,1)S(1)} collective-permute-done((bf16[432,256]{1,0:T(8,128)(2,1)S(1)}, bf16[432,256]{1,0:T(8,128)(2,1)S(1)}, u32[]{:S(2)}, u32[]{:S(2)}) %collective-permute-start.3) | collective-permute-done | bytes 221216 | tf_op jit(solution)/shard_map/ppermute | solution.py:445
  34.0 0.1 shard_map.149
  34.1 14.2 %all_to_all.16.blocks_ref = bf16[8,80,256]{2,1,0:T(8,128)(2,1)S(1)} all-to-all(bf16[8,80,256]{2,1,0:T(8,128)(2,1)S(1)} %shard_map.149), channel_id=1, replica_groups={{0,2,4,6,8,10,12,14},{1,3,5,7,9,11,13,15},{16,18,20,22,24,26,28,30},{17..., dimensions={0} | all-to-all | bytes 655360 | tf_op jit(solution)/shard_map/all_to_all | solution.py:448
  48.2 0.7 %copy-done.12 = s32[2,16]{1,0:T(2,128)S(1)} copy-done((s32[2,16]{1,0:T(2,128)S(1)}, s32[2,16]{1,0:T(2,128)}, u32[]{:S(2)}) %copy-start.12) | copy-done | bytes 152
  48.9 0.8 %shard_map.150 = (bf16[8,48,256]{2,1,0:T(8,128)(2,1)S(1)}, f32[128,256]{1,0:T(8,128)}, f32[2,256]{1,0:T(2,128)}) custom-call(bf16[8,80,256]{2,1,0:T(8,128)(2,1)S(1)} %all_to_all.16.blocks_ref, bf16[432,256]{1,0:T(8,128)(2,1)S(1)} %collective-permute-done.3.came_ref, f32[128,256]{1,0:T(8,128)S(1)} %get-tuple-element.31.node_part_ref, s32[2,16]{1,0:T(2,128)S(1)} %copy-done.12, ...), custom_call_target="tpu_custom_call" | custom-call | tf_op jit(solution)/shard_map/pallas_call | solution.py:403
  49.8 10.6 %all_to_all.17.mine_ref = bf16[8,48,256]{2,1,0:T(8,128)(2,1)S(1)} all-to-all(bf16[8,48,256]{2,1,0:T(8,128)(2,1)S(1)} %get-tuple-element.34), channel_id=1, replica_groups={{0,2,4,6,8,10,12,14},{1,3,5,7,9,11,13,15},{16,18,20,22,24,26,28,30},{17..., dimensions={0} | all-to-all | bytes 393216 | tf_op jit(solution)/shard_map/all_to_all | solution.py:448
  60.4 0.0 collective-permute-start.4
  60.4 1.4 %collective-permute-done.4.theirs_ref = bf16[8,48,256]{2,1,0:T(8,128)(2,1)S(1)} collective-permute-done((bf16[8,48,256]{2,1,0:T(8,128)(2,1)S(1)}, bf16[8,48,256]{2,1,0:T(8,128)(2,1)S(1)}, u32[]{:S(2)}, u32[]{:S(2)}) %collective-permute-start.4) | collective-permute-done | bytes 196640 | tf_op jit(solution)/shard_map/ppermute | solution.py:445
  61.8 1.0 %shard_map.151 = f32[768,256]{1,0:T(8,128)} custom-call(bf16[8,48,256]{2,1,0:T(8,128)(2,1)S(1)} %all_to_all.17.mine_ref, bf16[8,48,256]{2,1,0:T(8,128)(2,1)S(1)} %collective-permute-done.4.theirs_ref), custom_call_target="tpu_custom_call" | custom-call | tf_op jit(solution)/shard_map/pallas_call | solution.py:403
  (1 shorter events, 0.0 us)
Async XLA Ops:
  0.6 0.8 %copy-start.2 = (bf16[128,256]{1,0:T(8,128)(2,1)S(1)}, bf16[128,256]{1,0:T(8,128)(2,1)}, u32[]{:S(2)}) copy-start(bf16[128,256]{1,0:T(8,128)(2,1)} %nodes_ref.5) | copy-start | bytes 196612
  1.5 0.7 %copy-start.11 = (s32[2,16]{1,0:T(2,128)S(1)}, s32[2,16]{1,0:T(2,128)}, u32[]{:S(2)}) copy-start(s32[2,16]{1,0:T(2,128)} %lists_ref.3) | copy-start | bytes 388
  2.2 2.1 %copy-start.3 = (bf16[128,256]{1,0:T(8,128)(2,1)S(1)}, bf16[128,256]{1,0:T(8,128)(2,1)}, u32[]{:S(2)}) copy-start(bf16[128,256]{1,0:T(8,128)(2,1)} %nodes_ref.5) | copy-start | bytes 196612
  2.3 2.0 %copy-start.9 = (s32[8,16]{1,0:T(8,128)S(1)}, s32[8,16]{1,0:T(8,128)}, u32[]{:S(2)}) copy-start(s32[8,16]{1,0:T(8,128)} %members_ref.3) | copy-start | bytes 1540
  2.3 1.9 %collective-permute-start = (bf16[16,256]{1,0:T(8,128)(2,1)S(1)}, bf16[16,256]{1,0:T(8,128)(2,1)S(1)}, u32[]{:S(2)}, u32[]{:S(2)}) collective-permute-start(bf16[16,256]{1,0:T(8,128)(2,1)S(1)} %get-tuple-element.21), channel_id=1, source_target_pairs={{0,1},{1,0},{2,3},{3,2},{4,5},{5,4},{6,7},{7,6},{8,9},{9,8},{10,11... | collective-permute-start | bytes 24584 | tf_op jit(solution)/shard_map/ppermute | solution.py:445
  2.8 1.5 %copy-start.10 = (f32[2,256]{1,0:T(2,128)S(1)}, f32[2,256]{1,0:T(2,128)}, u32[]{:S(2)}) copy-start(f32[2,256]{1,0:T(2,128)} %biases_ref.3) | copy-start | bytes 6148
  2.8 1.5 %collective-permute-start.1 = (bf16[16,256]{1,0:T(8,128)(2,1)S(1)}, bf16[16,256]{1,0:T(8,128)(2,1)S(1)}, u32[]{:S(2)}, u32[]{:S(2)}) collective-permute-start(bf16[16,256]{1,0:T(8,128)(2,1)S(1)} %get-tuple-element.22), channel_id=1, source_target_pairs={{1,2},{3,4},{5,6},{7,8},{9,10},{11,12},{13,14},{2,1},{4,3},{6,5},{... | collective-permute-start | bytes 24584 | tf_op jit(solution)/shard_map/ppermute | solution.py:453
  4.2 0.7 %copy-start.13 = (s32[128]{0:T(128)S(1)}, s32[128]{0:T(128)}, u32[]{:S(2)}) copy-start(s32[128]{0:T(128)} %param.20) | copy-start | bytes 1540
  4.2 0.7 %copy-start.14 = (s32[2,48]{1,0:T(2,128)S(1)}, s32[2,48]{1,0:T(2,128)}, u32[]{:S(2)}) copy-start(s32[2,48]{1,0:T(2,128)} %links_ref.1) | copy-start | bytes 1156
  4.9 1.0 %copy-start = (bf16[3,256,256]{2,1,0:T(8,128)(2,1)S(1)}, bf16[3,256,256]{2,1,0:T(8,128)(2,1)}, u32[]{:S(2)}) copy-start(bf16[3,256,256]{2,1,0:T(8,128)(2,1)} %weights_ref.3) | copy-start | bytes 1179652
  5.9 0.8 %copy-start.5 = (bf16[128,256]{1,0:T(8,128)(2,1)S(1)}, bf16[128,256]{1,0:T(8,128)(2,1)}, u32[]{:S(2)}) copy-start(bf16[128,256]{1,0:T(8,128)(2,1)} %cotangent_ref.3) | copy-start | bytes 196612
  6.8 0.7 %copy-start.7 = (s32[2,1536]{1,0:T(2,128)S(1)}, s32[2,1536]{1,0:T(2,128)}, u32[]{:S(2)}) copy-start(s32[2,1536]{1,0:T(2,128)} %ends_ref.3) | copy-start | bytes 36868
  7.5 21.7 %copy-start.1 = (bf16[3,256,256]{2,1,0:T(8,128)(2,1)S(1)}, bf16[3,256,256]{2,1,0:T(8,128)(2,1)}, u32[]{:S(2)}) copy-start(bf16[3,256,256]{2,1,0:T(8,128)(2,1)} %weights_ref.3) | copy-start | bytes 1179652
  7.5 21.7 %copy-start.4 = (bf16[3,256,256]{2,1,0:T(8,128)(2,1)S(1)}, bf16[3,256,256]{2,1,0:T(8,128)(2,1)}, u32[]{:S(2)}) copy-start(bf16[3,256,256]{2,1,0:T(8,128)(2,1)} %coarse_weights_ref.1) | copy-start | bytes 1179652
  9.4 19.7 %copy-start.6 = (bf16[128,256]{1,0:T(8,128)(2,1)S(1)}, bf16[128,256]{1,0:T(8,128)(2,1)}, u32[]{:S(2)}) copy-start(bf16[128,256]{1,0:T(8,128)(2,1)} %cotangent_ref.3) | copy-start | bytes 196612
  9.4 19.7 %copy-start.8 = (s32[2,1536]{1,0:T(2,128)S(1)}, s32[2,1536]{1,0:T(2,128)}, u32[]{:S(2)}) copy-start(s32[2,1536]{1,0:T(2,128)} %ends_ref.3) | copy-start | bytes 36868
  27.7 1.4 %collective-permute-start.2 = (bf16[8,48,256]{2,1,0:T(8,128)(2,1)S(1)}, bf16[8,48,256]{2,1,0:T(8,128)(2,1)S(1)}, u32[]{:S(2)}, u32[]{:S(2)}) collective-permute-start(bf16[8,48,256]{2,1,0:T(8,128)(2,1)S(1)} %all_to_all.15.mine_ref), channel_id=1, source_target_pairs={{0,1},{1,0},{2,3},{3,2},{4,5},{5,4},{6,7},{7,6},{8,9},{9,8},{10,11... | collective-permute-start | bytes 589832 | tf_op jit(solution)/shard_map/ppermute | solution.py:445
  32.5 1.5 %collective-permute-start.3 = (bf16[432,256]{1,0:T(8,128)(2,1)S(1)}, bf16[432,256]{1,0:T(8,128)(2,1)S(1)}, u32[]{:S(2)}, u32[]{:S(2)}) collective-permute-start(bf16[432,256]{1,0:T(8,128)(2,1)S(1)} %get-tuple-element.30), channel_id=1, source_target_pairs={{0,1},{1,0},{2,3},{3,2},{4,5},{5,4},{6,7},{7,6},{8,9},{9,8},{10,11... | collective-permute-start | bytes 663560 | tf_op jit(solution)/shard_map/ppermute | solution.py:445
  48.2 0.7 %copy-start.12 = (s32[2,16]{1,0:T(2,128)S(1)}, s32[2,16]{1,0:T(2,128)}, u32[]{:S(2)}) copy-start(s32[2,16]{1,0:T(2,128)} %lists_ref.3) | copy-start | bytes 388
  60.4 1.4 %collective-permute-start.4 = (bf16[8,48,256]{2,1,0:T(8,128)(2,1)S(1)}, bf16[8,48,256]{2,1,0:T(8,128)(2,1)S(1)}, u32[]{:S(2)}, u32[]{:S(2)}) collective-permute-start(bf16[8,48,256]{2,1,0:T(8,128)(2,1)S(1)} %all_to_all.17.mine_ref), channel_id=1, source_target_pairs={{0,1},{1,0},{2,3},{3,2},{4,5},{5,4},{6,7},{7,6},{8,9},{9,8},{10,11... | collective-permute-start | bytes 589832 | tf_op jit(solution)/shard_map/ppermute | solution.py:445

commit v3 on v2

v3 whole, which is shorter than its diff:
```python
import functools
import math

import jax
import jax.numpy as jnp
from jax import lax
from jax.experimental import pallas as pl
from jax.experimental.pallas import tpu as pltpu
from jax.sharding import PartitionSpec as P

BF16 = jnp.bfloat16
F32 = jnp.float32
EDGE_BLOCK = 128
ROW_TILE = 16
MIB = 1024 * 1024


def dot(left, right):
    return jnp.dot(left, right, preferred_element_type=F32)


def dot_tn(left, right):
    return lax.dot_general(left, right, (((0,), (0,)), ((), ())), preferred_element_type=F32)


def dot_nt(left, right):
    return lax.dot_general(left, right, (((1,), (1,)), ((), ())), preferred_element_type=F32)


def split(value):
    high = value.astype(BF16)
    return high, (value - high.astype(F32)).astype(BF16)


def one_hot_rows(index_row, count):
    spots = lax.broadcasted_iota(jnp.int32, (count, index_row.shape[1]), 0)
    return jnp.where(spots == index_row, 1.0, 0.0).astype(BF16)


def one_hot_cols(index_col, count):
    spots = lax.broadcasted_iota(jnp.int32, (index_col.shape[0], count), 1)
    return jnp.where(spots == index_col, 1.0, 0.0).astype(BF16)


def to_column(index_row):
    return jnp.transpose(jnp.broadcast_to(index_row, (8, index_row.shape[1])))[:, :1]


def silu_and_slope(value):
    sig = 0.5 * jnp.tanh(0.5 * value) + 0.5
    message = value * sig
    return message, sig + message * (1.0 - sig)


def membership(members, node_count):
    spots = lax.broadcasted_iota(jnp.int32, (node_count, members.shape[1]), 0)
    total = jnp.zeros(spots.shape, F32)
    for row in range(members.shape[0]):
        total = total + jnp.where(spots == members[row : row + 1], 1.0, 0.0)
    return total.astype(BF16)


def place():
    me = lax.axis_index("dom")
    return me, lax.rem(me, 2), lax.div(me, 2)


def live_rows(ends_ref, live_ref, row):
    index = ends_ref[row : row + 1, :]
    slot = lax.broadcasted_iota(jnp.int32, index.shape, 1)
    return jnp.where(slot < live_ref[0] * EDGE_BLOCK, index, -1)


def pick_kernel(nodes_ref, lists_ref, near_ref, far_ref, nodes_out, lists_out, sems):
    copies = (
        pltpu.make_async_copy(nodes_ref, nodes_out, sems.at[0]),
        pltpu.make_async_copy(lists_ref, lists_out, sems.at[1]),
    )
    for copy in copies:
        copy.start()
    for copy in copies:
        copy.wait()
    _, odd, _ = place()
    lists = lists_out[...]
    near = jnp.where(odd == 1, lists[0:1], lists[1:2])
    far = jnp.where(odd == 1, lists[1:2], lists[0:1])
    nodes = nodes_out[...]
    near_ref[...] = dot_tn(one_hot_rows(near, nodes.shape[0]), nodes).astype(BF16)
    far_ref[...] = dot_tn(one_hot_rows(far, nodes.shape[0]), nodes).astype(BF16)


def rims(near, far, odd):
    return jnp.where(odd == 1, near, far), jnp.where(odd == 1, far, near)


def prepare_kernel(
    ndom,
    rim,
    nodes_ref,
    weights_hbm,
    biases_hbm,
    ends_hbm,
    live_ref,
    members_hbm,
    parents_hbm,
    cotangent_hbm,
    links_hbm,
    weights_ref,
    ends_ref,
    cotangent_ref,
    pre_ref,
    rim_hot_ref,
    to_nodes_ref,
    into_ref,
    share_ref,
    family_ref,
    side_ref,
    biases_ref,
    members_ref,
    parents_ref,
    links_ref,
    link_ref,
    sems,
):
    pairs = (
        (ends_hbm, ends_ref),
        (weights_hbm, weights_ref),
        (biases_hbm, biases_ref),
        (members_hbm, members_ref),
        (parents_hbm, parents_ref),
        (cotangent_hbm, cotangent_ref),
        (links_hbm, links_ref),
    )
    copies = [
        pltpu.make_async_copy(source, target, sems.at[spot])
        for spot, (source, target) in enumerate(pairs)
    ]
    for copy in copies:
        copy.start()
    for copy in copies:
        copy.wait()
    me, _, _ = place()
    nodes = nodes_ref[...]
    node_count, width = nodes.shape
    coarse_count = family_ref.shape[0]
    slots = ends_ref.shape[1]
    src_proj = dot(nodes, weights_ref[0]).astype(BF16)
    dst_proj = dot(nodes, weights_ref[1]).astype(BF16)
    bias = biases_ref[0:1, :]
    chunk = 2 * EDGE_BLOCK
    for start in range(0, slots, chunk):
        span = slice(start, start + chunk)
        senders = to_column(ends_ref[0:1, span])
        receivers = to_column(ends_ref[1:2, span])
        to_nodes = one_hot_cols(receivers, node_count)
        to_nodes_ref[span, :] = to_nodes
        inner = one_hot_cols(senders - rim, node_count)
        spot = jnp.where(
            senders < rim, senders, jnp.where(senders < rim + node_count, -1, senders - node_count)
        )
        rim_hot_ref[span, :] = one_hot_cols(spot, 2 * rim)
        pre_ref[span, :] = dot(inner, src_proj) + dot(to_nodes, dst_proj) + bias
    into_ref[...] = one_hot_rows(live_rows(ends_ref, live_ref, 1), node_count)
    share_ref[...] = membership(members_ref[...], node_count)
    family = one_hot_rows(parents_ref[...], coarse_count)
    family_ref[...] = family
    side_ref[:coarse_count, :] = dot(family, cotangent_ref[...]).astype(BF16)

    links = links_ref[...]
    own = links.shape[1]
    pieces = -(-own * ndom // width)
    spot = lax.broadcasted_iota(jnp.int32, (own, pieces * width), 1)
    source = lax.broadcasted_iota(jnp.int32, (own, pieces * width), 0)
    spread = jnp.where(spot == source + me * own, 1.0, 0.0).astype(BF16)
    coded = (
        dot((links >> 8).astype(F32).astype(BF16), spread),
        dot((links & 255).astype(F32).astype(BF16), spread),
    )
    link_ref[...] = jnp.zeros(link_ref.shape, F32)
    for part in range(2):
        for end in range(2):
            for piece in range(pieces):
                row = (part * 2 + end) * pieces + piece
                link_ref[row : row + 1, :] = coded[part][
                    end : end + 1, piece * width : (piece + 1) * width
                ]
    side_ref[coarse_count:, :] = link_ref[...].astype(BF16)


def forward_kernel(
    member_count,
    nodes_ref,
    near_ref,
    far_ref,
    weights_ref,
    pre_ref,
    rim_hot_ref,
    into_ref,
    share_ref,
    side_ref,
    updated_ref,
    summed_ref,
    slopes_ref,
    packet_ref,
    message_ref,
):
    _, odd, _ = place()
    nodes = nodes_ref[...]
    low, high = rims(near_ref[...], far_ref[...], odd)
    rim_proj = dot(jnp.concatenate([low, high], 0), weights_ref[0]).astype(BF16)
    slots = pre_ref.shape[0]
    chunk = 2 * EDGE_BLOCK
    for start in range(0, slots, chunk):
        span = slice(start, start + chunk)
        pre = pre_ref[span, :] + dot(rim_hot_ref[span, :], rim_proj)
        message, slope = silu_and_slope(pre)
        message_ref[span, :] = message.astype(BF16)
        slopes_ref[span, :] = slope.astype(BF16)
    summed = dot(into_ref[...], message_ref[...]).astype(BF16)
    summed_ref[...] = summed
    updated = nodes.astype(F32) + dot(summed, weights_ref[2])
    updated_ref[...] = updated
    share = share_ref[...]
    high, low = split(updated)
    pooled = dot_tn(share, high) + dot_tn(share, low)
    coarse = (pooled / member_count).astype(BF16)
    coarse_count = coarse.shape[0]
    side = side_ref[...]
    for chip in range(packet_ref.shape[0]):
        packet_ref[chip, :coarse_count, :] = coarse
        packet_ref[chip, coarse_count:, :] = side


def between_kernel(into_ref, slopes_ref, ends_ref, live_ref, slopes_sum_ref, back_ref):
    slopes_sum_ref[...] = dot(into_ref[...], slopes_ref[...])
    back_ref[...] = one_hot_rows(live_rows(ends_ref, live_ref, 0), back_ref.shape[0])


def ordered(mine_ref, theirs_ref, odd, start, count):
    blocks = []
    for chip in range(mine_ref.shape[0]):
        mine = mine_ref[chip, start : start + count, :]
        theirs = theirs_ref[chip, start : start + count, :]
        blocks.append(jnp.where(odd == 1, theirs, mine))
        blocks.append(jnp.where(odd == 1, mine, theirs))
    return blocks


def backward_kernel(
    ndom,
    edge_count2,
    member_count,
    mine_ref,
    theirs_ref,
    coarse_weights_ref,
    biases_ref,
    nodes_ref,
    near_ref,
    far_ref,
    weights_ref,
    share_ref,
    cotangent_ref,
    summed_ref,
    slopes_sum_ref,
    slopes_ref,
    to_nodes_ref,
    back_ref,
    send_ref,
    keep_ref,
    far_grad_ref,
    coarse_ref,
    parent_ref,
    coarse_sum_ref,
    grad_src2_ref,
    grad_dst2_ref,
    bias2_ref,
    grad_updated_ref,
    grad_src_ref,
    grad_dst_ref,
    link_ref,
    message2_ref,
    slope2_ref,
    edge2_ref,
    grads_ref,
    edge_ref,
):
    me, odd, _ = place()
    nodes = nodes_ref[...]
    node_count, width = nodes.shape
    coarse_count = share_ref.shape[1]
    total = ndom * coarse_count

    coarse = jnp.concatenate(ordered(mine_ref, theirs_ref, odd, 0, coarse_count), 0)
    parent_all = jnp.concatenate(
        ordered(mine_ref, theirs_ref, odd, coarse_count, coarse_count), 0
    )
    link_rows = link_ref.shape[0]
    gathered = jnp.zeros(link_ref.shape, F32)
    for chip in range(mine_ref.shape[0]):
        for ref in (mine_ref, theirs_ref):
            gathered = gathered + ref[
                chip, 2 * coarse_count : 2 * coarse_count + link_rows, :
            ].astype(F32)
    link_ref[...] = gathered
    pieces = -(-edge_count2 // width)
    ends2 = []
    for end in range(2):
        rows = []
        for piece in range(pieces):
            top = end * pieces + piece
            bottom = (2 + end) * pieces + piece
            code = 256.0 * link_ref[top : top + 1, :] + link_ref[bottom : bottom + 1, :]
            spot = lax.broadcasted_iota(jnp.int32, code.shape, 1) + piece * width
            rows.append(jnp.where(spot < edge_count2, code.astype(jnp.int32), -1))
        ends2.append(rows)
    src2 = dot(coarse, coarse_weights_ref[0]).astype(BF16)
    dst2 = dot(coarse, coarse_weights_ref[1]).astype(BF16)
    grad_agg2 = dot_nt(parent_all, coarse_weights_ref[2])
    grad_agg2_near = grad_agg2.astype(BF16)
    bias = biases_ref[1:2, :]
    for piece in range(pieces):
        span = slice(piece * width, (piece + 1) * width)
        from_nodes = one_hot_cols(to_column(ends2[0][piece]), total)
        to_nodes = one_hot_cols(to_column(ends2[1][piece]), total)
        pre = dot(from_nodes, src2) + dot(to_nodes, dst2) + bias
        message, slope = silu_and_slope(pre)
        message2_ref[span, :] = message.astype(BF16)
        slope2_ref[span, :] = slope.astype(BF16)
        edge2_ref[span, :] = (dot(to_nodes, grad_agg2_near) * slope).astype(BF16)
    into = jnp.concatenate([one_hot_rows(row, total) for row in ends2[1]], 1)
    coarse_sum_ref[...] = dot(into, message2_ref[...]).astype(BF16)
    grad_dst2 = dot(into, slope2_ref[...]) * grad_agg2
    back = jnp.concatenate([one_hot_rows(row, total) for row in ends2[0]], 1)
    grad_src2 = dot(back, edge2_ref[...])
    bias2_ref[...] = jnp.sum(grad_dst2, 0, keepdims=True)
    grad_src2_ref[...] = grad_src2.astype(BF16)
    grad_dst2_ref[...] = grad_dst2.astype(BF16)
    coarse_ref[...] = coarse
    parent_ref[...] = parent_all

    rows = pl.ds(pl.multiple_of(me * coarse_count, coarse_count), coarse_count)
    coarse_grad = (
        parent_ref[rows, :].astype(F32)
        + dot_nt(grad_src2_ref[rows, :], coarse_weights_ref[0])
        + dot_nt(grad_dst2_ref[rows, :], coarse_weights_ref[1])
    )
    share = share_ref[...]
    high, low = split(coarse_grad / member_count)
    grad_updated = cotangent_ref[...].astype(F32) + dot(share, high) + dot(share, low)
    grad_updated_ref[...] = grad_updated

    low, high = rims(near_ref[...], far_ref[...], odd)
    extended = jnp.concatenate([low, nodes, high], 0)
    rim = low.shape[0]
    slots = slopes_ref.shape[0]
    grad_updated_near = grad_updated.astype(BF16)
    grad_summed = dot_nt(grad_updated_near, weights_ref[2])
    grad_summed_near = grad_summed.astype(BF16)
    grad_dst = slopes_sum_ref[...] * grad_summed
    chunk = 2 * EDGE_BLOCK
    for start in range(0, slots, chunk):
        span = slice(start, start + chunk)
        slope = slopes_ref[span, :].astype(F32)
        edge_ref[span, :] = (dot(to_nodes_ref[span, :], grad_summed_near) * slope).astype(BF16)
    grad_src = dot(back_ref[...], edge_ref[...]).astype(BF16)
    bias1 = jnp.sum(grad_dst, 0, keepdims=True)
    grad_dst = grad_dst.astype(BF16)
    grad_src_ref[...] = grad_src
    grad_dst_ref[...] = grad_dst
    low = dot_nt(grad_src[:rim], weights_ref[0]).astype(BF16)
    high = dot_nt(grad_src[rim + node_count :], weights_ref[0]).astype(BF16)
    grads_ref[0:width, :] = dot_tn(extended, grad_src).astype(BF16)
    grads_ref[width : 2 * width, :] = dot_tn(nodes, grad_dst).astype(BF16)
    grads_ref[2 * width : 3 * width, :] = dot_tn(summed_ref[...], grad_updated_near).astype(BF16)
    if grads_ref.shape[0] > 3 * width:
        grads_ref[3 * width :, :] = jnp.zeros((grads_ref.shape[0] - 3 * width, width), BF16)
    half = grads_ref.shape[0] // 2
    keep_ref[:half, :] = grads_ref[pl.ds(pl.multiple_of(odd * half, ROW_TILE), half), :]
    send_ref[:half, :] = grads_ref[pl.ds(pl.multiple_of((1 - odd) * half, ROW_TILE), half), :]
    bias_rows = two_rows(bias1, ROW_TILE)
    keep_ref[half : half + ROW_TILE, :] = bias_rows
    send_ref[half : half + ROW_TILE, :] = bias_rows
    send_ref[half + ROW_TILE :, :] = jnp.where(odd == 1, low, high)
    far_grad_ref[...] = jnp.where(odd == 1, high, low)


def two_rows(value, count):
    high = value.astype(BF16).astype(F32)
    row = lax.broadcasted_iota(jnp.int32, (count, value.shape[1]), 0)
    return jnp.where(row == 0, high, jnp.where(row == 1, value - high, 0.0)).astype(BF16)


def pair_kernel(keep_ref, came_ref, blocks_ref):
    half = keep_ref.shape[0] - ROW_TILE
    chips, depth, _ = blocks_ref.shape
    rows = half // chips
    bias = keep_ref[half:, :].astype(F32) + came_ref[half : half + ROW_TILE, :].astype(F32)
    bias = two_rows(jnp.sum(bias, 0, keepdims=True), depth - rows)
    for chip in range(chips):
        span = slice(chip * rows, (chip + 1) * rows)
        blocks_ref[chip, :rows, :] = (
            keep_ref[span, :].astype(F32) + came_ref[span, :].astype(F32)
        ).astype(BF16)
        blocks_ref[chip, rows:, :] = bias


def coarse_kernel(
    coarse_weights_ref,
    weights_ref,
    coarse_ref,
    parent_ref,
    coarse_sum_ref,
    grad_src2_ref,
    grad_dst2_ref,
    updated_ref,
    family_ref,
    grad_updated_ref,
    grad_src_ref,
    grad_dst_ref,
    lists_ref,
    came_ref,
    moved_ref,
    coarse_grads_ref,
    node_part_ref,
):
    me, odd, _ = place()
    node_count = updated_ref.shape[0]
    coarse_count = family_ref.shape[0]
    rim = lists_ref.shape[1]
    rows = pl.ds(pl.multiple_of(me * coarse_count, coarse_count), coarse_count)
    coarse_new = coarse_ref[rows, :].astype(F32) + dot(
        coarse_sum_ref[rows, :], coarse_weights_ref[2]
    )
    family = family_ref[...]
    high, low = split(coarse_new)
    moved_ref[...] = updated_ref[...] + dot_tn(family, high) + dot_tn(family, low)
    coarse = coarse_ref[...]
    coarse_grads_ref[0] = dot_tn(coarse, grad_src2_ref[...])
    coarse_grads_ref[1] = dot_tn(coarse, grad_dst2_ref[...])
    coarse_grads_ref[2] = dot_tn(coarse_sum_ref[...], parent_ref[...])
    lists = lists_ref[...]
    near_list = jnp.where(odd == 1, lists[0:1], lists[1:2])
    near = came_ref[came_ref.shape[0] - rim :, :]
    both = jnp.concatenate([grad_src_ref[rim : rim + node_count, :], grad_dst_ref[...]], 1)
    node_part_ref[...] = grad_updated_ref[...] + dot_nt(
        both, jnp.concatenate([weights_ref[0], weights_ref[1]], 1)
    )
    node_part_ref[...] += dot(one_hot_rows(near_list, node_count), near)


def sum_kernel(blocks_ref, node_part_ref, far_grad_ref, part_ref, bias1_ref):
    chips, rows, _ = part_ref.shape
    total = blocks_ref[0].astype(F32)
    for other in range(1, chips):
        total = total + blocks_ref[other].astype(F32)
    part = total[:rows].astype(BF16)
    for other in range(chips):
        part_ref[other] = part
    bias1_ref[...] = jnp.sum(total[rows:], 0, keepdims=True)


def finish_kernel(
    node_part_ref, far_grad_ref, lists_ref, bias1_ref, bias2_ref, node_grads_ref, bias_ref
):
    _, odd, _ = place()
    lists = lists_ref[...]
    far_list = jnp.where(odd == 1, lists[1:2], lists[0:1])
    node_count = node_part_ref.shape[0]
    node_grads_ref[...] = node_part_ref[...] + dot(
        one_hot_rows(far_list, node_count), far_grad_ref[...]
    )
    bias_ref[0:1, :] = bias1_ref[...]
    bias_ref[1:2, :] = bias2_ref[...]


def join_kernel(mine_ref, theirs_ref, out_ref):
    _, odd, _ = place()
    chips, rows, _ = mine_ref.shape
    limit = out_ref.shape[0]
    for side in range(2):
        for chip in range(chips):
            start = (side * chips + chip) * rows
            count = min(rows, limit - start)
            if count <= 0:
                continue
            mine = mine_ref[chip, :count, :]
            theirs = theirs_ref[chip, :count, :]
            out_ref[start : start + count, :] = jnp.where(odd == side, mine, theirs).astype(F32)


def call(kernel, outs, args, room, scratch=(), scalars=(), outside=(), copies=0, flops=0):
    vmem = pl.BlockSpec(memory_space=pltpu.VMEM)
    scalar = pl.BlockSpec(memory_space=pltpu.SMEM)
    hbm = pl.BlockSpec(memory_space=pltpu.HBM)
    specs = [
        scalar if spot in scalars else hbm if spot in outside else vmem for spot in range(len(args))
    ]
    args = [
        pltpu.with_memory_space_constraint(value, pltpu.HBM) if spot in outside else value
        for spot, value in enumerate(args)
    ]
    moved = sum(value.size * value.dtype.itemsize for value in args)
    moved += sum(math.prod(shape) * jnp.dtype(kind).itemsize for shape, kind in outs)
    scratch = [pltpu.VMEM(shape, kind) for shape, kind in scratch]
    if copies:
        scratch.append(pltpu.SemaphoreType.DMA((copies,)))
    return pl.pallas_call(
        kernel,
        out_shape=[jax.ShapeDtypeStruct(shape, kind) for shape, kind in outs],
        in_specs=specs,
        out_specs=[vmem] * len(outs),
        scratch_shapes=scratch,
        compiler_params=pltpu.CompilerParams(vmem_limit_bytes=room * MIB),
        cost_estimate=pl.CostEstimate(flops=flops, bytes_accessed=moved, transcendentals=0),
    )(*args)


def round_up(value, unit):
    return -(-value // unit) * unit


def shards(
    nodes,
    cotangent,
    fine_weights,
    coarse_weights,
    biases,
    send_lists,
    edge_ends,
    live_blocks,
    pool_members,
    parents,
    coarse_ends,
):
    ndom = lax.axis_size("dom")
    chips = ndom // 2
    node_count, width = nodes.shape
    rim = send_lists.shape[1]
    member_count, coarse_count = pool_members.shape
    slots = edge_ends.shape[1]
    edge_count2 = coarse_ends.shape[1] * ndom
    total = coarse_count * ndom
    parents = parents.reshape(1, node_count)
    pairs = [(i, i ^ 1) for i in range(ndom)]
    across = [(i, i + 1) for i in range(1, ndom - 1, 2)]
    across = across + [(target, source) for source, target in across]
    same_core = [[2 * chip + core for chip in range(chips)] for core in range(2)]

    def swap(value):
        return lax.ppermute(value, "dom", pairs)

    def exchange(value):
        return lax.all_to_all(value, "dom", 0, 0, axis_index_groups=same_core)

    rim_rows = ((rim, width), BF16)
    square = ((width, width), BF16)
    near, far, nodes, lists = call(
        pick_kernel,
        [rim_rows, rim_rows, (nodes.shape, BF16), (send_lists.shape, jnp.int32)],
        (nodes, send_lists),
        2,
        outside=(0, 1),
        copies=2,
    )
    far = lax.ppermute(far, "dom", across)
    near = swap(near)

    pieces = -(-edge_count2 // width)
    link_rows = round_up(4 * pieces, ROW_TILE)
    side_rows = coarse_count + link_rows
    fine, ends, upstream, pre, rim_hot, to_nodes, into, share, family, side = call(
        functools.partial(prepare_kernel, ndom, rim),
        [
            (fine_weights.shape, BF16),
            (edge_ends.shape, jnp.int32),
            (cotangent.shape, BF16),
            ((slots, width), F32),
            ((slots, 2 * rim), BF16),
            ((slots, node_count), BF16),
            ((node_count, slots), BF16),
            ((node_count, coarse_count), BF16),
            ((coarse_count, node_count), BF16),
            ((side_rows, width), BF16),
        ],
        (
            nodes,
            fine_weights,
            biases,
            edge_ends,
            live_blocks,
            pool_members,
            parents,
            cotangent,
            coarse_ends,
        ),
        10,
        scratch=[
            (biases.shape, F32),
            (pool_members.shape, jnp.int32),
            (parents.shape, jnp.int32),
            (coarse_ends.shape, jnp.int32),
            ((link_rows, width), F32),
        ],
        scalars=(4,),
        outside=(1, 2, 3, 5, 6, 7, 8),
        copies=7,
        flops=2 * slots * width * (2 * node_count + 2 * rim),
    )
    updated, summed, slopes, packet = call(
        functools.partial(forward_kernel, member_count),
        [
            ((node_count, width), F32),
            ((node_count, width), BF16),
            ((slots, width), BF16),
            ((chips, coarse_count + side_rows, width), BF16),
        ],
        (nodes, near, far, fine, pre, rim_hot, into, share, side),
        10,
        scratch=[((slots, width), BF16)],
    )
    mine = exchange(packet)
    slopes_sum, back = call(
        between_kernel,
        [((node_count, width), F32), ((node_count + 2 * rim, slots), BF16)],
        (into, slopes, ends, live_blocks),
        8,
        scalars=(3,),
        flops=2 * slots * width * node_count,
    )
    theirs = swap(mine)

    rows = round_up(-(-3 * width // ndom), ROW_TILE)
    half = rows * chips
    edges2 = pieces * width
    coarse_whole = ((total, width), BF16)
    (
        send,
        keep,
        far_grad,
        coarse,
        parent_all,
        coarse_sum,
        grad_src2,
        grad_dst2,
        bias2,
        grad_updated,
        grad_src,
        grad_dst,
    ) = call(
        functools.partial(backward_kernel, ndom, edge_count2, member_count),
        [
            ((half + ROW_TILE + rim, width), BF16),
            ((half + ROW_TILE, width), BF16),
            rim_rows,
            coarse_whole,
            coarse_whole,
            coarse_whole,
            coarse_whole,
            coarse_whole,
            ((1, width), F32),
            ((node_count, width), F32),
            ((node_count + 2 * rim, width), BF16),
            ((node_count, width), BF16),
        ],
        (
            mine,
            theirs,
            coarse_weights,
            biases,
            nodes,
            near,
            far,
            fine,
            share,
            upstream,
            summed,
            slopes_sum,
            slopes,
            to_nodes,
            back,
        ),
        20 if total <= 256 else 48,
        scratch=[
            ((link_rows, width), F32),
            ((edges2, width), BF16),
            ((edges2, width), BF16),
            ((edges2, width), BF16),
            ((2 * half, width), BF16),
            ((slots, width), BF16),
        ],
    )
    came = swap(send)
    (blocks,) = call(pair_kernel, [((chips, rows + 8, width), BF16)], (keep, came), 4)
    blocks = exchange(blocks)
    far_grad = lax.ppermute(far_grad, "dom", across)
    moved, coarse_grads, node_part = call(
        coarse_kernel,
        [
            ((node_count, width), F32),
            ((3, width, width), F32),
            ((node_count, width), F32),
        ],
        (
            coarse_weights,
            fine,
            coarse,
            parent_all,
            coarse_sum,
            grad_src2,
            grad_dst2,
            updated,
            family,
            grad_updated,
            grad_src,
            grad_dst,
            lists,
            came,
        ),
        8,
        flops=6 * total * width * width,
    )
    part, bias1 = call(
        sum_kernel,
        [((chips, rows, width), BF16), ((1, width), F32)],
        (blocks, node_part, far_grad),
        4,
    )
    mine = exchange(part)
    node_grads, bias_grads = call(
        finish_kernel,
        [((node_count, width), F32), ((2, width), F32)],
        (node_part, far_grad, lists, bias1, bias2),
        4,
    )
    theirs = swap(mine)
    (fine_grads,) = call(join_kernel, [((3 * width, width), F32)], (mine, theirs), 4)
    return moved, node_grads, fine_grads.reshape(3, width, width), coarse_grads, bias_grads


def solution(mesh):
    return jax.shard_map(
        shards,
        mesh=mesh,
        in_specs=(
            P(("groups", "dom"), None),
            P(("groups", "dom"), None),
            P(),
            P(),
            P(),
            P("groups", "dom"),
            P("groups", "dom"),
            P(("groups", "dom")),
            P("groups", "dom"),
            P(("groups", "dom")),
            P("groups", "dom"),
        ),
        out_specs=(
            P(("groups", "dom"), None),
            P(("groups", "dom"), None),
            P("groups", None, None),
            P("groups", None, None),
            P("groups", None),
        ),
        check_vma=False,
    )
```

time: 63.3 us -> 57.1 us (0.902)
  blocking collectives: 43.1 us -> 27.8 us
  waiting for transfers between devices: 4.22 us -> 9.94 us
  local copies, waits for them, and re-layouts: 5.39 us -> 0.01 us
  Pallas kernels: 7.3 us -> 12.1 us
  starting transfers between devices: 1.43 us -> 5.45 us
    all_to_all x3 -> x2, blocking collectives: 43.1 us -> 27.8 us  [exchange(): return lax.all_to_all(value, 'dom', 0, 0, axis_index_groups=same_core)]
    all_to_all x0 -> x1, waiting for transfers between devices: none -> 6.98 us  [exchange(): return lax.all_to_all(value, 'dom', 0, 0, axis_index_groups=same_core)]
    unnamed x30 -> x4, local copies, waits for them, and re-layouts: 5.39 us -> 0.01 us
    pallas_call x6 -> x10, Pallas kernels: 7.3 us -> 12.1 us  [call(): pl.pallas_call(kernel, out_shape=[jax.ShapeDtypeStruct(shape, kind) for s...]
    all_to_all x0 -> x1, starting transfers between devices: none -> 3.4 us  [exchange(): return lax.all_to_all(value, 'dom', 0, 0, axis_index_groups=same_core)]
    ppermute x4, waiting for transfers between devices: 4.22 us -> 2.96 us  [swap(): return lax.ppermute(value, 'dom', pairs)]
    ppermute x0 -> x1, starting transfers between devices: none -> 0.66 us  [shards(): far_grad = lax.ppermute(far_grad, 'dom', across)]
  transfers between devices with their start and end apart: 5 -> 7, of which waited for: 3 -> 4; matrix products, arithmetic and copies ran while one was open for 0% -> 0% of each run, Pallas kernels for 0% -> 9%
where the time goes in v3:
time: 57.1 us; the launch traced here: 56.7 us
  blocking collectives  27.8 us (49%)
  Pallas kernels  12.1 us (21%)
  waiting for transfers between devices  9.94 us (17%)
  starting transfers between devices  5.45 us (10%)
  between operations  1.37 us (2%)
    all_to_all x2, blocking collectives, exchange(): return lax.all_to_all(value, 'dom', 0, 0, axis_index_groups=same_core)  27.8 us
    pallas_call x10, Pallas kernels, call(): pl.pallas_call(kernel, out_shape=[jax.ShapeDtypeStruct(shape, kind) for s...  12.1 us
    all_to_all x1, waiting for transfers between devices, exchange(): return lax.all_to_all(value, 'dom', 0, 0, axis_index_groups=same_core)  6.98 us
    all_to_all x1, starting transfers between devices, exchange(): return lax.all_to_all(value, 'dom', 0, 0, axis_index_groups=same_core)  3.4 us
    ppermute x4, waiting for transfers between devices, swap(): return lax.ppermute(value, 'dom', pairs)  2.96 us
  transfers between devices with their start and end apart: 7, of which 4 were waited for; matrix products, arithmetic and copies ran while one was open for 0% of the time, Pallas kernels for 9%

profile of v3, /device:TPU:0, one launch (start us, length us, event | category | flops | bytes accessed | tf_op | source)
XLA Modules:
  0.0 56.7 jit_solution(11091260303603264286)
XLA Ops:
  0.6 1.0 %shard_map.146 = (bf16[16,256]{1,0:T(8,128)(2,1)S(1)}, bf16[16,256]{1,0:T(8,128)(2,1)S(1)}, bf16[128,256]{1,0:T(8,128)(2,1)S(1)}, s32[2,16]{1,0:T(2,128)S(1)}) custom-call(bf16[128,256]{1,0:T(8,128)(2,1)} %nodes_ref.1, s32[2,16]{1,0:T(2,128)} %lists_ref.1), custom_call_target="tpu_custom_call" | custom-call | bytes 147712 | tf_op jit(solution)/shard_map/pallas_call | solution.py:507
  1.7 0.5 collective-permute-start
  2.2 0.6 %collective-permute-start.1 = (bf16[16,256]{1,0:T(8,128)(2,1)S(1)}, bf16[16,256]{1,0:T(8,128)(2,1)S(1)}, u32[]{:S(2)}, u32[]{:S(2)}) collective-permute-start(bf16[16,256]{1,0:T(8,128)(2,1)S(1)} %get-tuple-element.47), channel_id=1, source_target_pairs={{1,2},{3,4},{5,6},{7,8},{9,10},{11,12},{13,14},{2,1},{4,3},{6,5},{... | collective-permute-start | bytes 24584 | tf_op jit(solution)/shard_map/ppermute | solution.py:565
  3.5 2.6 %shard_map.147 = (bf16[3,256,256]{2,1,0:T(8,128)(2,1)S(1)}, s32[2,1536]{1,0:T(2,128)S(1)}, bf16[128,256]{1,0:T(8,128)(2,1)S(1)}, f32[1536,256]{1,0:T(8,128)S(1)}...) custom-call(bf16[128,256]{1,0:T(8,128)(2,1)S(1)} %get-tuple-element., ...), custom_call_target="tpu_custom_call" | custom-call | flops 226492416 | bytes 3493252 | tf_op jit(solution)/shard_map/pallas_call | solution.py:507
  6.2 0.0 collective-permute-done.near_ref
  6.2 0.0 collective-permute-done.1.far_ref
  6.2 0.0 copy-start
  6.2 0.0 copy-start.1
  6.2 1.2 %shard_map.148 = (f32[128,256]{1,0:T(8,128)S(1)}, bf16[128,256]{1,0:T(8,128)(2,1)S(1)}, bf16[1536,256]{1,0:T(8,128)(2,1)S(1)}, bf16[8,48,256]{2,1,0:T(8,128)(2,1)S(1)}) custom-call(bf16[128,256]{1,0:T(8,128)(2,1)S(1)} %get-tuple-element.44.nodes_ref, bf16[16,256]{1,0:T(8,128)(2,1)S(1)} %collective-permute-done.near_ref, ...), custom_call_target="tpu_custom_call" | custom-call | bytes 3739648 | tf_op jit(solution)/shard_map/pallas_call | solution.py:507
  7.4 16.7 %all_to_all.15.mine_ref = bf16[8,48,256]{2,1,0:T(8,128)(2,1)S(1)} all-to-all(bf16[8,48,256]{2,1,0:T(8,128)(2,1)S(1)} %get-tuple-element.53), channel_id=1, replica_groups={{0,2,4,6,8,10,12,14},{1,3,5,7,9,11,13,15},{16,18,20,22,24,26,28,30},{17..., dimensions={0} | all-to-all | bytes 393216 | tf_op jit(solution)/shard_map/all_to_all | solution.py:553
  24.1 0.0 collective-permute-start.2
  24.1 0.4 shard_map.149
  24.6 1.0 %collective-permute-done.2.theirs_ref = bf16[8,48,256]{2,1,0:T(8,128)(2,1)S(1)} collective-permute-done((bf16[8,48,256]{2,1,0:T(8,128)(2,1)S(1)}, bf16[8,48,256]{2,1,0:T(8,128)(2,1)S(1)}, u32[]{:S(2)}, u32[]{:S(2)}) %collective-permute-start.2) | collective-permute-done | bytes 196640 | tf_op jit(solution)/shard_map/ppermute | solution.py:550
  25.6 0.0 copy-done
  25.6 0.0 copy-done.1
  25.6 2.9 %shard_map.150 = (bf16[416,256]{1,0:T(8,128)(2,1)S(1)}, bf16[400,256]{1,0:T(8,128)(2,1)S(1)}, bf16[16,256]{1,0:T(8,128)(2,1)S(1)}, bf16[256,256]{1,0:T(8,128)(2,...) custom-call(bf16[8,48,256]{2,1,0:T(8,128)(2,1)S(1)} %all_to_all.15.m, ...), custom_call_target="tpu_custom_call" | custom-call | bytes 4561920 | tf_op jit(solution)/shard_map/pallas_call | solution.py:507
  28.5 0.2 collective-permute-start.3
  28.7 1.3 %collective-permute-done.3.came_ref = bf16[416,256]{1,0:T(8,128)(2,1)S(1)} collective-permute-done((bf16[416,256]{1,0:T(8,128)(2,1)S(1)}, bf16[416,256]{1,0:T(8,128)(2,1)S(1)}, u32[]{:S(2)}, u32[]{:S(2)}) %collective-permute-start.3) | collective-permute-done | bytes 213024 | tf_op jit(solution)/shard_map/ppermute | solution.py:550
  30.0 0.7 %shard_map.152 = bf16[8,56,256]{2,1,0:T(8,128)(2,1)} custom-call(bf16[400,256]{1,0:T(8,128)(2,1)S(1)} %get-tuple-element.76.keep_ref, bf16[416,256]{1,0:T(8,128)(2,1)S(1)} %collective-permute-done.3.came_ref), custom_call_target="tpu_custom_call" | custom-call | bytes 647168 | tf_op jit(solution)/shard_map/pallas_call | solution.py:507
  30.8 3.4 %all-to-all-start.1 = ((bf16[8,56,256]{2,1,0:T(8,128)(2,1)}), bf16[8,56,256]{2,1,0:T(8,128)(2,1)S(1)}, u32[]{:S(2)}, u32[]{:S(2)}) async-start(bf16[8,56,256]{2,1,0:T(8,128)(2,1)} %shard_map.152), calls=%async_computation.1 | async-start | bytes 458752 | tf_op jit(solution)/shard_map/all_to_all | solution.py:553
  34.2 0.7 %collective-permute-start.4 = (bf16[16,256]{1,0:T(8,128)(2,1)S(1)}, bf16[16,256]{1,0:T(8,128)(2,1)S(1)}, u32[]{:S(2)}, u32[]{:S(2)}) collective-permute-start(bf16[16,256]{1,0:T(8,128)(2,1)S(1)} %get-tuple-element.75), channel_id=1, source_target_pairs={{1,2},{3,4},{5,6},{7,8},{9,10},{11,12},{13,14},{2,1},{4,3},{6,5},{... | collective-permute-start | bytes 24584 | tf_op jit(solution)/shard_map/ppermute | solution.py:695
  34.9 1.3 %shard_map.151 = (f32[128,256]{1,0:T(8,128)}, f32[3,256,256]{2,1,0:T(8,128)}, f32[128,256]{1,0:T(8,128)S(1)}) custom-call(bf16[3,256,256]{2,1,0:T(8,128)(2,1)S(1)} %copy-done, bf16[3,256,256]{2,1,0:T(8,128)(2,1)S(1)} %get-tuple-element.45.weights_ref, bf16[256,256]{1,0:T(8,128)(2,1)S(1)} %get-tuple-element.61.coarse_ref, ...), custom_call_target="tpu_custom_call" | custom-call | flops 100663296 | bytes 3117184 | tf_op jit(solution)/shard_map/pallas_call | solution.py:507
  36.2 0.0 collective-permute-done.4.far_grad_ref
  36.2 7.0 %all-to-all-done.1.blocks_ref = bf16[8,56,256]{2,1,0:T(8,128)(2,1)S(1)} async-done(((bf16[8,56,256]{2,1,0:T(8,128)(2,1)}), bf16[8,56,256]{2,1,0:T(8,128)(2,1)S(1)}, u32[]{:S(2)}, u32[]{:S(2)}) %all-to-all-start.1) | async-done | bytes 229408 | tf_op jit(solution)/shard_map/all_to_all | solution.py:553
  43.2 11.1 %all_to_all.16.mine_ref = bf16[8,48,256]{2,1,0:T(8,128)(2,1)S(1)} all-to-all(bf16[8,48,256]{2,1,0:T(8,128)(2,1)S(1)} %get-tuple-element.80), channel_id=1, replica_groups={{0,2,4,6,8,10,12,14},{1,3,5,7,9,11,13,15},{16,18,20,22,24,26,28,30},{17..., dimensions={0} | all-to-all | bytes 393216 | tf_op jit(solution)/shard_map/all_to_all | solution.py:553
  54.3 0.0 collective-permute-start.5
  54.3 0.8 %shard_map.154 = (f32[128,256]{1,0:T(8,128)}, f32[2,256]{1,0:T(2,128)}) custom-call(f32[128,256]{1,0:T(8,128)S(1)} %get-tuple-element.74.node_part_ref, bf16[16,256]{1,0:T(8,128)(2,1)S(1)} %collective-permute-done.4.far_grad_ref, s32[2,16]{1,0:T(2,128)S(1)} %get-tuple-element.71.lists_ref, f32[1,256]{1,0:T(1,128)S(1)} %get-tuple-element.77.bias1_ref, ...), custom_call_target="tpu_custom_call" | custom-call | bytes 274560 | tf_op jit(solution)/shard_map/pallas_call | solution.py:507
  55.1 0.6 %collective-permute-done.5.theirs_ref = bf16[8,48,256]{2,1,0:T(8,128)(2,1)S(1)} collective-permute-done((bf16[8,48,256]{2,1,0:T(8,128)(2,1)S(1)}, bf16[8,48,256]{2,1,0:T(8,128)(2,1)S(1)}, u32[]{:S(2)}, u32[]{:S(2)}) %collective-permute-start.5) | collective-permute-done | bytes 196640 | tf_op jit(solution)/shard_map/ppermute | solution.py:550
  55.8 1.0 %shard_map.155 = f32[768,256]{1,0:T(8,128)} custom-call(bf16[8,48,256]{2,1,0:T(8,128)(2,1)S(1)} %all_to_all.16.mine_ref, bf16[8,48,256]{2,1,0:T(8,128)(2,1)S(1)} %collective-permute-done.5.theirs_ref), custom_call_target="tpu_custom_call" | custom-call | bytes 1179648 | tf_op jit(solution)/shard_map/pallas_call | solution.py:507
  (1 shorter events, 0.0 us)
Async XLA Ops:
  1.7 4.5 %collective-permute-start = (bf16[16,256]{1,0:T(8,128)(2,1)S(1)}, bf16[16,256]{1,0:T(8,128)(2,1)S(1)}, u32[]{:S(2)}, u32[]{:S(2)}) collective-permute-start(bf16[16,256]{1,0:T(8,128)(2,1)S(1)} %get-tuple-element.46), channel_id=1, source_target_pairs={{0,1},{1,0},{2,3},{3,2},{4,5},{5,4},{6,7},{7,6},{8,9},{9,8},{10,11... | collective-permute-start | bytes 24584 | tf_op jit(solution)/shard_map/ppermute | solution.py:550
  2.2 4.0 %collective-permute-start.1 = (bf16[16,256]{1,0:T(8,128)(2,1)S(1)}, bf16[16,256]{1,0:T(8,128)(2,1)S(1)}, u32[]{:S(2)}, u32[]{:S(2)}) collective-permute-start(bf16[16,256]{1,0:T(8,128)(2,1)S(1)} %get-tuple-element.47), channel_id=1, source_target_pairs={{1,2},{3,4},{5,6},{7,8},{9,10},{11,12},{13,14},{2,1},{4,3},{6,5},{... | collective-permute-start | bytes 24584 | tf_op jit(solution)/shard_map/ppermute | solution.py:565
  6.2 19.4 %copy-start = (bf16[3,256,256]{2,1,0:T(8,128)(2,1)S(1)}, bf16[3,256,256]{2,1,0:T(8,128)(2,1)}, u32[]{:S(2)}) copy-start(bf16[3,256,256]{2,1,0:T(8,128)(2,1)} %coarse_weights_ref.3) | copy-start | bytes 1179652
  6.2 19.4 %copy-start.1 = (f32[2,256]{1,0:T(2,128)S(1)}, f32[2,256]{1,0:T(2,128)}, u32[]{:S(2)}) copy-start(f32[2,256]{1,0:T(2,128)} %biases_ref.1) | copy-start | bytes 6148
  24.1 1.4 %collective-permute-start.2 = (bf16[8,48,256]{2,1,0:T(8,128)(2,1)S(1)}, bf16[8,48,256]{2,1,0:T(8,128)(2,1)S(1)}, u32[]{:S(2)}, u32[]{:S(2)}) collective-permute-start(bf16[8,48,256]{2,1,0:T(8,128)(2,1)S(1)} %all_to_all.15.mine_ref), channel_id=1, source_target_pairs={{0,1},{1,0},{2,3},{3,2},{4,5},{5,4},{6,7},{7,6},{8,9},{9,8},{10,11... | collective-permute-start | bytes 589832 | tf_op jit(solution)/shard_map/ppermute | solution.py:550
  28.5 1.5 %collective-permute-start.3 = (bf16[416,256]{1,0:T(8,128)(2,1)S(1)}, bf16[416,256]{1,0:T(8,128)(2,1)S(1)}, u32[]{:S(2)}, u32[]{:S(2)}) collective-permute-start(bf16[416,256]{1,0:T(8,128)(2,1)S(1)} %get-tuple-element.72), channel_id=1, source_target_pairs={{0,1},{1,0},{2,3},{3,2},{4,5},{5,4},{6,7},{7,6},{8,9},{9,8},{10,11... | collective-permute-start | bytes 638984 | tf_op jit(solution)/shard_map/ppermute | solution.py:550
  30.8 12.4 %all-to-all-start.1 = ((bf16[8,56,256]{2,1,0:T(8,128)(2,1)}), bf16[8,56,256]{2,1,0:T(8,128)(2,1)S(1)}, u32[]{:S(2)}, u32[]{:S(2)}) async-start(bf16[8,56,256]{2,1,0:T(8,128)(2,1)} %shard_map.152), calls=%async_computation.1 | async-start | bytes 458752 | tf_op jit(solution)/shard_map/all_to_all | solution.py:553
  34.2 2.0 %collective-permute-start.4 = (bf16[16,256]{1,0:T(8,128)(2,1)S(1)}, bf16[16,256]{1,0:T(8,128)(2,1)S(1)}, u32[]{:S(2)}, u32[]{:S(2)}) collective-permute-start(bf16[16,256]{1,0:T(8,128)(2,1)S(1)} %get-tuple-element.75), channel_id=1, source_target_pairs={{1,2},{3,4},{5,6},{7,8},{9,10},{11,12},{13,14},{2,1},{4,3},{6,5},{... | collective-permute-start | bytes 24584 | tf_op jit(solution)/shard_map/ppermute | solution.py:695
  54.3 1.4 %collective-permute-start.5 = (bf16[8,48,256]{2,1,0:T(8,128)(2,1)S(1)}, bf16[8,48,256]{2,1,0:T(8,128)(2,1)S(1)}, u32[]{:S(2)}, u32[]{:S(2)}) collective-permute-start(bf16[8,48,256]{2,1,0:T(8,128)(2,1)S(1)} %all_to_all.16.mine_ref), channel_id=1, source_target_pairs={{0,1},{1,0},{2,3},{3,2},{4,5},{5,4},{6,7},{7,6},{8,9},{9,8},{10,11... | collective-permute-start | bytes 589832 | tf_op jit(solution)/shard_map/ppermute | solution.py:550

commit v4 on v3

--- a/solution.py
+++ b/solution.py
@@ -37,13 +37,9 @@
     return jnp.where(spots == index_row, 1.0, 0.0).astype(BF16)
 
 
-def one_hot_cols(index_col, count):
-    spots = lax.broadcasted_iota(jnp.int32, (index_col.shape[0], count), 1)
-    return jnp.where(spots == index_col, 1.0, 0.0).astype(BF16)
-
-
-def to_column(index_row):
-    return jnp.transpose(jnp.broadcast_to(index_row, (8, index_row.shape[1])))[:, :1]
+def column(row, lanes):
+    upright = jnp.transpose(jnp.broadcast_to(row, (8, row.shape[1])))[:, :1]
+    return jnp.broadcast_to(upright, (row.shape[1], lanes))
 
 
 def silu_and_slope(value):
@@ -71,25 +67,35 @@
     return jnp.where(slot < live_ref[0] * EDGE_BLOCK, index, -1)
 
 
-def pick_kernel(nodes_ref, lists_ref, near_ref, far_ref, nodes_out, lists_out, sems):
-    copies = (
-        pltpu.make_async_copy(nodes_ref, nodes_out, sems.at[0]),
-        pltpu.make_async_copy(lists_ref, lists_out, sems.at[1]),
-    )
+def pick_kernel(*refs):
+    count = (len(refs) - 3) // 2
+    inputs, (near_ref, far_ref), outputs = refs[:count], refs[count : count + 2], refs[count + 2 : -1]
+    copies = [
+        pltpu.make_async_copy(source, target, refs[-1].at[spot])
+        for spot, (source, target) in enumerate(zip(inputs, outputs, strict=True))
+    ]
     for copy in copies:
         copy.start()
-    for copy in copies:
+    for copy in copies[:2]:
         copy.wait()
     _, odd, _ = place()
-    lists = lists_out[...]
+    lists = outputs[1][...]
     near = jnp.where(odd == 1, lists[0:1], lists[1:2])
     far = jnp.where(odd == 1, lists[1:2], lists[0:1])
-    nodes = nodes_out[...]
-    near_ref[...] = dot_tn(one_hot_rows(near, nodes.shape[0]), nodes).astype(BF16)
-    far_ref[...] = dot_tn(one_hot_rows(far, nodes.shape[0]), nodes).astype(BF16)
-
-
-def rims(near, far, odd):
+    nodes = outputs[0][...]
+    rim = near_ref.shape[0]
+    near = dot_tn(one_hot_rows(near, nodes.shape[0]), nodes).astype(BF16)
+    near_ref[...] = near
+    far = dot_tn(one_hot_rows(far, nodes.shape[0]), nodes).astype(BF16)
+    for start in range(0, far_ref.shape[0], rim):
+        far_ref[start : start + rim, :] = far
+    for copy in copies[2:]:
+        copy.wait()
+
+
+def rims(near_ref, far_ref, odd):
+    near = near_ref[...]
+    far = far_ref[: near.shape[0], :]
     return jnp.where(odd == 1, near, far), jnp.where(odd == 1, far, near)
 
 
@@ -97,80 +103,58 @@
     ndom,
     rim,
     nodes_ref,
-    weights_hbm,
-    biases_hbm,
-    ends_hbm,
+    weights_ref,
+    biases_ref,
+    ends_ref,
     live_ref,
-    members_hbm,
-    parents_hbm,
-    cotangent_hbm,
-    links_hbm,
-    weights_ref,
-    ends_ref,
+    members_ref,
+    parents_ref,
     cotangent_ref,
+    links_ref,
     pre_ref,
-    rim_hot_ref,
-    to_nodes_ref,
+    outof_ref,
     into_ref,
     share_ref,
     family_ref,
     side_ref,
-    biases_ref,
-    members_ref,
-    parents_ref,
-    links_ref,
+    upright_ref,
+    pooled_ref,
     link_ref,
-    sems,
 ):
-    pairs = (
-        (ends_hbm, ends_ref),
-        (weights_hbm, weights_ref),
-        (biases_hbm, biases_ref),
-        (members_hbm, members_ref),
-        (parents_hbm, parents_ref),
-        (cotangent_hbm, cotangent_ref),
-        (links_hbm, links_ref),
-    )
-    copies = [
-        pltpu.make_async_copy(source, target, sems.at[spot])
-        for spot, (source, target) in enumerate(pairs)
-    ]
-    for copy in copies:
-        copy.start()
-    for copy in copies:
-        copy.wait()
     me, _, _ = place()
-    nodes = nodes_ref[...]
-    node_count, width = nodes.shape
+    node_count, width = nodes_ref.shape
     coarse_count = family_ref.shape[0]
     slots = ends_ref.shape[1]
-    src_proj = dot(nodes, weights_ref[0]).astype(BF16)
-    dst_proj = dot(nodes, weights_ref[1]).astype(BF16)
-    bias = biases_ref[0:1, :]
+    lanes = link_ref.shape[1]
+    outof_ref[...] = one_hot_rows(live_rows(ends_ref, live_ref, 0), node_count + 2 * rim)
+    into_ref[...] = one_hot_rows(live_rows(ends_ref, live_ref, 1), node_count)
+    nodes = nodes_ref[...]
+    src_proj = jnp.transpose(dot(nodes, weights_ref[0])).astype(BF16)
+    dst_proj = jnp.transpose(dot(nodes, weights_ref[1])).astype(BF16)
     chunk = 2 * EDGE_BLOCK
+    bias = column(biases_ref[0:1, :], chunk)
     for start in range(0, slots, chunk):
         span = slice(start, start + chunk)
-        senders = to_column(ends_ref[0:1, span])
-        receivers = to_column(ends_ref[1:2, span])
-        to_nodes = one_hot_cols(receivers, node_count)
-        to_nodes_ref[span, :] = to_nodes
-        inner = one_hot_cols(senders - rim, node_count)
-        spot = jnp.where(
-            senders < rim, senders, jnp.where(senders < rim + node_count, -1, senders - node_count)
+        pre_ref[:, span] = (
+            dot(src_proj, outof_ref[rim : rim + node_count, span])
+            + dot(dst_proj, into_ref[:, span])
+            + bias
         )
-        rim_hot_ref[span, :] = one_hot_cols(spot, 2 * rim)
-        pre_ref[span, :] = dot(inner, src_proj) + dot(to_nodes, dst_proj) + bias
-    into_ref[...] = one_hot_rows(live_rows(ends_ref, live_ref, 1), node_count)
-    share_ref[...] = membership(members_ref[...], node_count)
+    upright_ref[...] = jnp.transpose(weights_ref[0].astype(F32)).astype(BF16)
+    share = membership(members_ref[...], node_count)
+    share_ref[...] = share
+    pooled_ref[...] = dot_tn(share, nodes)
     family = one_hot_rows(parents_ref[...], coarse_count)
     family_ref[...] = family
-    side_ref[:coarse_count, :] = dot(family, cotangent_ref[...]).astype(BF16)
+    parent_grad = dot(family, cotangent_ref[...]).astype(BF16)
+    side_ref[:coarse_count, :] = parent_grad[:, :lanes]
+    side_ref[coarse_count : 2 * coarse_count, :] = parent_grad[:, lanes:]
 
     links = links_ref[...]
     own = links.shape[1]
-    pieces = -(-own * ndom // width)
-    spot = lax.broadcasted_iota(jnp.int32, (own, pieces * width), 1)
-    source = lax.broadcasted_iota(jnp.int32, (own, pieces * width), 0)
+    pieces = -(-own * ndom // lanes)
+    spot = lax.broadcasted_iota(jnp.int32, (own, pieces * lanes), 1)
+    source = lax.broadcasted_iota(jnp.int32, (own, pieces * lanes), 0)
     spread = jnp.where(spot == source + me * own, 1.0, 0.0).astype(BF16)
     coded = (
         dot((links >> 8).astype(F32).astype(BF16), spread),
@@ -182,68 +166,84 @@
             for piece in range(pieces):
                 row = (part * 2 + end) * pieces + piece
                 link_ref[row : row + 1, :] = coded[part][
-                    end : end + 1, piece * width : (piece + 1) * width
+                    end : end + 1, piece * lanes : (piece + 1) * lanes
                 ]
-    side_ref[coarse_count:, :] = link_ref[...].astype(BF16)
+    side_ref[2 * coarse_count :, :] = link_ref[...].astype(BF16)
 
 
 def forward_kernel(
     member_count,
-    nodes_ref,
     near_ref,
     far_ref,
+    upright_ref,
     weights_ref,
     pre_ref,
-    rim_hot_ref,
+    outof_ref,
     into_ref,
     share_ref,
+    pooled_ref,
     side_ref,
-    updated_ref,
     summed_ref,
     slopes_ref,
     packet_ref,
     message_ref,
 ):
     _, odd, _ = place()
-    nodes = nodes_ref[...]
-    low, high = rims(near_ref[...], far_ref[...], odd)
-    rim_proj = dot(jnp.concatenate([low, high], 0), weights_ref[0]).astype(BF16)
-    slots = pre_ref.shape[0]
+    low, high = rims(near_ref, far_ref, odd)
+    rim = low.shape[0]
+    node_count = into_ref.shape[0]
+    rim_proj = dot_nt(upright_ref[...], jnp.concatenate([low, high], 0)).astype(BF16)
+    slots = pre_ref.shape[1]
     chunk = 2 * EDGE_BLOCK
     for start in range(0, slots, chunk):
         span = slice(start, start + chunk)
-        pre = pre_ref[span, :] + dot(rim_hot_ref[span, :], rim_proj)
-        message, slope = silu_and_slope(pre)
-        message_ref[span, :] = message.astype(BF16)
-        slopes_ref[span, :] = slope.astype(BF16)
-    summed = dot(into_ref[...], message_ref[...]).astype(BF16)
+        at_rim = jnp.concatenate([outof_ref[:rim, span], outof_ref[rim + node_count :, span]], 0)
+        message, slope = silu_and_slope(pre_ref[:, span] + dot(rim_proj, at_rim))
+        message_ref[:, span] = message.astype(BF16)
+        slopes_ref[:, span] = slope.astype(BF16)
+    summed = dot_nt(into_ref[...], message_ref[...]).astype(BF16)
     summed_ref[...] = summed
-    updated = nodes.astype(F32) + dot(summed, weights_ref[2])
-    updated_ref[...] = updated
-    share = share_ref[...]
-    high, low = split(updated)
-    pooled = dot_tn(share, high) + dot_tn(share, low)
+    high, low = split(dot_tn(share_ref[...], summed))
+    pooled = pooled_ref[...] + dot(high, weights_ref[2]) + dot(low, weights_ref[2])
     coarse = (pooled / member_count).astype(BF16)
-    coarse_count = coarse.shape[0]
+    count = coarse.shape[0]
+    lanes = packet_ref.shape[2]
     side = side_ref[...]
     for chip in range(packet_ref.shape[0]):
-        packet_ref[chip, :coarse_count, :] = coarse
-        packet_ref[chip, coarse_count:, :] = side
-
-
-def between_kernel(into_ref, slopes_ref, ends_ref, live_ref, slopes_sum_ref, back_ref):
-    slopes_sum_ref[...] = dot(into_ref[...], slopes_ref[...])
-    back_ref[...] = one_hot_rows(live_rows(ends_ref, live_ref, 0), back_ref.shape[0])
+        packet_ref[chip, :count, :] = coarse[:, :lanes]
+        packet_ref[chip, count : 2 * count, :] = coarse[:, lanes:]
+        packet_ref[chip, 2 * count :, :] = side
+
+
+def between_kernel(
+    into_ref,
+    slopes_ref,
+    nodes_ref,
+    summed_ref,
+    weights_ref,
+    coarse_weights_ref,
+    slopes_sum_ref,
+    updated_ref,
+    upright2_ref,
+):
+    for spot in range(2):
+        upright2_ref[spot] = jnp.transpose(coarse_weights_ref[spot].astype(F32)).astype(BF16)
+    slopes_sum_ref[...] = dot_nt(into_ref[...], slopes_ref[...])
+    updated_ref[...] = nodes_ref[...].astype(F32) + dot(summed_ref[...], weights_ref[2])
 
 
 def ordered(mine_ref, theirs_ref, odd, start, count):
     blocks = []
     for chip in range(mine_ref.shape[0]):
-        mine = mine_ref[chip, start : start + count, :]
-        theirs = theirs_ref[chip, start : start + count, :]
-        blocks.append(jnp.where(odd == 1, theirs, mine))
-        blocks.append(jnp.where(odd == 1, mine, theirs))
-    return blocks
+        halves = []
+        for half in range(2):
+            span = slice(start + half * count, start + (half + 1) * count)
+            mine = mine_ref[chip, span, :]
+            theirs = theirs_ref[chip, span, :]
+            halves.append((jnp.where(odd == 1, theirs, mine), jnp.where(odd == 1, mine, theirs)))
+        for core in range(2):
+            blocks.append(jnp.concatenate([halves[0][core], halves[1][core]], 1))
+    return jnp.concatenate(blocks, 0)
 
 
 def backward_kernel(
@@ -253,6 +253,7 @@
     mine_ref,
     theirs_ref,
     coarse_weights_ref,
+    upright2_ref,
     biases_ref,
     nodes_ref,
     near_ref,
@@ -263,14 +264,15 @@
     summed_ref,
     slopes_sum_ref,
     slopes_ref,
-    to_nodes_ref,
-    back_ref,
+    outof_ref,
+    into_ref,
     send_ref,
     keep_ref,
     far_grad_ref,
     coarse_ref,
     parent_ref,
-    coarse_sum_ref,
+    into2_ref,
+    message2_ref,
     grad_src2_ref,
     grad_dst2_ref,
     bias2_ref,
@@ -278,11 +280,10 @@
     grad_src_ref,
     grad_dst_ref,
     link_ref,
-    message2_ref,
     slope2_ref,
     edge2_ref,
+    outof2_ref,
     grads_ref,
-    edge_ref,
 ):
     me, odd, _ = place()
     nodes = nodes_ref[...]
@@ -290,19 +291,15 @@
     coarse_count = share_ref.shape[1]
     total = ndom * coarse_count
 
-    coarse = jnp.concatenate(ordered(mine_ref, theirs_ref, odd, 0, coarse_count), 0)
-    parent_all = jnp.concatenate(
-        ordered(mine_ref, theirs_ref, odd, coarse_count, coarse_count), 0
-    )
-    link_rows = link_ref.shape[0]
+    coarse = ordered(mine_ref, theirs_ref, odd, 0, coarse_count)
+    parent_all = ordered(mine_ref, theirs_ref, odd, 2 * coarse_count, coarse_count)
+    link_rows, lanes = link_ref.shape
     gathered = jnp.zeros(link_ref.shape, F32)
     for chip in range(mine_ref.shape[0]):
         for ref in (mine_ref, theirs_ref):
-            gathered = gathered + ref[
-                chip, 2 * coarse_count : 2 * coarse_count + link_rows, :
-            ].astype(F32)
+            gathered = gathered + ref[chip, 4 * coarse_count :, :].astype(F32)
     link_ref[...] = gathered
-    pieces = -(-edge_count2 // width)
+    pieces = -(-edge_count2 // lanes)
     ends2 = []
     for end in range(2):
         rows = []
@@ -310,28 +307,29 @@
             top = end * pieces + piece
             bottom = (2 + end) * pieces + piece
             code = 256.0 * link_ref[top : top + 1, :] + link_ref[bottom : bottom + 1, :]
-            spot = lax.broadcasted_iota(jnp.int32, code.shape, 1) + piece * width
+            spot = lax.broadcasted_iota(jnp.int32, code.shape, 1) + piece * lanes
             rows.append(jnp.where(spot < edge_count2, code.astype(jnp.int32), -1))
         ends2.append(rows)
-    src2 = dot(coarse, coarse_weights_ref[0]).astype(BF16)
-    dst2 = dot(coarse, coarse_weights_ref[1]).astype(BF16)
+    src2 = dot_nt(upright2_ref[0], coarse).astype(BF16)
+    dst2 = dot_nt(upright2_ref[1], coarse).astype(BF16)
     grad_agg2 = dot_nt(parent_all, coarse_weights_ref[2])
-    grad_agg2_near = grad_agg2.astype(BF16)
-    bias = biases_ref[1:2, :]
-    for piece in range(pieces):
-        span = slice(piece * width, (piece + 1) * width)
-        from_nodes = one_hot_cols(to_column(ends2[0][piece]), total)
-        to_nodes = one_hot_cols(to_column(ends2[1][piece]), total)
-        pre = dot(from_nodes, src2) + dot(to_nodes, dst2) + bias
-        message, slope = silu_and_slope(pre)
-        message2_ref[span, :] = message.astype(BF16)
-        slope2_ref[span, :] = slope.astype(BF16)
-        edge2_ref[span, :] = (dot(to_nodes, grad_agg2_near) * slope).astype(BF16)
-    into = jnp.concatenate([one_hot_rows(row, total) for row in ends2[1]], 1)
-    coarse_sum_ref[...] = dot(into, message2_ref[...]).astype(BF16)
-    grad_dst2 = dot(into, slope2_ref[...]) * grad_agg2
-    back = jnp.concatenate([one_hot_rows(row, total) for row in ends2[0]], 1)
-    grad_src2 = dot(back, edge2_ref[...])
+    grad_agg2_near = dot_nt(coarse_weights_ref[2], parent_all).astype(BF16)
+    bias = column(biases_ref[1:2, :], width)
+    step = 2 * lanes
+    for start in range(0, message2_ref.shape[1], step):
+        span = slice(start, start + step)
+        first = start // lanes
+        outof, into = (
+            one_hot_rows(jnp.concatenate(rows[first : first + 2], 1), total) for rows in ends2
+        )
+        outof2_ref[:, span] = outof
+        into2_ref[:, span] = into
+        message, slope = silu_and_slope(dot(src2, outof) + dot(dst2, into) + bias)
+        message2_ref[:, span] = message.astype(BF16)
+        slope2_ref[:, span] = slope.astype(BF16)
+        edge2_ref[:, span] = (dot(grad_agg2_near, into) * slope).astype(BF16)
+    grad_dst2 = dot_nt(into2_ref[...], slope2_ref[...]) * grad_agg2
+    grad_src2 = dot_nt(outof2_ref[...], edge2_ref[...])
     bias2_ref[...] = jnp.sum(grad_dst2, 0, keepdims=True)
     grad_src2_ref[...] = grad_src2.astype(BF16)
     grad_dst2_ref[...] = grad_dst2.astype(BF16)
@@ -349,20 +347,21 @@
     grad_updated = cotangent_ref[...].astype(F32) + dot(share, high) + dot(share, low)
     grad_updated_ref[...] = grad_updated
 
-    low, high = rims(near_ref[...], far_ref[...], odd)
+    low, high = rims(near_ref, far_ref, odd)
     extended = jnp.concatenate([low, nodes, high], 0)
     rim = low.shape[0]
-    slots = slopes_ref.shape[0]
+    slots = slopes_ref.shape[1]
     grad_updated_near = grad_updated.astype(BF16)
-    grad_summed = dot_nt(grad_updated_near, weights_ref[2])
-    grad_summed_near = grad_summed.astype(BF16)
-    grad_dst = slopes_sum_ref[...] * grad_summed
+    grad_dst = slopes_sum_ref[...] * dot_nt(grad_updated_near, weights_ref[2])
+    grad_summed = dot_nt(weights_ref[2], grad_updated_near).astype(BF16)
     chunk = 2 * EDGE_BLOCK
+    grad_src = jnp.zeros((outof_ref.shape[0], width), F32)
     for start in range(0, slots, chunk):
         span = slice(start, start + chunk)
-        slope = slopes_ref[span, :].astype(F32)
-        edge_ref[span, :] = (dot(to_nodes_ref[span, :], grad_summed_near) * slope).astype(BF16)
-    grad_src = dot(back_ref[...], edge_ref[...]).astype(BF16)
+        slope = slopes_ref[:, span].astype(F32)
+        edge = (dot(grad_summed, into_ref[:, span]) * slope).astype(BF16)
+        grad_src = grad_src + dot_nt(outof_ref[:, span], edge)
+    grad_src = grad_src.astype(BF16)
     bias1 = jnp.sum(grad_dst, 0, keepdims=True)
     grad_dst = grad_dst.astype(BF16)
     grad_src_ref[...] = grad_src
@@ -392,16 +391,23 @@
 
 def pair_kernel(keep_ref, came_ref, blocks_ref):
     half = keep_ref.shape[0] - ROW_TILE
-    chips, depth, _ = blocks_ref.shape
+    chips, _, lanes = blocks_ref.shape
     rows = half // chips
     bias = keep_ref[half:, :].astype(F32) + came_ref[half : half + ROW_TILE, :].astype(F32)
-    bias = two_rows(jnp.sum(bias, 0, keepdims=True), depth - rows)
+    bias = jnp.sum(bias, 0, keepdims=True)
+    row = lax.broadcasted_iota(jnp.int32, (8, lanes), 0)
+    tail = jnp.zeros((8, lanes), F32)
+    for side in range(2):
+        value = bias[:, side * lanes : (side + 1) * lanes]
+        high = value.astype(BF16).astype(F32)
+        tail = jnp.where(row == 2 * side, high, jnp.where(row == 2 * side + 1, value - high, tail))
+    tail = tail.astype(BF16)
     for chip in range(chips):
         span = slice(chip * rows, (chip + 1) * rows)
-        blocks_ref[chip, :rows, :] = (
-            keep_ref[span, :].astype(F32) + came_ref[span, :].astype(F32)
-        ).astype(BF16)
-        blocks_ref[chip, rows:, :] = bias
+        total = (keep_ref[span, :].astype(F32) + came_ref[span, :].astype(F32)).astype(BF16)
+        blocks_ref[chip, :rows, :] = total[:, :lanes]
+        blocks_ref[chip, rows : 2 * rows, :] = total[:, lanes:]
+        blocks_ref[chip, 2 * rows :, :] = tail
 
 
 def coarse_kernel(
@@ -409,7 +415,8 @@
     weights_ref,
     coarse_ref,
     parent_ref,
-    coarse_sum_ref,
+    into2_ref,
+    message2_ref,
     grad_src2_ref,
     grad_dst2_ref,
     updated_ref,
@@ -422,12 +429,14 @@
     moved_ref,
     coarse_grads_ref,
     node_part_ref,
+    coarse_sum_ref,
 ):
     me, odd, _ = place()
     node_count = updated_ref.shape[0]
     coarse_count = family_ref.shape[0]
     rim = lists_ref.shape[1]
     rows = pl.ds(pl.multiple_of(me * coarse_count, coarse_count), coarse_count)
+    coarse_sum_ref[...] = dot_nt(into2_ref[...], message2_ref[...]).astype(BF16)
     coarse_new = coarse_ref[rows, :].astype(F32) + dot(
         coarse_sum_ref[rows, :], coarse_weights_ref[2]
     )
@@ -453,10 +462,15 @@
     total = blocks_ref[0].astype(F32)
     for other in range(1, chips):
         total = total + blocks_ref[other].astype(F32)
-    part = total[:rows].astype(BF16)
+    part = jnp.concatenate([total[:rows], total[rows : 2 * rows]], 1).astype(BF16)
     for other in range(chips):
         part_ref[other] = part
-    bias1_ref[...] = jnp.sum(total[rows:], 0, keepdims=True)
+    lanes = total.shape[1]
+    for side in range(2):
+        row = 2 * rows + 2 * side
+        bias1_ref[:, side * lanes : (side + 1) * lanes] = jnp.sum(
+            total[row : row + 2], 0, keepdims=True
+        )
 
 
 def finish_kernel(
@@ -554,84 +568,96 @@
 
     rim_rows = ((rim, width), BF16)
     square = ((width, width), BF16)
-    near, far, nodes, lists = call(
+    inputs = (
+        nodes,
+        send_lists,
+        fine_weights,
+        edge_ends,
+        cotangent,
+        biases,
+        pool_members,
+        parents,
+        coarse_ends,
+    )
+    (
+        near,
+        far,
+        nodes,
+        lists,
+        fine,
+        edge_ends,
+        upstream,
+        own_biases,
+        pool_members,
+        parents,
+        coarse_ends,
+    ) = call(
         pick_kernel,
-        [rim_rows, rim_rows, (nodes.shape, BF16), (send_lists.shape, jnp.int32)],
-        (nodes, send_lists),
-        2,
-        outside=(0, 1),
-        copies=2,
+        [rim_rows, ((4 * rim, width), BF16)] + [(value.shape, value.dtype) for value in inputs],
+        inputs,
+        4,
+        outside=range(len(inputs)),
+        copies=len(inputs),
     )
     far = lax.ppermute(far, "dom", across)
     near = swap(near)
 
-    pieces = -(-edge_count2 // width)
-    link_rows = round_up(4 * pieces, ROW_TILE)
-    side_rows = coarse_count + link_rows
-    fine, ends, upstream, pre, rim_hot, to_nodes, into, share, family, side = call(
+    lanes = width // 2
+    pieces = round_up(-(-edge_count2 // lanes), 2)
+    link_rows = round_up(4 * pieces, 8)
+    side_rows = 2 * coarse_count + link_rows
+    pre, outof, into, share, family, side, upright, pooled = call(
         functools.partial(prepare_kernel, ndom, rim),
         [
-            (fine_weights.shape, BF16),
-            (edge_ends.shape, jnp.int32),
-            (cotangent.shape, BF16),
-            ((slots, width), F32),
-            ((slots, 2 * rim), BF16),
-            ((slots, node_count), BF16),
+            ((width, slots), F32),
+            ((node_count + 2 * rim, slots), BF16),
             ((node_count, slots), BF16),
             ((node_count, coarse_count), BF16),
             ((coarse_count, node_count), BF16),
-            ((side_rows, width), BF16),
+            ((side_rows, lanes), BF16),
+            square,
+            ((coarse_count, width), F32),
         ],
         (
             nodes,
-            fine_weights,
-            biases,
+            fine,
+            own_biases,
             edge_ends,
             live_blocks,
             pool_members,
             parents,
-            cotangent,
+            upstream,
             coarse_ends,
         ),
         10,
-        scratch=[
-            (biases.shape, F32),
-            (pool_members.shape, jnp.int32),
-            (parents.shape, jnp.int32),
-            (coarse_ends.shape, jnp.int32),
-            ((link_rows, width), F32),
-        ],
+        scratch=[((link_rows, lanes), F32)],
         scalars=(4,),
-        outside=(1, 2, 3, 5, 6, 7, 8),
-        copies=7,
         flops=2 * slots * width * (2 * node_count + 2 * rim),
     )
-    updated, summed, slopes, packet = call(
+    summed, slopes, packet = call(
         functools.partial(forward_kernel, member_count),
         [
-            ((node_count, width), F32),
             ((node_count, width), BF16),
-            ((slots, width), BF16),
-            ((chips, coarse_count + side_rows, width), BF16),
+            ((width, slots), BF16),
+            ((chips, 2 * coarse_count + side_rows, lanes), BF16),
         ],
-        (nodes, near, far, fine, pre, rim_hot, into, share, side),
+        (near, far, upright, fine, pre, outof, into, share, pooled, side),
         10,
-        scratch=[((slots, width), BF16)],
+        scratch=[((width, slots), BF16)],
     )
     mine = exchange(packet)
-    slopes_sum, back = call(
+    slopes_sum, updated, upright2 = call(
         between_kernel,
-        [((node_count, width), F32), ((node_count + 2 * rim, slots), BF16)],
-        (into, slopes, ends, live_blocks),
+        [((node_count, width), F32), ((node_count, width), F32), ((2, width, width), BF16)],
+        (into, slopes, nodes, summed, fine, coarse_weights),
         8,
-        scalars=(3,),
         flops=2 * slots * width * node_count,
     )
     theirs = swap(mine)
 
     rows = round_up(-(-3 * width // ndom), ROW_TILE)
     half = rows * chips
-    edges2 = pieces * width
+    edges2 = pieces * lanes
     coarse_whole = ((total, width), BF16)
     (
         send,
@@ -639,7 +665,8 @@
         far_grad,
         coarse,
         parent_all,
-        coarse_sum,
+        into2,
+        message2,
         grad_src2,
         grad_dst2,
         bias2,
@@ -654,7 +681,8 @@
             rim_rows,
             coarse_whole,
             coarse_whole,
-            coarse_whole,
+            ((total, edges2), BF16),
+            ((width, edges2), BF16),
             coarse_whole,
             coarse_whole,
             ((1, width), F32),
@@ -666,7 +694,8 @@
             mine,
             theirs,
             coarse_weights,
-            biases,
+            upright2,
+            own_biases,
             nodes,
             near,
             far,
@@ -676,21 +705,20 @@
             summed,
             slopes_sum,
             slopes,
-            to_nodes,
-            back,
+            outof,
+            into,
         ),
         20 if total <= 256 else 48,
         scratch=[
-            ((link_rows, width), F32),
-            ((edges2, width), BF16),
-            ((edges2, width), BF16),
-            ((edges2, width), BF16),
+            ((link_rows, lanes), F32),
+            ((width, edges2), BF16),
+            ((width, edges2), BF16),
+            ((total, edges2), BF16),
             ((2 * half, width), BF16),
-            ((slots, width), BF16),
         ],
     )
     came = swap(send)
-    (blocks,) = call(pair_kernel, [((chips, rows + 8, width), BF16)], (keep, came), 4)
+    (blocks,) = call(pair_kernel, [((chips, 2 * rows + 8, lanes), BF16)], (keep, came), 4)
     blocks = exchange(blocks)
     far_grad = lax.ppermute(far_grad, "dom", across)
     moved, coarse_grads, node_part = call(
@@ -705,7 +733,8 @@
             fine,
             coarse,
             parent_all,
-            coarse_sum,
+            into2,
+            message2,
             grad_src2,
             grad_dst2,
             updated,
@@ -716,7 +745,8 @@
             lists,
             came,
         ),
-        8,
+        8 if total <= 256 else 24,
+        scratch=[coarse_whole],
         flops=6 * total * width * width,
     )
     part, bias1 = call(

time: 57.1 us -> 55.2 us (0.967)
  starting transfers between devices: 5.45 us -> 9.33 us
  blocking collectives: 27.8 us -> 24.3 us
  Pallas kernels: 12.1 us -> 10.7 us
  waiting for transfers between devices: 9.94 us -> 9.22 us
    ppermute x4, starting transfers between devices: 0.73 us -> 4.6 us  [swap(): return lax.ppermute(value, 'dom', pairs)]
    all_to_all x2, blocking collectives: 27.8 us -> 24.3 us  [exchange(): return lax.all_to_all(value, 'dom', 0, 0, axis_index_groups=same_core)]
    pallas_call x10, Pallas kernels: 12.1 us -> 10.7 us  [call(): pl.pallas_call(kernel, out_shape=[jax.ShapeDtypeStruct(shape, kind) for s...]
    all_to_all x1, waiting for transfers between devices: 6.98 us -> 6.26 us  [exchange(): return lax.all_to_all(value, 'dom', 0, 0, axis_index_groups=same_core)]
  transfers between devices with their start and end apart: 7 -> 7, of which waited for: 4 -> 4; matrix products, arithmetic and copies ran while one was open for 0% -> 0% of each run, Pallas kernels for 9% -> 7%
where the time goes in v4:
time: 55.2 us; the launch traced here: 54.9 us
  blocking collectives  24.3 us (44%)
  Pallas kernels  10.7 us (19%)
  starting transfers between devices  9.33 us (17%)
  waiting for transfers between devices  9.22 us (17%)
  between operations  1.36 us (2%)
    all_to_all x2, blocking collectives, exchange(): return lax.all_to_all(value, 'dom', 0, 0, axis_index_groups=same_core)  24.3 us
    pallas_call x10, Pallas kernels, call(): pl.pallas_call(kernel, out_shape=[jax.ShapeDtypeStruct(shape, kind) for s...  10.7 us
    all_to_all x1, waiting for transfers between devices, exchange(): return lax.all_to_all(value, 'dom', 0, 0, axis_index_groups=same_core)  6.26 us
    ppermute x4, starting transfers between devices, swap(): return lax.ppermute(value, 'dom', pairs)  4.6 us
    all_to_all x1, starting transfers between devices, exchange(): return lax.all_to_all(value, 'dom', 0, 0, axis_index_groups=same_core)  3.4 us
    ppermute x4, waiting for transfers between devices, swap(): return lax.ppermute(value, 'dom', pairs)  2.95 us
  transfers between devices with their start and end apart: 7, of which 4 were waited for; matrix products, arithmetic and copies ran while one was open for 0% of the time, Pallas kernels for 7%

profile of v4, /device:TPU:0, one launch (start us, length us, event | category | flops | bytes accessed | tf_op | source)
XLA Modules:
  0.0 54.9 jit_solution(6134155945206292582)
XLA Ops:
  0.6 1.1 %shard_map.146 = (bf16[16,256]{1,0:T(8,128)(2,1)S(1)}, bf16[64,256]{1,0:T(8,128)(2,1)S(1)}, bf16[128,256]{1,0:T(8,128)(2,1)S(1)}, s32[2,16]{1,0:T(2,128)S(1)}, b...) custom-call(bf16[128,256]{1,0:T(8,128)(2,1)} %refs_0_.1, ...), custom_call_target="tpu_custom_call" | custom-call | bytes 1121280 | tf_op jit(solution)/shard_map/pallas_call | solution.py:521
  1.8 0.7 %collective-permute-start.1 = (bf16[64,256]{1,0:T(8,128)(2,1)S(1)}, bf16[64,256]{1,0:T(8,128)(2,1)S(1)}, u32[]{:S(2)}, u32[]{:S(2)}) collective-permute-start(bf16[64,256]{1,0:T(8,128)(2,1)S(1)} %get-tuple-element.52), channel_id=1, source_target_pairs={{1,2},{3,4},{5,6},{7,8},{9,10},{11,12},{13,14},{2,1},{4,3},{6,5},{... | collective-permute-start | bytes 98312 | tf_op jit(solution)/shard_map/ppermute | solution.py:602
  2.5 4.4 %collective-permute-start = (bf16[16,256]{1,0:T(8,128)(2,1)S(1)}, bf16[16,256]{1,0:T(8,128)(2,1)S(1)}, u32[]{:S(2)}, u32[]{:S(2)}) collective-permute-start(bf16[16,256]{1,0:T(8,128)(2,1)S(1)} %get-tuple-element.51), channel_id=1, source_target_pairs={{0,1},{1,0},{2,3},{3,2},{4,5},{5,4},{6,7},{7,6},{8,9},{9,8},{10,11... | collective-permute-start | bytes 24584 | tf_op jit(solution)/shard_map/ppermute | solution.py:564
  7.5 0.9 %shard_map.147 = (f32[256,1536]{1,0:T(8,128)S(1)}, bf16[160,1536]{1,0:T(8,128)(2,1)S(1)}, bf16[128,1536]{1,0:T(8,128)(2,1)S(1)}, bf16[128,16]{1,0:T(8,128)(2,1)S...) custom-call(bf16[128,256]{1,0:T(8,128)(2,1)S(1)} %get-tuple-element., ...), custom_call_target="tpu_custom_call" | custom-call | flops 226492416 | bytes 3167620 | tf_op jit(solution)/shard_map/pallas_call | solution.py:521
  8.4 0.0 collective-permute-done.near_ref
  8.4 0.0 collective-permute-done.1.far_ref
  8.4 0.0 copy-start
  8.4 1.4 %shard_map.148 = (bf16[128,256]{1,0:T(8,128)(2,1)S(1)}, bf16[256,1536]{1,0:T(8,128)(2,1)S(1)}, bf16[8,88,128]{2,1,0:T(8,128)(2,1)S(1)}) custom-call(bf16[16,256]{1,0:T(8,128)(2,1)S(1)} %collective-permute-done.near_ref, bf16[64,256]{1,0:T(8,128)(2,1)S(1)} %collective-permute-done.1.far_ref, bf16[256,256]{1,0:T(8,128)(2,1)S(1)} %get-tuple-element.60.upright_ref, ...), custom_call_target="tpu_custom_call" | custom-call | bytes 4089856 | tf_op jit(solution)/shard_map/pallas_call | solution.py:521
  9.8 13.4 %all_to_all.15.mine_ref = bf16[8,88,128]{2,1,0:T(8,128)(2,1)S(1)} all-to-all(bf16[8,88,128]{2,1,0:T(8,128)(2,1)S(1)} %get-tuple-element.67), channel_id=1, replica_groups={{0,2,4,6,8,10,12,14},{1,3,5,7,9,11,13,15},{16,18,20,22,24,26,28,30},{17..., dimensions={0} | all-to-all | bytes 360448 | tf_op jit(solution)/shard_map/all_to_all | solution.py:567
  23.2 0.0 collective-permute-start.2
  23.2 0.0 copy-done
  23.2 0.4 shard_map.149
  23.6 1.0 %collective-permute-done.2.theirs_ref = bf16[8,88,128]{2,1,0:T(8,128)(2,1)S(1)} collective-permute-done((bf16[8,88,128]{2,1,0:T(8,128)(2,1)S(1)}, bf16[8,88,128]{2,1,0:T(8,128)(2,1)S(1)}, u32[]{:S(2)}, u32[]{:S(2)}) %collective-permute-start.2) | collective-permute-done | bytes 180256 | tf_op jit(solution)/shard_map/ppermute | solution.py:564
  24.6 2.5 %shard_map.150 = (bf16[416,256]{1,0:T(8,128)(2,1)S(1)}, bf16[400,256]{1,0:T(8,128)(2,1)S(1)}, bf16[16,256]{1,0:T(8,128)(2,1)S(1)}, bf16[256,256]{1,0:T(8,128)(2,...) custom-call(bf16[8,88,128]{2,1,0:T(8,128)(2,1)S(1)} %all_to_all.15.m, ...), custom_call_target="tpu_custom_call" | custom-call | bytes 5471232 | tf_op jit(solution)/shard_map/pallas_call | solution.py:521
  27.1 0.2 collective-permute-start.3
  27.3 1.3 %collective-permute-done.3.came_ref = bf16[416,256]{1,0:T(8,128)(2,1)S(1)} collective-permute-done((bf16[416,256]{1,0:T(8,128)(2,1)S(1)}, bf16[416,256]{1,0:T(8,128)(2,1)S(1)}, u32[]{:S(2)}, u32[]{:S(2)}) %collective-permute-start.3) | collective-permute-done | bytes 213024 | tf_op jit(solution)/shard_map/ppermute | solution.py:564
  28.6 0.7 %shard_map.152 = bf16[8,104,128]{2,1,0:T(8,128)(2,1)} custom-call(bf16[400,256]{1,0:T(8,128)(2,1)S(1)} %get-tuple-element.88.keep_ref, bf16[416,256]{1,0:T(8,128)(2,1)S(1)} %collective-permute-done.3.came_ref), custom_call_target="tpu_custom_call" | custom-call | bytes 630784 | tf_op jit(solution)/shard_map/pallas_call | solution.py:521
  29.4 3.4 %all-to-all-start.1 = ((bf16[8,104,128]{2,1,0:T(8,128)(2,1)}), bf16[8,104,128]{2,1,0:T(8,128)(2,1)S(1)}, u32[]{:S(2)}, u32[]{:S(2)}) async-start(bf16[8,104,128]{2,1,0:T(8,128)(2,1)} %shard_map.152), calls=%async_computation.1 | async-start | bytes 425984 | tf_op jit(solution)/shard_map/all_to_all | solution.py:567
  32.8 0.7 %collective-permute-start.4 = (bf16[16,256]{1,0:T(8,128)(2,1)S(1)}, bf16[16,256]{1,0:T(8,128)(2,1)S(1)}, u32[]{:S(2)}, u32[]{:S(2)}) collective-permute-start(bf16[16,256]{1,0:T(8,128)(2,1)S(1)} %get-tuple-element.87), channel_id=1, source_target_pairs={{1,2},{3,4},{5,6},{7,8},{9,10},{11,12},{13,14},{2,1},{4,3},{6,5},{... | collective-permute-start | bytes 24584 | tf_op jit(solution)/shard_map/ppermute | solution.py:723
  33.4 1.8 %shard_map.151 = (f32[128,256]{1,0:T(8,128)}, f32[3,256,256]{2,1,0:T(8,128)}, f32[128,256]{1,0:T(8,128)S(1)}) custom-call(bf16[3,256,256]{2,1,0:T(8,128)(2,1)S(1)} %copy-done, bf16[3,256,256]{2,1,0:T(8,128)(2,1)S(1)} %get-tuple-element.50.weights_ref, bf16[256,256]{1,0:T(8,128)(2,1)S(1)} %get-tuple-element.72.coarse_ref, ...), custom_call_target="tpu_custom_call" | custom-call | flops 100663296 | bytes 3772544 | tf_op jit(solution)/shard_map/pallas_call | solution.py:521
  35.2 0.0 collective-permute-done.4.far_grad_ref
  35.2 6.3 %all-to-all-done.1.blocks_ref = bf16[8,104,128]{2,1,0:T(8,128)(2,1)S(1)} async-done(((bf16[8,104,128]{2,1,0:T(8,128)(2,1)}), bf16[8,104,128]{2,1,0:T(8,128)(2,1)S(1)}, u32[]{:S(2)}, u32[]{:S(2)}) %all-to-all-start.1) | async-done | bytes 213024 | tf_op jit(solution)/shard_map/all_to_all | solution.py:567
  41.5 11.0 %all_to_all.16.mine_ref = bf16[8,48,256]{2,1,0:T(8,128)(2,1)S(1)} all-to-all(bf16[8,48,256]{2,1,0:T(8,128)(2,1)S(1)} %get-tuple-element.92), channel_id=1, replica_groups={{0,2,4,6,8,10,12,14},{1,3,5,7,9,11,13,15},{16,18,20,22,24,26,28,30},{17..., dimensions={0} | all-to-all | bytes 393216 | tf_op jit(solution)/shard_map/all_to_all | solution.py:567
  52.5 0.0 collective-permute-start.5
  52.5 0.8 %shard_map.154 = (f32[128,256]{1,0:T(8,128)}, f32[2,256]{1,0:T(2,128)}) custom-call(f32[128,256]{1,0:T(8,128)S(1)} %get-tuple-element.86.node_part_ref, bf16[16,256]{1,0:T(8,128)(2,1)S(1)} %collective-permute-done.4.far_grad_ref, s32[2,16]{1,0:T(2,128)S(1)} %get-tuple-element.83.lists_ref, f32[1,256]{1,0:T(1,128)S(1)} %get-tuple-element.89.bias1_ref, ...), custom_call_target="tpu_custom_call" | custom-call | bytes 274560 | tf_op jit(solution)/shard_map/pallas_call | solution.py:521
  53.3 0.6 %collective-permute-done.5.theirs_ref = bf16[8,48,256]{2,1,0:T(8,128)(2,1)S(1)} collective-permute-done((bf16[8,48,256]{2,1,0:T(8,128)(2,1)S(1)}, bf16[8,48,256]{2,1,0:T(8,128)(2,1)S(1)}, u32[]{:S(2)}, u32[]{:S(2)}) %collective-permute-start.5) | collective-permute-done | bytes 196640 | tf_op jit(solution)/shard_map/ppermute | solution.py:564
  54.0 1.0 %shard_map.155 = f32[768,256]{1,0:T(8,128)} custom-call(bf16[8,48,256]{2,1,0:T(8,128)(2,1)S(1)} %all_to_all.16.mine_ref, bf16[8,48,256]{2,1,0:T(8,128)(2,1)S(1)} %collective-permute-done.5.theirs_ref), custom_call_target="tpu_custom_call" | custom-call | bytes 1179648 | tf_op jit(solution)/shard_map/pallas_call | solution.py:521
  (1 shorter events, 0.0 us)
Async XLA Ops:
  1.8 6.6 %collective-permute-start.1 = (bf16[64,256]{1,0:T(8,128)(2,1)S(1)}, bf16[64,256]{1,0:T(8,128)(2,1)S(1)}, u32[]{:S(2)}, u32[]{:S(2)}) collective-permute-start(bf16[64,256]{1,0:T(8,128)(2,1)S(1)} %get-tuple-element.52), channel_id=1, source_target_pairs={{1,2},{3,4},{5,6},{7,8},{9,10},{11,12},{13,14},{2,1},{4,3},{6,5},{... | collective-permute-start | bytes 98312 | tf_op jit(solution)/shard_map/ppermute | solution.py:602
  2.5 5.9 %collective-permute-start = (bf16[16,256]{1,0:T(8,128)(2,1)S(1)}, bf16[16,256]{1,0:T(8,128)(2,1)S(1)}, u32[]{:S(2)}, u32[]{:S(2)}) collective-permute-start(bf16[16,256]{1,0:T(8,128)(2,1)S(1)} %get-tuple-element.51), channel_id=1, source_target_pairs={{0,1},{1,0},{2,3},{3,2},{4,5},{5,4},{6,7},{7,6},{8,9},{9,8},{10,11... | collective-permute-start | bytes 24584 | tf_op jit(solution)/shard_map/ppermute | solution.py:564
  8.4 14.8 %copy-start = (bf16[3,256,256]{2,1,0:T(8,128)(2,1)S(1)}, bf16[3,256,256]{2,1,0:T(8,128)(2,1)}, u32[]{:S(2)}) copy-start(bf16[3,256,256]{2,1,0:T(8,128)(2,1)} %coarse_weights_ref.5) | copy-start | bytes 1179652
  23.2 1.4 %collective-permute-start.2 = (bf16[8,88,128]{2,1,0:T(8,128)(2,1)S(1)}, bf16[8,88,128]{2,1,0:T(8,128)(2,1)S(1)}, u32[]{:S(2)}, u32[]{:S(2)}) collective-permute-start(bf16[8,88,128]{2,1,0:T(8,128)(2,1)S(1)} %all_to_all.15.mine_ref), channel_id=1, source_target_pairs={{0,1},{1,0},{2,3},{3,2},{4,5},{5,4},{6,7},{7,6},{8,9},{9,8},{10,11... | collective-permute-start | bytes 540680 | tf_op jit(solution)/shard_map/ppermute | solution.py:564
  27.1 1.5 %collective-permute-start.3 = (bf16[416,256]{1,0:T(8,128)(2,1)S(1)}, bf16[416,256]{1,0:T(8,128)(2,1)S(1)}, u32[]{:S(2)}, u32[]{:S(2)}) collective-permute-start(bf16[416,256]{1,0:T(8,128)(2,1)S(1)} %get-tuple-element.84), channel_id=1, source_target_pairs={{0,1},{1,0},{2,3},{3,2},{4,5},{5,4},{6,7},{7,6},{8,9},{9,8},{10,11... | collective-permute-start | bytes 638984 | tf_op jit(solution)/shard_map/ppermute | solution.py:564
  29.4 12.1 %all-to-all-start.1 = ((bf16[8,104,128]{2,1,0:T(8,128)(2,1)}), bf16[8,104,128]{2,1,0:T(8,128)(2,1)S(1)}, u32[]{:S(2)}, u32[]{:S(2)}) async-start(bf16[8,104,128]{2,1,0:T(8,128)(2,1)} %shard_map.152), calls=%async_computation.1 | async-start | bytes 425984 | tf_op jit(solution)/shard_map/all_to_all | solution.py:567
  32.8 2.5 %collective-permute-start.4 = (bf16[16,256]{1,0:T(8,128)(2,1)S(1)}, bf16[16,256]{1,0:T(8,128)(2,1)S(1)}, u32[]{:S(2)}, u32[]{:S(2)}) collective-permute-start(bf16[16,256]{1,0:T(8,128)(2,1)S(1)} %get-tuple-element.87), channel_id=1, source_target_pairs={{1,2},{3,4},{5,6},{7,8},{9,10},{11,12},{13,14},{2,1},{4,3},{6,5},{... | collective-permute-start | bytes 24584 | tf_op jit(solution)/shard_map/ppermute | solution.py:723
  52.5 1.4 %collective-permute-start.5 = (bf16[8,48,256]{2,1,0:T(8,128)(2,1)S(1)}, bf16[8,48,256]{2,1,0:T(8,128)(2,1)S(1)}, u32[]{:S(2)}, u32[]{:S(2)}) collective-permute-start(bf16[8,48,256]{2,1,0:T(8,128)(2,1)S(1)} %all_to_all.16.mine_ref), channel_id=1, source_target_pairs={{0,1},{1,0},{2,3},{3,2},{4,5},{5,4},{6,7},{7,6},{8,9},{9,8},{10,11... | collective-permute-start | bytes 589832 | tf_op jit(solution)/shard_map/ppermute | solution.py:564

commit v5 on v4

--- a/solution.py
+++ b/solution.py
@@ -268,7 +268,6 @@
     into_ref,
     send_ref,
     keep_ref,
-    far_grad_ref,
     coarse_ref,
     parent_ref,
     into2_ref,
@@ -379,8 +378,9 @@
     bias_rows = two_rows(bias1, ROW_TILE)
     keep_ref[half : half + ROW_TILE, :] = bias_rows
     send_ref[half : half + ROW_TILE, :] = bias_rows
-    send_ref[half + ROW_TILE :, :] = jnp.where(odd == 1, low, high)
-    far_grad_ref[...] = jnp.where(odd == 1, high, low)
+    base = half + ROW_TILE
+    send_ref[base : base + rim, :] = jnp.where(odd == 1, low, high)
+    send_ref[base + rim :, :] = jnp.where(odd == 1, high, low)
 
 
 def two_rows(value, count):
@@ -389,36 +389,84 @@
     return jnp.where(row == 0, high, jnp.where(row == 1, value - high, 0.0)).astype(BF16)
 
 
-def pair_kernel(keep_ref, came_ref, blocks_ref):
+def tail_spots(rows, chips, rim):
+    share = -(-rim // chips)
+    chip = rows >> (share.bit_length() - 1)
+    return 8 * chip + 4 + rows - share * chip, share
+
+
+def pair_kernel(keep_ref, came_ref, made_ref, blocks_ref):
     half = keep_ref.shape[0] - ROW_TILE
     chips, _, lanes = blocks_ref.shape
     rows = half // chips
+    rim = (came_ref.shape[0] - half - ROW_TILE) // 2
     bias = keep_ref[half:, :].astype(F32) + came_ref[half : half + ROW_TILE, :].astype(F32)
     bias = jnp.sum(bias, 0, keepdims=True)
-    row = lax.broadcasted_iota(jnp.int32, (8, lanes), 0)
-    tail = jnp.zeros((8, lanes), F32)
+    far = came_ref[half + ROW_TILE + rim :, :]
+    spot, share = tail_spots(lax.broadcasted_iota(jnp.int32, (8 * chips, rim), 1), chips, rim)
+    row = lax.broadcasted_iota(jnp.int32, (8 * chips, rim), 0)
+    line = lax.broadcasted_iota(jnp.int32, (8, lanes), 0)
+    tails = jnp.zeros((8 * chips, lanes), F32)
+    bias_tail = jnp.zeros((8, lanes), F32)
     for side in range(2):
-        value = bias[:, side * lanes : (side + 1) * lanes]
+        span = slice(side * lanes, (side + 1) * lanes)
+        pick = jnp.where(row == spot + side * share, 1.0, 0.0).astype(BF16)
+        tails = tails + dot(pick, far[:, span])
+        value = bias[:, span]
         high = value.astype(BF16).astype(F32)
-        tail = jnp.where(row == 2 * side, high, jnp.where(row == 2 * side + 1, value - high, tail))
-    tail = tail.astype(BF16)
+        bias_tail = jnp.where(line == 2 * side, high, bias_tail)
+        bias_tail = jnp.where(line == 2 * side + 1, value - high, bias_tail)
     for chip in range(chips):
         span = slice(chip * rows, (chip + 1) * rows)
         total = (keep_ref[span, :].astype(F32) + came_ref[span, :].astype(F32)).astype(BF16)
         blocks_ref[chip, :rows, :] = total[:, :lanes]
         blocks_ref[chip, rows : 2 * rows, :] = total[:, lanes:]
-        blocks_ref[chip, 2 * rows :, :] = tail
+        blocks_ref[chip, 2 * rows :, :] = (tails[8 * chip : 8 * chip + 8] + bias_tail).astype(BF16)
+
+
+def sum_kernel(blocks_ref, part_ref, bias1_ref):
+    _, odd, _ = place()
+    chips, depth, lanes = blocks_ref.shape
+    rows = depth - 8
+    total = blocks_ref[0].astype(F32)
+    for other in range(1, chips):
+        total = total + blocks_ref[other].astype(F32)
+    part = total[:rows].astype(BF16)
+    for other in range(chips):
+        after = blocks_ref[min(other + 1, chips - 1), rows:, :]
+        before = blocks_ref[max(other - 1, 0), rows:, :]
+        part_ref[other, :rows, :] = part
+        part_ref[other, rows:, :] = jnp.where(odd == 1, after, before)
+    for side in range(2):
+        row = rows + 2 * side
+        bias1_ref[:, side * lanes : (side + 1) * lanes] = jnp.sum(
+            total[row : row + 2], 0, keepdims=True
+        )
 
 
 def coarse_kernel(
-    coarse_weights_ref,
-    weights_ref,
     coarse_ref,
     parent_ref,
     into2_ref,
     message2_ref,
     grad_src2_ref,
     grad_dst2_ref,
+    coarse_grads_ref,
+    coarse_sum_ref,
+):
+    coarse = coarse_ref[...]
+    coarse_sum = dot_nt(into2_ref[...], message2_ref[...]).astype(BF16)
+    coarse_sum_ref[...] = coarse_sum
+    coarse_grads_ref[0] = dot_tn(coarse, grad_src2_ref[...])
+    coarse_grads_ref[1] = dot_tn(coarse, grad_dst2_ref[...])
+    coarse_grads_ref[2] = dot_tn(coarse_sum, parent_ref[...])
+
+
+def finish_kernel(
+    coarse_weights_ref,
+    weights_ref,
+    coarse_ref,
+    coarse_sum_ref,
     updated_ref,
     family_ref,
     grad_updated_ref,
@@ -426,80 +474,67 @@
     grad_dst_ref,
     lists_ref,
     came_ref,
+    mine_ref,
+    bias1_ref,
+    bias2_ref,
     moved_ref,
-    coarse_grads_ref,
-    node_part_ref,
-    coarse_sum_ref,
+    node_grads_ref,
+    bias_ref,
 ):
-    me, odd, _ = place()
+    me, odd, chip = place()
     node_count = updated_ref.shape[0]
     coarse_count = family_ref.shape[0]
+    chips, depth, lanes = mine_ref.shape
     rim = lists_ref.shape[1]
     rows = pl.ds(pl.multiple_of(me * coarse_count, coarse_count), coarse_count)
-    coarse_sum_ref[...] = dot_nt(into2_ref[...], message2_ref[...]).astype(BF16)
     coarse_new = coarse_ref[rows, :].astype(F32) + dot(
         coarse_sum_ref[rows, :], coarse_weights_ref[2]
     )
     family = family_ref[...]
     high, low = split(coarse_new)
     moved_ref[...] = updated_ref[...] + dot_tn(family, high) + dot_tn(family, low)
-    coarse = coarse_ref[...]
-    coarse_grads_ref[0] = dot_tn(coarse, grad_src2_ref[...])
-    coarse_grads_ref[1] = dot_tn(coarse, grad_dst2_ref[...])
-    coarse_grads_ref[2] = dot_tn(coarse_sum_ref[...], parent_ref[...])
+    both = jnp.concatenate([grad_src_ref[rim : rim + node_count, :], grad_dst_ref[...]], 1)
+    node_grads_ref[...] = grad_updated_ref[...] + dot_nt(
+        both, jnp.concatenate([weights_ref[0], weights_ref[1]], 1)
+    )
     lists = lists_ref[...]
     near_list = jnp.where(odd == 1, lists[0:1], lists[1:2])
-    near = came_ref[came_ref.shape[0] - rim :, :]
-    both = jnp.concatenate([grad_src_ref[rim : rim + node_count, :], grad_dst_ref[...]], 1)
-    node_part_ref[...] = grad_updated_ref[...] + dot_nt(
-        both, jnp.concatenate([weights_ref[0], weights_ref[1]], 1)
-    )
-    node_part_ref[...] += dot(one_hot_rows(near_list, node_count), near)
-
-
-def sum_kernel(blocks_ref, node_part_ref, far_grad_ref, part_ref, bias1_ref):
-    chips, rows, _ = part_ref.shape
-    total = blocks_ref[0].astype(F32)
-    for other in range(1, chips):
-        total = total + blocks_ref[other].astype(F32)
-    part = jnp.concatenate([total[:rows], total[rows : 2 * rows]], 1).astype(BF16)
-    for other in range(chips):
-        part_ref[other] = part
-    lanes = total.shape[1]
+    far_list = jnp.where(odd == 1, lists[1:2], lists[0:1])
+    inside = jnp.logical_or(jnp.logical_and(odd == 1, chip < chips - 1), jnp.logical_and(odd == 0, chip > 0))
+    far_list = jnp.where(inside, far_list, -1)
+    near = came_ref[came_ref.shape[0] - 2 * rim : came_ref.shape[0] - rim, :]
+    node_grads_ref[...] += dot(one_hot_rows(near_list, node_count), near)
+    tails = [mine_ref[other, depth - 8 :, :].astype(F32) for other in range(chips)]
+    tails = jnp.concatenate(tails, 0).astype(BF16)
+    spot, share = tail_spots(lax.broadcasted_iota(jnp.int32, (rim, 8 * chips), 0), chips, rim)
+    column_spot = lax.broadcasted_iota(jnp.int32, (rim, 8 * chips), 1)
+    into = one_hot_rows(far_list, node_count)
     for side in range(2):
-        row = 2 * rows + 2 * side
-        bias1_ref[:, side * lanes : (side + 1) * lanes] = jnp.sum(
-            total[row : row + 2], 0, keepdims=True
-        )
-
-
-def finish_kernel(
-    node_part_ref, far_grad_ref, lists_ref, bias1_ref, bias2_ref, node_grads_ref, bias_ref
-):
-    _, odd, _ = place()
-    lists = lists_ref[...]
-    far_list = jnp.where(odd == 1, lists[1:2], lists[0:1])
-    node_count = node_part_ref.shape[0]
-    node_grads_ref[...] = node_part_ref[...] + dot(
-        one_hot_rows(far_list, node_count), far_grad_ref[...]
-    )
+        pick = jnp.where(column_spot == spot + side * share, 1.0, 0.0).astype(BF16)
+        far = dot(pick, tails).astype(BF16)
+        node_grads_ref[:, side * lanes : (side + 1) * lanes] += dot(into, far)
     bias_ref[0:1, :] = bias1_ref[...]
     bias_ref[1:2, :] = bias2_ref[...]
 
 
 def join_kernel(mine_ref, theirs_ref, out_ref):
     _, odd, _ = place()
-    chips, rows, _ = mine_ref.shape
+    chips, depth, lanes = mine_ref.shape
+    rows = (depth - 8) // 2
     limit = out_ref.shape[0]
-    for side in range(2):
+    for core in range(2):
         for chip in range(chips):
-            start = (side * chips + chip) * rows
+            start = (core * chips + chip) * rows
             count = min(rows, limit - start)
             if count <= 0:
                 continue
-            mine = mine_ref[chip, :count, :]
-            theirs = theirs_ref[chip, :count, :]
-            out_ref[start : start + count, :] = jnp.where(odd == side, mine, theirs).astype(F32)
+            for side in range(2):
+                span = slice(side * rows, side * rows + count)
+                mine = mine_ref[chip, span, :]
+                theirs = theirs_ref[chip, span, :]
+                out_ref[start : start + count, side * lanes : (side + 1) * lanes] = jnp.where(
+                    odd == core, mine, theirs
+                ).astype(F32)
 
 
 def call(kernel, outs, args, room, scratch=(), scalars=(), outside=(), copies=0, flops=0):
@@ -662,7 +697,6 @@
     (
         send,
         keep,
-        far_grad,
         coarse,
         parent_all,
         into2,
@@ -676,9 +710,8 @@
     ) = call(
         functools.partial(backward_kernel, ndom, edge_count2, member_count),
         [
-            ((half + ROW_TILE + rim, width), BF16),
+            ((half + ROW_TILE + 2 * rim, width), BF16),
             ((half + ROW_TILE, width), BF16),
-            rim_rows,
             coarse_whole,
             coarse_whole,
             ((total, edges2), BF16),
@@ -718,25 +751,26 @@
         ],
     )
     came = swap(send)
-    (blocks,) = call(pair_kernel, [((chips, 2 * rows + 8, lanes), BF16)], (keep, came), 4)
+    coarse_grads, coarse_sum = call(
+        coarse_kernel,
+        [((3, width, width), F32), coarse_whole],
+        (coarse, parent_all, into2, message2, grad_src2, grad_dst2),
+        8 if total <= 256 else 24,
+        flops=6 * total * width * width,
+    )
+    block = ((chips, 2 * rows + 8, lanes), BF16)
+    (blocks,) = call(pair_kernel, [block], (keep, came, coarse_sum), 4)
     blocks = exchange(blocks)
-    far_grad = lax.ppermute(far_grad, "dom", across)
-    moved, coarse_grads, node_part = call(
-        coarse_kernel,
-        [
-            ((node_count, width), F32),
-            ((3, width, width), F32),
-            ((node_count, width), F32),
-        ],
+    part, bias1 = call(sum_kernel, [block, ((1, width), F32)], (blocks,), 4)
+    mine = exchange(part)
+    moved, node_grads, bias_grads = call(
+        finish_kernel,
+        [((node_count, width), F32), ((node_count, width), F32), ((2, width), F32)],
         (
             coarse_weights,
             fine,
             coarse,
-            parent_all,
-            into2,
-            message2,
-            grad_src2,
-            grad_dst2,
+            coarse_sum,
             updated,
             family,
             grad_updated,
@@ -744,23 +778,12 @@
             grad_dst,
             lists,
             came,
+            mine,
+            bias1,
+            bias2,
         ),
-        8 if total <= 256 else 24,
-        scratch=[coarse_whole],
-        flops=6 * total * width * width,
-    )
-    part, bias1 = call(
-        sum_kernel,
-        [((chips, rows, width), BF16), ((1, width), F32)],
-        (blocks, node_part, far_grad),
-        4,
-    )
-    mine = exchange(part)
-    node_grads, bias_grads = call(
-        finish_kernel,
-        [((node_count, width), F32), ((2, width), F32)],
-        (node_part, far_grad, lists, bias1, bias2),
-        4,
+        8,
+        flops=8 * node_count * width * width,
     )
     theirs = swap(mine)
     (fine_grads,) = call(join_kernel, [((3 * width, width), F32)], (mine, theirs), 4)

time: 55.2 us -> 54.2 us (0.982)
  blocking collectives: 24.3 us -> 35.8 us
  waiting for transfers between devices: 9.22 us -> 1.12 us
  starting transfers between devices: 9.33 us -> 5.28 us
    all_to_all x2 -> x3, blocking collectives: 24.3 us -> 35.8 us  [exchange(): return lax.all_to_all(value, 'dom', 0, 0, axis_index_groups=same_core)]
    all_to_all x1 -> x0, waiting for transfers between devices: 6.26 us -> none  [exchange(): return lax.all_to_all(value, 'dom', 0, 0, axis_index_groups=same_core)]
    all_to_all x1 -> x0, starting transfers between devices: 3.4 us -> none  [exchange(): return lax.all_to_all(value, 'dom', 0, 0, axis_index_groups=same_core)]
    ppermute x4, waiting for transfers between devices: 2.95 us -> 1.11 us  [swap(): return lax.ppermute(value, 'dom', pairs)]
    ppermute x1 -> x0, starting transfers between devices: 0.66 us -> none  [shards(): far_grad = lax.ppermute(far_grad, 'dom', across)]
  transfers between devices with their start and end apart: 7 -> 5, of which waited for: 4 -> 2; matrix products, arithmetic and copies ran while one was open for 0% -> 0% of each run, Pallas kernels for 7% -> 8%
where the time goes in v5:
time: 54.2 us; the launch traced here: 53.9 us
  blocking collectives  35.8 us (66%)
  Pallas kernels  10.4 us (19%)
  starting transfers between devices  5.28 us (10%)
  between operations  1.35 us (2%)
  waiting for transfers between devices  1.12 us (2%)
    all_to_all x3, blocking collectives, exchange(): return lax.all_to_all(value, 'dom', 0, 0, axis_index_groups=same_core)  35.8 us
    pallas_call x10, Pallas kernels, call(): pl.pallas_call(kernel, out_shape=[jax.ShapeDtypeStruct(shape, kind) for s...  10.4 us
    ppermute x4, starting transfers between devices, swap(): return lax.ppermute(value, 'dom', pairs)  4.61 us
    ppermute x4, waiting for transfers between devices, swap(): return lax.ppermute(value, 'dom', pairs)  1.11 us
  transfers between devices with their start and end apart: 5, of which 2 were waited for; matrix products, arithmetic and copies ran while one was open for 0% of the time, Pallas kernels for 8%

profile of v5, /device:TPU:0, one launch (start us, length us, event | category | flops | bytes accessed | tf_op | source)
XLA Modules:
  0.0 53.9 jit_solution(9319177015842305527)
XLA Ops:
  0.6 1.1 %shard_map.146 = (bf16[16,256]{1,0:T(8,128)(2,1)S(1)}, bf16[64,256]{1,0:T(8,128)(2,1)S(1)}, bf16[128,256]{1,0:T(8,128)(2,1)S(1)}, s32[2,16]{1,0:T(2,128)S(1)}, b...) custom-call(bf16[128,256]{1,0:T(8,128)(2,1)} %refs_0_.1, ...), custom_call_target="tpu_custom_call" | custom-call | bytes 1121280 | tf_op jit(solution)/shard_map/pallas_call | solution.py:556
  1.8 0.7 %collective-permute-start.1 = (bf16[64,256]{1,0:T(8,128)(2,1)S(1)}, bf16[64,256]{1,0:T(8,128)(2,1)S(1)}, u32[]{:S(2)}, u32[]{:S(2)}) collective-permute-start(bf16[64,256]{1,0:T(8,128)(2,1)S(1)} %get-tuple-element.51), channel_id=1, source_target_pairs={{1,2},{3,4},{5,6},{7,8},{9,10},{11,12},{13,14},{2,1},{4,3},{6,5},{... | collective-permute-start | bytes 98312 | tf_op jit(solution)/shard_map/ppermute | solution.py:637
  2.5 4.4 %collective-permute-start = (bf16[16,256]{1,0:T(8,128)(2,1)S(1)}, bf16[16,256]{1,0:T(8,128)(2,1)S(1)}, u32[]{:S(2)}, u32[]{:S(2)}) collective-permute-start(bf16[16,256]{1,0:T(8,128)(2,1)S(1)} %get-tuple-element.50), channel_id=1, source_target_pairs={{0,1},{1,0},{2,3},{3,2},{4,5},{5,4},{6,7},{7,6},{8,9},{9,8},{10,11... | collective-permute-start | bytes 24584 | tf_op jit(solution)/shard_map/ppermute | solution.py:599
  7.5 0.9 %shard_map.147 = (f32[256,1536]{1,0:T(8,128)S(1)}, bf16[160,1536]{1,0:T(8,128)(2,1)S(1)}, bf16[128,1536]{1,0:T(8,128)(2,1)S(1)}, bf16[128,16]{1,0:T(8,128)(2,1)S...) custom-call(bf16[128,256]{1,0:T(8,128)(2,1)S(1)} %get-tuple-element., ...), custom_call_target="tpu_custom_call" | custom-call | flops 226492416 | bytes 3167620 | tf_op jit(solution)/shard_map/pallas_call | solution.py:556
  8.4 0.0 collective-permute-done.near_ref
  8.4 0.0 collective-permute-done.1.far_ref
  8.4 0.0 copy-start
  8.4 1.4 %shard_map.148 = (bf16[128,256]{1,0:T(8,128)(2,1)S(1)}, bf16[256,1536]{1,0:T(8,128)(2,1)S(1)}, bf16[8,88,128]{2,1,0:T(8,128)(2,1)S(1)}) custom-call(bf16[16,256]{1,0:T(8,128)(2,1)S(1)} %collective-permute-done.near_ref, bf16[64,256]{1,0:T(8,128)(2,1)S(1)} %collective-permute-done.1.far_ref, bf16[256,256]{1,0:T(8,128)(2,1)S(1)} %get-tuple-element.59.upright_ref, ...), custom_call_target="tpu_custom_call" | custom-call | bytes 4089856 | tf_op jit(solution)/shard_map/pallas_call | solution.py:556
  9.8 13.4 %all_to_all.15.mine_ref = bf16[8,88,128]{2,1,0:T(8,128)(2,1)S(1)} all-to-all(bf16[8,88,128]{2,1,0:T(8,128)(2,1)S(1)} %get-tuple-element.66), channel_id=1, replica_groups={{0,2,4,6,8,10,12,14},{1,3,5,7,9,11,13,15},{16,18,20,22,24,26,28,30},{17..., dimensions={0} | all-to-all | bytes 360448 | tf_op jit(solution)/shard_map/all_to_all | solution.py:602
  23.2 0.0 collective-permute-start.2
  23.2 0.0 copy-done
  23.2 0.4 shard_map.149
  23.6 1.0 %collective-permute-done.2.theirs_ref = bf16[8,88,128]{2,1,0:T(8,128)(2,1)S(1)} collective-permute-done((bf16[8,88,128]{2,1,0:T(8,128)(2,1)S(1)}, bf16[8,88,128]{2,1,0:T(8,128)(2,1)S(1)}, u32[]{:S(2)}, u32[]{:S(2)}) %collective-permute-start.2) | collective-permute-done | bytes 180256 | tf_op jit(solution)/shard_map/ppermute | solution.py:599
  24.6 2.5 %shard_map.150 = (bf16[432,256]{1,0:T(8,128)(2,1)S(1)}, bf16[400,256]{1,0:T(8,128)(2,1)S(1)}, bf16[256,256]{1,0:T(8,128)(2,1)S(1)}, bf16[256,256]{1,0:T(8,128)(2...) custom-call(bf16[8,88,128]{2,1,0:T(8,128)(2,1)S(1)} %all_to_all.15.m, ...), custom_call_target="tpu_custom_call" | custom-call | bytes 5471232 | tf_op jit(solution)/shard_map/pallas_call | solution.py:556
  27.1 0.2 collective-permute-start.3
  27.3 1.5 %shard_map.151 = (f32[3,256,256]{2,1,0:T(8,128)}, bf16[256,256]{1,0:T(8,128)(2,1)S(1)}) custom-call(bf16[256,256]{1,0:T(8,128)(2,1)S(1)} %get-tuple-element.71.coarse_ref, bf16[256,256]{1,0:T(8,128)(2,1)S(1)} %get-tuple-element.72.parent_ref, bf16[256,768]{1,0:T(8,128)(2,1)S(1)} %get-tuple-element.73.into2_ref, ...), custom_call_target="tpu_custom_call" | custom-call | flops 100663296 | bytes 2228224 | tf_op jit(solution)/shard_map/pallas_call | solution.py:556
  28.8 0.0 collective-permute-done.3.came_ref
  28.8 0.1 shard_map.152
  29.0 11.5 %all_to_all.16.blocks_ref = bf16[8,104,128]{2,1,0:T(8,128)(2,1)S(1)} all-to-all(bf16[8,104,128]{2,1,0:T(8,128)(2,1)S(1)} %shard_map.152), channel_id=1, replica_groups={{0,2,4,6,8,10,12,14},{1,3,5,7,9,11,13,15},{16,18,20,22,24,26,28,30},{17..., dimensions={0} | all-to-all | bytes 425984 | tf_op jit(solution)/shard_map/all_to_all | solution.py:602
  40.5 11.0 %all_to_all.17.mine_ref = bf16[8,104,128]{2,1,0:T(8,128)(2,1)S(1)} all-to-all(bf16[8,104,128]{2,1,0:T(8,128)(2,1)S(1)} %get-tuple-element.86), channel_id=1, replica_groups={{0,2,4,6,8,10,12,14},{1,3,5,7,9,11,13,15},{16,18,20,22,24,26,28,30},{17..., dimensions={0} | all-to-all | bytes 425984 | tf_op jit(solution)/shard_map/all_to_all | solution.py:602
  51.4 0.0 collective-permute-start.4
  51.4 1.3 %shard_map.154 = (f32[128,256]{1,0:T(8,128)}, f32[128,256]{1,0:T(8,128)}, f32[2,256]{1,0:T(2,128)}) custom-call(bf16[3,256,256]{2,1,0:T(8,128)(2,1)S(1)} %copy-done, bf16[3,256,256]{2,1,0:T(8,128)(2,1)S(1)} %get-tuple-element.49.weights_ref, bf16[256,256]{1,0:T(8,128)(2,1)S(1)} %get-tuple-element.71.coarse_ref, ...), custom_call_target="tpu_custom_call" | custom-call | flops 67108864 | bytes 2162816 | tf_op jit(solution)/shard_map/pallas_call | solution.py:556
  52.8 0.1 collective-permute-done.4.theirs_ref
  52.9 1.0 %shard_map.155 = f32[768,256]{1,0:T(8,128)} custom-call(bf16[8,104,128]{2,1,0:T(8,128)(2,1)S(1)} %all_to_all.17.mine_ref, bf16[8,104,128]{2,1,0:T(8,128)(2,1)S(1)} %collective-permute-done.4.theirs_ref), custom_call_target="tpu_custom_call" | custom-call | bytes 1212416 | tf_op jit(solution)/shard_map/pallas_call | solution.py:556
  (1 shorter events, 0.0 us)
Async XLA Ops:
  1.8 6.6 %collective-permute-start.1 = (bf16[64,256]{1,0:T(8,128)(2,1)S(1)}, bf16[64,256]{1,0:T(8,128)(2,1)S(1)}, u32[]{:S(2)}, u32[]{:S(2)}) collective-permute-start(bf16[64,256]{1,0:T(8,128)(2,1)S(1)} %get-tuple-element.51), channel_id=1, source_target_pairs={{1,2},{3,4},{5,6},{7,8},{9,10},{11,12},{13,14},{2,1},{4,3},{6,5},{... | collective-permute-start | bytes 98312 | tf_op jit(solution)/shard_map/ppermute | solution.py:637
  2.5 5.9 %collective-permute-start = (bf16[16,256]{1,0:T(8,128)(2,1)S(1)}, bf16[16,256]{1,0:T(8,128)(2,1)S(1)}, u32[]{:S(2)}, u32[]{:S(2)}) collective-permute-start(bf16[16,256]{1,0:T(8,128)(2,1)S(1)} %get-tuple-element.50), channel_id=1, source_target_pairs={{0,1},{1,0},{2,3},{3,2},{4,5},{5,4},{6,7},{7,6},{8,9},{9,8},{10,11... | collective-permute-start | bytes 24584 | tf_op jit(solution)/shard_map/ppermute | solution.py:599
  8.4 14.8 %copy-start = (bf16[3,256,256]{2,1,0:T(8,128)(2,1)S(1)}, bf16[3,256,256]{2,1,0:T(8,128)(2,1)}, u32[]{:S(2)}) copy-start(bf16[3,256,256]{2,1,0:T(8,128)(2,1)} %coarse_weights_ref.5) | copy-start | bytes 1179652
  23.2 1.4 %collective-permute-start.2 = (bf16[8,88,128]{2,1,0:T(8,128)(2,1)S(1)}, bf16[8,88,128]{2,1,0:T(8,128)(2,1)S(1)}, u32[]{:S(2)}, u32[]{:S(2)}) collective-permute-start(bf16[8,88,128]{2,1,0:T(8,128)(2,1)S(1)} %all_to_all.15.mine_ref), channel_id=1, source_target_pairs={{0,1},{1,0},{2,3},{3,2},{4,5},{5,4},{6,7},{7,6},{8,9},{9,8},{10,11... | collective-permute-start | bytes 540680 | tf_op jit(solution)/shard_map/ppermute | solution.py:599
  27.1 1.7 %collective-permute-start.3 = (bf16[432,256]{1,0:T(8,128)(2,1)S(1)}, bf16[432,256]{1,0:T(8,128)(2,1)S(1)}, u32[]{:S(2)}, u32[]{:S(2)}) collective-permute-start(bf16[432,256]{1,0:T(8,128)(2,1)S(1)} %get-tuple-element.84), channel_id=1, source_target_pairs={{0,1},{1,0},{2,3},{3,2},{4,5},{5,4},{6,7},{7,6},{8,9},{9,8},{10,11... | collective-permute-start | bytes 663560 | tf_op jit(solution)/shard_map/ppermute | solution.py:599
  51.4 1.5 %collective-permute-start.4 = (bf16[8,104,128]{2,1,0:T(8,128)(2,1)S(1)}, bf16[8,104,128]{2,1,0:T(8,128)(2,1)S(1)}, u32[]{:S(2)}, u32[]{:S(2)}) collective-permute-start(bf16[8,104,128]{2,1,0:T(8,128)(2,1)S(1)} %all_to_all.17.mine_ref), channel_id=1, source_target_pairs={{0,1},{1,0},{2,3},{3,2},{4,5},{5,4},{6,7},{7,6},{8,9},{9,8},{10,11... | collective-permute-start | bytes 638984 | tf_op jit(solution)/shard_map/ppermute | solution.py:599

commit v6 on v5

--- a/solution.py
+++ b/solution.py
@@ -13,6 +13,7 @@
 EDGE_BLOCK = 128
 ROW_TILE = 16
 MIB = 1024 * 1024
+JOIN_COPIES = 4
 
 
 def dot(left, right):
@@ -84,8 +85,7 @@
     far = jnp.where(odd == 1, lists[1:2], lists[0:1])
     nodes = outputs[0][...]
     rim = near_ref.shape[0]
-    near = dot_tn(one_hot_rows(near, nodes.shape[0]), nodes).astype(BF16)
-    near_ref[...] = near
+    near_ref[...] = dot_tn(one_hot_rows(near, nodes.shape[0]), nodes).astype(BF16)
     far = dot_tn(one_hot_rows(far, nodes.shape[0]), nodes).astype(BF16)
     for start in range(0, far_ref.shape[0], rim):
         far_ref[start : start + rim, :] = far
@@ -186,7 +186,6 @@
     summed_ref,
     slopes_ref,
     packet_ref,
-    message_ref,
 ):
     _, odd, _ = place()
     low, high = rims(near_ref, far_ref, odd)
@@ -195,13 +194,14 @@
     rim_proj = dot_nt(upright_ref[...], jnp.concatenate([low, high], 0)).astype(BF16)
     slots = pre_ref.shape[1]
     chunk = 2 * EDGE_BLOCK
+    summed = jnp.zeros((node_count, pre_ref.shape[0]), F32)
     for start in range(0, slots, chunk):
         span = slice(start, start + chunk)
         at_rim = jnp.concatenate([outof_ref[:rim, span], outof_ref[rim + node_count :, span]], 0)
         message, slope = silu_and_slope(pre_ref[:, span] + dot(rim_proj, at_rim))
-        message_ref[:, span] = message.astype(BF16)
+        summed = summed + dot_nt(into_ref[:, span], message.astype(BF16))
         slopes_ref[:, span] = slope.astype(BF16)
-    summed = dot_nt(into_ref[...], message_ref[...]).astype(BF16)
+    summed = summed.astype(BF16)
     summed_ref[...] = summed
     high, low = split(dot_tn(share_ref[...], summed))
     pooled = pooled_ref[...] + dot(high, weights_ref[2]) + dot(low, weights_ref[2])
@@ -477,10 +477,17 @@
     mine_ref,
     bias1_ref,
     bias2_ref,
+    coarse_grads_ref,
     moved_ref,
     node_grads_ref,
     bias_ref,
+    coarse_grads_hbm,
+    sems,
 ):
+    copy = pltpu.make_async_copy(coarse_grads_ref, coarse_grads_hbm, sems.at[0])
+    copy.start()
+    bias_ref[0:1, :] = bias1_ref[...]
+    bias_ref[1:2, :] = bias2_ref[...]
     me, odd, chip = place()
     node_count = updated_ref.shape[0]
     coarse_count = family_ref.shape[0]
@@ -513,31 +520,70 @@
         pick = jnp.where(column_spot == spot + side * share, 1.0, 0.0).astype(BF16)
         far = dot(pick, tails).astype(BF16)
         node_grads_ref[:, side * lanes : (side + 1) * lanes] += dot(into, far)
-    bias_ref[0:1, :] = bias1_ref[...]
-    bias_ref[1:2, :] = bias2_ref[...]
-
-
-def join_kernel(mine_ref, theirs_ref, out_ref):
+    copy.wait()
+
+
+def join_kernel(
+    mine_ref,
+    theirs_ref,
+    moved_ref,
+    node_grads_ref,
+    bias_ref,
+    out_hbm,
+    moved_hbm,
+    node_grads_hbm,
+    bias_hbm,
+    out_ref,
+    sems,
+):
+    ready = (
+        (bias_ref, bias_hbm),
+        (moved_ref, moved_hbm),
+        (node_grads_ref, node_grads_hbm),
+    )
+    copies = [
+        pltpu.make_async_copy(source, target, sems.at[spot])
+        for spot, (source, target) in enumerate(ready)
+    ]
+    for copy in copies:
+        copy.start()
     _, odd, _ = place()
     chips, depth, lanes = mine_ref.shape
     rows = (depth - 8) // 2
     limit = out_ref.shape[0]
-    for core in range(2):
-        for chip in range(chips):
-            start = (core * chips + chip) * rows
-            count = min(rows, limit - start)
-            if count <= 0:
-                continue
-            for side in range(2):
-                span = slice(side * rows, side * rows + count)
-                mine = mine_ref[chip, span, :]
-                theirs = theirs_ref[chip, span, :]
-                out_ref[start : start + count, side * lanes : (side + 1) * lanes] = jnp.where(
-                    odd == core, mine, theirs
-                ).astype(F32)
-
-
-def call(kernel, outs, args, room, scratch=(), scalars=(), outside=(), copies=0, flops=0):
+    pieces = 0
+    done = 0
+    for block in range(2 * chips):
+        core, chip = divmod(block, chips)
+        start = block * rows
+        count = min(rows, limit - start)
+        if count <= 0:
+            break
+        for side in range(2):
+            span = slice(side * rows, side * rows + count)
+            mine = mine_ref[chip, span, :]
+            theirs = theirs_ref[chip, span, :]
+            out_ref[start : start + count, side * lanes : (side + 1) * lanes] = jnp.where(
+                odd == core, mine, theirs
+            ).astype(F32)
+        end = start + count
+        if end == limit or end >= (pieces + 1) * limit // JOIN_COPIES:
+            pieces += 1
+            span = pl.ds(done, end - done)
+            copies.append(
+                pltpu.make_async_copy(
+                    out_ref.at[span, :], out_hbm.at[span, :], sems.at[len(copies)]
+                )
+            )
+            copies[-1].start()
+            done = end
+    for copy in copies:
+        copy.wait()
+
+
+def call(
+    kernel, outs, args, room, scratch=(), scalars=(), outside=(), copies=0, flops=0, outgoing=()
+):
     vmem = pl.BlockSpec(memory_space=pltpu.VMEM)
     scalar = pl.BlockSpec(memory_space=pltpu.SMEM)
     hbm = pl.BlockSpec(memory_space=pltpu.HBM)
@@ -557,7 +603,7 @@
         kernel,
         out_shape=[jax.ShapeDtypeStruct(shape, kind) for shape, kind in outs],
         in_specs=specs,
-        out_specs=[vmem] * len(outs),
+        out_specs=[hbm if spot in outgoing else vmem for spot in range(len(outs))],
         scratch_shapes=scratch,
         compiler_params=pltpu.CompilerParams(vmem_limit_bytes=room * MIB),
         cost_estimate=pl.CostEstimate(flops=flops, bytes_accessed=moved, transcendentals=0),
@@ -678,7 +724,6 @@
         ],
         (near, far, upright, fine, pre, outof, into, share, pooled, side),
         10,
-        scratch=[((width, slots), BF16)],
     )
     mine = exchange(packet)
     slopes_sum, updated, upright2 = call(
@@ -763,9 +808,12 @@
     blocks = exchange(blocks)
     part, bias1 = call(sum_kernel, [block, ((1, width), F32)], (blocks,), 4)
     mine = exchange(part)
-    moved, node_grads, bias_grads = call(
+    coarse_grads_shape = ((3, width, width), F32)
+    node_shape = ((node_count, width), F32)
+    bias_shape = ((2, width), F32)
+    moved, node_grads, bias_grads, coarse_grads = call(
         finish_kernel,
-        [((node_count, width), F32), ((node_count, width), F32), ((2, width), F32)],
+        [node_shape, node_shape, bias_shape, coarse_grads_shape],
         (
             coarse_weights,
             fine,
@@ -781,12 +829,23 @@
             mine,
             bias1,
             bias2,
+            coarse_grads,
         ),
         8,
+        copies=1,
+        outgoing=(3,),
         flops=8 * node_count * width * width,
     )
     theirs = swap(mine)
-    (fine_grads,) = call(join_kernel, [((3 * width, width), F32)], (mine, theirs), 4)
+    fine_grads, moved, node_grads, bias_grads = call(
+        join_kernel,
+        [((3 * width, width), F32), node_shape, node_shape, bias_shape],
+        (mine, theirs, moved, node_grads, bias_grads),
+        4,
+        scratch=[((3 * width, width), F32)],
+        copies=3 + JOIN_COPIES,
+        outgoing=range(4),
+    )
     return moved, node_grads, fine_grads.reshape(3, width, width), coarse_grads, bias_grads
 
 

time: 54.2 us -> 53.7 us (level)
  Pallas kernels: 10.4 us -> 9.17 us
  waiting for transfers between devices: 1.12 us -> 2.07 us
    pallas_call x10, Pallas kernels: 10.4 us -> 9.17 us  [call(): pl.pallas_call(kernel, out_shape=[jax.ShapeDtypeStruct(shape, kind) for s...]
    ppermute x4, waiting for transfers between devices: 1.11 us -> 2.06 us  [swap(): return lax.ppermute(value, 'dom', pairs)]
  transfers between devices with their start and end apart: 5 -> 5, of which waited for: 2 -> 3; matrix products, arithmetic and copies ran while one was open for 0% -> 0% of each run, Pallas kernels for 8% -> 6%
where the time goes in v6:
time: 53.7 us; the launch traced here: 53.5 us
  blocking collectives  35.6 us (66%)
  Pallas kernels  9.17 us (17%)
  starting transfers between devices  5.27 us (10%)
  waiting for transfers between devices  2.07 us (4%)
  between operations  1.36 us (3%)
    all_to_all x3, blocking collectives, exchange(): return lax.all_to_all(value, 'dom', 0, 0, axis_index_groups=same_core)  35.6 us
    pallas_call x10, Pallas kernels, call(): pl.pallas_call(kernel, out_shape=[jax.ShapeDtypeStruct(shape, kind) for s...  9.17 us
    ppermute x4, starting transfers between devices, swap(): return lax.ppermute(value, 'dom', pairs)  4.61 us
    ppermute x4, waiting for transfers between devices, swap(): return lax.ppermute(value, 'dom', pairs)  2.06 us
  transfers between devices with their start and end apart: 5, of which 3 were waited for; matrix products, arithmetic and copies ran while one was open for 0% of the time, Pallas kernels for 6%

profile of v6, /device:TPU:0, one launch (start us, length us, event | category | flops | bytes accessed | tf_op | source)
XLA Modules:
  0.0 53.5 jit_solution(4125290201251925350)
XLA Ops:
  0.6 1.1 %shard_map.146 = (bf16[16,256]{1,0:T(8,128)(2,1)S(1)}, bf16[64,256]{1,0:T(8,128)(2,1)S(1)}, bf16[128,256]{1,0:T(8,128)(2,1)S(1)}, s32[2,16]{1,0:T(2,128)S(1)}, b...) custom-call(bf16[128,256]{1,0:T(8,128)(2,1)} %refs_0_.1, ...), custom_call_target="tpu_custom_call" | custom-call | bytes 1121280 | tf_op jit(solution)/shard_map/pallas_call | solution.py:602
  1.8 0.7 %collective-permute-start.1 = (bf16[64,256]{1,0:T(8,128)(2,1)S(1)}, bf16[64,256]{1,0:T(8,128)(2,1)S(1)}, u32[]{:S(2)}, u32[]{:S(2)}) collective-permute-start(bf16[64,256]{1,0:T(8,128)(2,1)S(1)} %get-tuple-element.55), channel_id=1, source_target_pairs={{1,2},{3,4},{5,6},{7,8},{9,10},{11,12},{13,14},{2,1},{4,3},{6,5},{... | collective-permute-start | bytes 98312 | tf_op jit(solution)/shard_map/ppermute | solution.py:683
  2.5 4.4 %collective-permute-start = (bf16[16,256]{1,0:T(8,128)(2,1)S(1)}, bf16[16,256]{1,0:T(8,128)(2,1)S(1)}, u32[]{:S(2)}, u32[]{:S(2)}) collective-permute-start(bf16[16,256]{1,0:T(8,128)(2,1)S(1)} %get-tuple-element.54), channel_id=1, source_target_pairs={{0,1},{1,0},{2,3},{3,2},{4,5},{5,4},{6,7},{7,6},{8,9},{9,8},{10,11... | collective-permute-start | bytes 24584 | tf_op jit(solution)/shard_map/ppermute | solution.py:645
  7.5 0.9 %shard_map.147 = (f32[256,1536]{1,0:T(8,128)S(1)}, bf16[160,1536]{1,0:T(8,128)(2,1)S(1)}, bf16[128,1536]{1,0:T(8,128)(2,1)S(1)}, bf16[128,16]{1,0:T(8,128)(2,1)S...) custom-call(bf16[128,256]{1,0:T(8,128)(2,1)S(1)} %get-tuple-element., ...), custom_call_target="tpu_custom_call" | custom-call | flops 226492416 | bytes 3167620 | tf_op jit(solution)/shard_map/pallas_call | solution.py:602
  8.4 0.0 collective-permute-done.near_ref
  8.4 0.0 collective-permute-done.1.far_ref
  8.4 0.0 copy-start
  8.4 1.3 %shard_map.148 = (bf16[128,256]{1,0:T(8,128)(2,1)S(1)}, bf16[256,1536]{1,0:T(8,128)(2,1)S(1)}, bf16[8,88,128]{2,1,0:T(8,128)(2,1)S(1)}) custom-call(bf16[16,256]{1,0:T(8,128)(2,1)S(1)} %collective-permute-done.near_ref, bf16[64,256]{1,0:T(8,128)(2,1)S(1)} %collective-permute-done.1.far_ref, bf16[256,256]{1,0:T(8,128)(2,1)S(1)} %get-tuple-element.64.upright_ref, ...), custom_call_target="tpu_custom_call" | custom-call | bytes 4089856 | tf_op jit(solution)/shard_map/pallas_call | solution.py:602
  9.7 13.4 %all_to_all.15.mine_ref = bf16[8,88,128]{2,1,0:T(8,128)(2,1)S(1)} all-to-all(bf16[8,88,128]{2,1,0:T(8,128)(2,1)S(1)} %get-tuple-element.71), channel_id=1, replica_groups={{0,2,4,6,8,10,12,14},{1,3,5,7,9,11,13,15},{16,18,20,22,24,26,28,30},{17..., dimensions={0} | all-to-all | bytes 360448 | tf_op jit(solution)/shard_map/all_to_all | solution.py:648
  23.1 0.0 collective-permute-start.2
  23.1 0.0 copy-done
  23.1 0.4 shard_map.149
  23.5 1.0 %collective-permute-done.2.theirs_ref = bf16[8,88,128]{2,1,0:T(8,128)(2,1)S(1)} collective-permute-done((bf16[8,88,128]{2,1,0:T(8,128)(2,1)S(1)}, bf16[8,88,128]{2,1,0:T(8,128)(2,1)S(1)}, u32[]{:S(2)}, u32[]{:S(2)}) %collective-permute-start.2) | collective-permute-done | bytes 180256 | tf_op jit(solution)/shard_map/ppermute | solution.py:645
  24.5 2.5 %shard_map.150 = (bf16[432,256]{1,0:T(8,128)(2,1)S(1)}, bf16[400,256]{1,0:T(8,128)(2,1)S(1)}, bf16[256,256]{1,0:T(8,128)(2,1)S(1)}, bf16[256,256]{1,0:T(8,128)(2...) custom-call(bf16[8,88,128]{2,1,0:T(8,128)(2,1)S(1)} %all_to_all.15.m, ...), custom_call_target="tpu_custom_call" | custom-call | bytes 5471232 | tf_op jit(solution)/shard_map/pallas_call | solution.py:602
  27.0 0.2 collective-permute-start.3
  27.2 0.6 %shard_map.151 = (f32[3,256,256]{2,1,0:T(8,128)S(1)}, bf16[256,256]{1,0:T(8,128)(2,1)S(1)}) custom-call(bf16[256,256]{1,0:T(8,128)(2,1)S(1)} %get-tuple-element.78.coarse_ref, bf16[256,256]{1,0:T(8,128)(2,1)S(1)} %get-tuple-element.79.parent_ref, bf16[256,768]{1,0:T(8,128)(2,1)S(1)} %get-tuple-element.80.into2_ref, ...), custom_call_target="tpu_custom_call" | custom-call | flops 100663296 | bytes 2228224 | tf_op jit(solution)/shard_map/pallas_call | solution.py:602
  27.8 0.7 %collective-permute-done.3.came_ref = bf16[432,256]{1,0:T(8,128)(2,1)S(1)} collective-permute-done((bf16[432,256]{1,0:T(8,128)(2,1)S(1)}, bf16[432,256]{1,0:T(8,128)(2,1)S(1)}, u32[]{:S(2)}, u32[]{:S(2)}) %collective-permute-start.3) | collective-permute-done | bytes 221216 | tf_op jit(solution)/shard_map/ppermute | solution.py:645
  28.6 0.1 shard_map.152
  28.7 11.3 %all_to_all.16.blocks_ref = bf16[8,104,128]{2,1,0:T(8,128)(2,1)S(1)} all-to-all(bf16[8,104,128]{2,1,0:T(8,128)(2,1)S(1)} %shard_map.152), channel_id=1, replica_groups={{0,2,4,6,8,10,12,14},{1,3,5,7,9,11,13,15},{16,18,20,22,24,26,28,30},{17..., dimensions={0} | all-to-all | bytes 425984 | tf_op jit(solution)/shard_map/all_to_all | solution.py:648
  40.0 11.0 %all_to_all.17.mine_ref = bf16[8,104,128]{2,1,0:T(8,128)(2,1)S(1)} all-to-all(bf16[8,104,128]{2,1,0:T(8,128)(2,1)S(1)} %get-tuple-element.85), channel_id=1, replica_groups={{0,2,4,6,8,10,12,14},{1,3,5,7,9,11,13,15},{16,18,20,22,24,26,28,30},{17..., dimensions={0} | all-to-all | bytes 425984 | tf_op jit(solution)/shard_map/all_to_all | solution.py:648
  51.0 0.0 collective-permute-start.4
  51.0 1.1 %shard_map.154 = (f32[128,256]{1,0:T(8,128)S(1)}, f32[128,256]{1,0:T(8,128)S(1)}, f32[2,256]{1,0:T(2,128)S(1)}, f32[3,256,256]{2,1,0:T(8,128)}) custom-call(bf16[3,256,256]{2,1,0:T(8,128)(2,1)S(1)} %copy-done, bf16[3,256,256]{2,1,0:T(8,128)(2,1)S(1)} %get-tuple-element.57.weights_ref, bf16[256,256]{1,0:T(8,128)(2,1)S(1)} %get-tuple-element.78.coarse_ref, ...), custom_call_target="tpu_custom_call" | custom-call | flops 67108864 | bytes 3735680 | tf_op jit(solution)/shard_map/pallas_call | solution.py:602
  52.1 0.3 collective-permute-done.4.theirs_ref
  52.4 1.0 %shard_map.155 = (f32[768,256]{1,0:T(8,128)}, f32[128,256]{1,0:T(8,128)}, f32[128,256]{1,0:T(8,128)}, f32[2,256]{1,0:T(2,128)}) custom-call(bf16[8,104,128]{2,1,0:T(8,128)(2,1)S(1)} %all_to_all.17.mine_ref, bf16[8,104,128]{2,1,0:T(8,128)(2,1)S(1)} %collective-permute-done.4.theirs_ref, f32[128,256]{1,0:T(8,128)S(1)} %get-tuple-element.95.moved_ref, ...), custom_call_target="tpu_custom_call" | custom-call | bytes 1740800 | tf_op jit(solution)/shard_map/pallas_call | solution.py:602
  (1 shorter events, 0.0 us)
Async XLA Ops:
  1.8 6.6 %collective-permute-start.1 = (bf16[64,256]{1,0:T(8,128)(2,1)S(1)}, bf16[64,256]{1,0:T(8,128)(2,1)S(1)}, u32[]{:S(2)}, u32[]{:S(2)}) collective-permute-start(bf16[64,256]{1,0:T(8,128)(2,1)S(1)} %get-tuple-element.55), channel_id=1, source_target_pairs={{1,2},{3,4},{5,6},{7,8},{9,10},{11,12},{13,14},{2,1},{4,3},{6,5},{... | collective-permute-start | bytes 98312 | tf_op jit(solution)/shard_map/ppermute | solution.py:683
  2.5 5.9 %collective-permute-start = (bf16[16,256]{1,0:T(8,128)(2,1)S(1)}, bf16[16,256]{1,0:T(8,128)(2,1)S(1)}, u32[]{:S(2)}, u32[]{:S(2)}) collective-permute-start(bf16[16,256]{1,0:T(8,128)(2,1)S(1)} %get-tuple-element.54), channel_id=1, source_target_pairs={{0,1},{1,0},{2,3},{3,2},{4,5},{5,4},{6,7},{7,6},{8,9},{9,8},{10,11... | collective-permute-start | bytes 24584 | tf_op jit(solution)/shard_map/ppermute | solution.py:645
  8.4 14.7 %copy-start = (bf16[3,256,256]{2,1,0:T(8,128)(2,1)S(1)}, bf16[3,256,256]{2,1,0:T(8,128)(2,1)}, u32[]{:S(2)}) copy-start(bf16[3,256,256]{2,1,0:T(8,128)(2,1)} %coarse_weights_ref.5) | copy-start | bytes 1179652
  23.1 1.4 %collective-permute-start.2 = (bf16[8,88,128]{2,1,0:T(8,128)(2,1)S(1)}, bf16[8,88,128]{2,1,0:T(8,128)(2,1)S(1)}, u32[]{:S(2)}, u32[]{:S(2)}) collective-permute-start(bf16[8,88,128]{2,1,0:T(8,128)(2,1)S(1)} %all_to_all.15.mine_ref), channel_id=1, source_target_pairs={{0,1},{1,0},{2,3},{3,2},{4,5},{5,4},{6,7},{7,6},{8,9},{9,8},{10,11... | collective-permute-start | bytes 540680 | tf_op jit(solution)/shard_map/ppermute | solution.py:645
  27.0 1.5 %collective-permute-start.3 = (bf16[432,256]{1,0:T(8,128)(2,1)S(1)}, bf16[432,256]{1,0:T(8,128)(2,1)S(1)}, u32[]{:S(2)}, u32[]{:S(2)}) collective-permute-start(bf16[432,256]{1,0:T(8,128)(2,1)S(1)} %get-tuple-element.77), channel_id=1, source_target_pairs={{0,1},{1,0},{2,3},{3,2},{4,5},{5,4},{6,7},{7,6},{8,9},{9,8},{10,11... | collective-permute-start | bytes 663560 | tf_op jit(solution)/shard_map/ppermute | solution.py:645
  51.0 1.5 %collective-permute-start.4 = (bf16[8,104,128]{2,1,0:T(8,128)(2,1)S(1)}, bf16[8,104,128]{2,1,0:T(8,128)(2,1)S(1)}, u32[]{:S(2)}, u32[]{:S(2)}) collective-permute-start(bf16[8,104,128]{2,1,0:T(8,128)(2,1)S(1)} %all_to_all.17.mine_ref), channel_id=1, source_target_pairs={{0,1},{1,0},{2,3},{3,2},{4,5},{5,4},{6,7},{7,6},{8,9},{9,8},{10,11... | collective-permute-start | bytes 638984 | tf_op jit(solution)/shard_map/ppermute | solution.py:645

commit v7 on v6

--- a/solution.py
+++ b/solution.py
@@ -100,7 +100,6 @@
 
 
 def prepare_kernel(
-    ndom,
     rim,
     nodes_ref,
     weights_ref,
@@ -121,7 +120,6 @@
     pooled_ref,
     link_ref,
 ):
-    me, _, _ = place()
     node_count, width = nodes_ref.shape
     coarse_count = family_ref.shape[0]
     slots = ends_ref.shape[1]
@@ -152,22 +150,9 @@
 
     links = links_ref[...]
     own = links.shape[1]
-    pieces = -(-own * ndom // lanes)
-    spot = lax.broadcasted_iota(jnp.int32, (own, pieces * lanes), 1)
-    source = lax.broadcasted_iota(jnp.int32, (own, pieces * lanes), 0)
-    spread = jnp.where(spot == source + me * own, 1.0, 0.0).astype(BF16)
-    coded = (
-        dot((links >> 8).astype(F32).astype(BF16), spread),
-        dot((links & 255).astype(F32).astype(BF16), spread),
-    )
     link_ref[...] = jnp.zeros(link_ref.shape, F32)
-    for part in range(2):
-        for end in range(2):
-            for piece in range(pieces):
-                row = (part * 2 + end) * pieces + piece
-                link_ref[row : row + 1, :] = coded[part][
-                    end : end + 1, piece * lanes : (piece + 1) * lanes
-                ]
+    link_ref[0:2, :own] = (links >> 8).astype(F32)
+    link_ref[2:4, :own] = (links & 255).astype(F32)
     side_ref[2 * coarse_count :, :] = link_ref[...].astype(BF16)
 
 
@@ -215,7 +200,17 @@
         packet_ref[chip, 2 * count :, :] = side
 
 
+def edge_ends2(packet_ref, repeat_ref, block_ref):
+    links = [packet_ref[chip, packet_ref.shape[1] - 8 :, :] for chip in range(packet_ref.shape[0])]
+    links = jnp.concatenate([link.astype(F32) for link in links], 0).astype(BF16)
+    code = dot(links, repeat_ref[...]) * block_ref[...]
+    code = jnp.sum(code.reshape(packet_ref.shape[0], 8, code.shape[1]), 0)
+    return (256.0 * code[0:2] + code[2:4]).astype(jnp.int32)
+
+
 def between_kernel(
+    own,
+    mine_ref,
     into_ref,
     slopes_ref,
     nodes_ref,
@@ -225,7 +220,19 @@
     slopes_sum_ref,
     updated_ref,
     upright2_ref,
+    repeat_ref,
+    block_ref,
+    ends2_ref,
 ):
+    edge = lax.broadcasted_iota(jnp.int32, repeat_ref.shape, 1)
+    owner = ((edge.astype(F32) + 0.5) * (1.0 / own)).astype(jnp.int32)
+    spot = lax.broadcasted_iota(jnp.int32, repeat_ref.shape, 0)
+    repeat_ref[...] = jnp.where(edge - own * owner == spot, 1.0, 0.0).astype(BF16)
+    edge = lax.broadcasted_iota(jnp.int32, block_ref.shape, 1)
+    owner = ((edge.astype(F32) + 0.5) * (1.0 / own)).astype(jnp.int32)
+    block = lax.broadcasted_iota(jnp.int32, block_ref.shape, 0) >> 3
+    block_ref[...] = jnp.where(block == owner, 1.0, 0.0)
+    ends2_ref[...] = edge_ends2(mine_ref, repeat_ref, block_ref)
     for spot in range(2):
         upright2_ref[spot] = jnp.transpose(coarse_weights_ref[spot].astype(F32)).astype(BF16)
     slopes_sum_ref[...] = dot_nt(into_ref[...], slopes_ref[...])
@@ -248,12 +255,14 @@
 
 def backward_kernel(
     ndom,
-    edge_count2,
     member_count,
     mine_ref,
     theirs_ref,
     coarse_weights_ref,
     upright2_ref,
+    repeat_ref,
+    block_ref,
+    ends2_ref,
     biases_ref,
     nodes_ref,
     near_ref,
@@ -278,7 +287,6 @@
     grad_updated_ref,
     grad_src_ref,
     grad_dst_ref,
-    link_ref,
     slope2_ref,
     edge2_ref,
     outof2_ref,
@@ -292,35 +300,17 @@
 
     coarse = ordered(mine_ref, theirs_ref, odd, 0, coarse_count)
     parent_all = ordered(mine_ref, theirs_ref, odd, 2 * coarse_count, coarse_count)
-    link_rows, lanes = link_ref.shape
-    gathered = jnp.zeros(link_ref.shape, F32)
-    for chip in range(mine_ref.shape[0]):
-        for ref in (mine_ref, theirs_ref):
-            gathered = gathered + ref[chip, 4 * coarse_count :, :].astype(F32)
-    link_ref[...] = gathered
-    pieces = -(-edge_count2 // lanes)
-    ends2 = []
-    for end in range(2):
-        rows = []
-        for piece in range(pieces):
-            top = end * pieces + piece
-            bottom = (2 + end) * pieces + piece
-            code = 256.0 * link_ref[top : top + 1, :] + link_ref[bottom : bottom + 1, :]
-            spot = lax.broadcasted_iota(jnp.int32, code.shape, 1) + piece * lanes
-            rows.append(jnp.where(spot < edge_count2, code.astype(jnp.int32), -1))
-        ends2.append(rows)
+    ends2 = jnp.concatenate([ends2_ref[...], edge_ends2(theirs_ref, repeat_ref, block_ref)], 1)
     src2 = dot_nt(upright2_ref[0], coarse).astype(BF16)
     dst2 = dot_nt(upright2_ref[1], coarse).astype(BF16)
     grad_agg2 = dot_nt(parent_all, coarse_weights_ref[2])
     grad_agg2_near = dot_nt(coarse_weights_ref[2], parent_all).astype(BF16)
     bias = column(biases_ref[1:2, :], width)
-    step = 2 * lanes
+    step = width
     for start in range(0, message2_ref.shape[1], step):
         span = slice(start, start + step)
-        first = start // lanes
-        outof, into = (
-            one_hot_rows(jnp.concatenate(rows[first : first + 2], 1), total) for rows in ends2
-        )
+        outof = one_hot_rows(ends2[0:1, span], total)
+        into = one_hot_rows(ends2[1:2, span], total)
         outof2_ref[:, span] = outof
         into2_ref[:, span] = into
         message, slope = silu_and_slope(dot(src2, outof) + dot(dst2, into) + bias)
@@ -684,11 +674,9 @@
     near = swap(near)
 
     lanes = width // 2
-    pieces = round_up(-(-edge_count2 // lanes), 2)
-    link_rows = round_up(4 * pieces, 8)
-    side_rows = 2 * coarse_count + link_rows
+    side_rows = 2 * coarse_count + 8
     pre, outof, into, share, family, side, upright, pooled = call(
-        functools.partial(prepare_kernel, ndom, rim),
+        functools.partial(prepare_kernel, rim),
         [
             ((width, slots), F32),
             ((node_count + 2 * rim, slots), BF16),
@@ -711,7 +699,7 @@
             coarse_ends,
         ),
         10,
-        scratch=[((link_rows, lanes), F32)],
+        scratch=[((8, lanes), F32)],
         scalars=(4,),
         flops=2 * slots * width * (2 * node_count + 2 * rim),
     )
@@ -726,10 +714,18 @@
         10,
     )
     mine = exchange(packet)
-    slopes_sum, updated, upright2 = call(
-        between_kernel,
-        [((node_count, width), F32), ((node_count, width), F32), ((2, width, width), BF16)],
-        (into, slopes, nodes, summed, fine, coarse_weights),
+    edges2 = edge_count2 // 2
+    slopes_sum, updated, upright2, repeat, block, ends2 = call(
+        functools.partial(between_kernel, coarse_ends.shape[1]),
+        [
+            ((node_count, width), F32),
+            ((node_count, width), F32),
+            ((2, width, width), BF16),
+            ((lanes, edges2), BF16),
+            ((8 * chips, edges2), F32),
+            ((2, edges2), jnp.int32),
+        ],
+        (mine, into, slopes, nodes, summed, fine, coarse_weights),
         8,
         flops=2 * slots * width * node_count,
     )
@@ -737,7 +733,6 @@
 
     rows = round_up(-(-3 * width // ndom), ROW_TILE)
     half = rows * chips
-    edges2 = pieces * lanes
     coarse_whole = ((total, width), BF16)
     (
         send,
@@ -753,14 +748,14 @@
         grad_src,
         grad_dst,
     ) = call(
-        functools.partial(backward_kernel, ndom, edge_count2, member_count),
+        functools.partial(backward_kernel, ndom, member_count),
         [
             ((half + ROW_TILE + 2 * rim, width), BF16),
             ((half + ROW_TILE, width), BF16),
             coarse_whole,
             coarse_whole,
-            ((total, edges2), BF16),
-            ((width, edges2), BF16),
+            ((total, edge_count2), BF16),
+            ((width, edge_count2), BF16),
             coarse_whole,
             coarse_whole,
             ((1, width), F32),
@@ -773,6 +768,9 @@
             theirs,
             coarse_weights,
             upright2,
+            repeat,
+            block,
+            ends2,
             own_biases,
             nodes,
             near,
@@ -788,10 +786,9 @@
         ),
         20 if total <= 256 else 48,
         scratch=[
-            ((link_rows, lanes), F32),
-            ((width, edges2), BF16),
-            ((width, edges2), BF16),
-            ((total, edges2), BF16),
+            ((width, edge_count2), BF16),
+            ((width, edge_count2), BF16),
+            ((total, edge_count2), BF16),
             ((2 * half, width), BF16),
         ],
     )
@@ -803,10 +800,10 @@
         8 if total <= 256 else 24,
         flops=6 * total * width * width,
     )
-    block = ((chips, 2 * rows + 8, lanes), BF16)
-    (blocks,) = call(pair_kernel, [block], (keep, came, coarse_sum), 4)
+    packet = ((chips, 2 * rows + 8, lanes), BF16)
+    (blocks,) = call(pair_kernel, [packet], (keep, came, coarse_sum), 4)
     blocks = exchange(blocks)
-    part, bias1 = call(sum_kernel, [block, ((1, width), F32)], (blocks,), 4)
+    part, bias1 = call(sum_kernel, [packet, ((1, width), F32)], (blocks,), 4)
     mine = exchange(part)
     coarse_grads_shape = ((3, width, width), F32)
     node_shape = ((node_count, width), F32)

time: 53.7 us -> 53.7 us (level)
  no operation moved by 1% of the time
where the time goes in v7:
time: 53.7 us; the launch traced here: 53.5 us
  blocking collectives  35.6 us (66%)
  Pallas kernels  9.2 us (17%)
  starting transfers between devices  5.28 us (10%)
  waiting for transfers between devices  2 us (4%)
  between operations  1.37 us (3%)
    all_to_all x3, blocking collectives, exchange(): return lax.all_to_all(value, 'dom', 0, 0, axis_index_groups=same_core)  35.6 us
    pallas_call x10, Pallas kernels, call(): pl.pallas_call(kernel, out_shape=[jax.ShapeDtypeStruct(shape, kind) for s...  9.2 us
    ppermute x4, starting transfers between devices, swap(): return lax.ppermute(value, 'dom', pairs)  4.61 us
    ppermute x4, waiting for transfers between devices, swap(): return lax.ppermute(value, 'dom', pairs)  2 us
  transfers between devices with their start and end apart: 5, of which 3 were waited for; matrix products, arithmetic and copies ran while one was open for 0% of the time, Pallas kernels for 6%

profile of v7, /device:TPU:0, one launch (start us, length us, event | category | flops | bytes accessed | tf_op | source)
XLA Modules:
  0.0 53.5 jit_solution(16401843608428751874)
XLA Ops:
  0.6 1.1 %shard_map.146 = (bf16[16,256]{1,0:T(8,128)(2,1)S(1)}, bf16[64,256]{1,0:T(8,128)(2,1)S(1)}, bf16[128,256]{1,0:T(8,128)(2,1)S(1)}, s32[2,16]{1,0:T(2,128)S(1)}, b...) custom-call(bf16[128,256]{1,0:T(8,128)(2,1)} %refs_0_.1, ...), custom_call_target="tpu_custom_call" | custom-call | bytes 1121280 | tf_op jit(solution)/shard_map/pallas_call | solution.py:592
  1.8 0.7 %collective-permute-start.1 = (bf16[64,256]{1,0:T(8,128)(2,1)S(1)}, bf16[64,256]{1,0:T(8,128)(2,1)S(1)}, u32[]{:S(2)}, u32[]{:S(2)}) collective-permute-start(bf16[64,256]{1,0:T(8,128)(2,1)S(1)} %get-tuple-element.58), channel_id=1, source_target_pairs={{1,2},{3,4},{5,6},{7,8},{9,10},{11,12},{13,14},{2,1},{4,3},{6,5},{... | collective-permute-start | bytes 98312 | tf_op jit(solution)/shard_map/ppermute | solution.py:673
  2.5 4.4 %collective-permute-start = (bf16[16,256]{1,0:T(8,128)(2,1)S(1)}, bf16[16,256]{1,0:T(8,128)(2,1)S(1)}, u32[]{:S(2)}, u32[]{:S(2)}) collective-permute-start(bf16[16,256]{1,0:T(8,128)(2,1)S(1)} %get-tuple-element.57), channel_id=1, source_target_pairs={{0,1},{1,0},{2,3},{3,2},{4,5},{5,4},{6,7},{7,6},{8,9},{9,8},{10,11... | collective-permute-start | bytes 24584 | tf_op jit(solution)/shard_map/ppermute | solution.py:635
  7.5 0.9 %shard_map.147 = (f32[256,1536]{1,0:T(8,128)S(1)}, bf16[160,1536]{1,0:T(8,128)(2,1)S(1)}, bf16[128,1536]{1,0:T(8,128)(2,1)S(1)}, bf16[128,16]{1,0:T(8,128)(2,1)S...) custom-call(bf16[128,256]{1,0:T(8,128)(2,1)S(1)} %get-tuple-element., ...), custom_call_target="tpu_custom_call" | custom-call | flops 226492416 | bytes 3163524 | tf_op jit(solution)/shard_map/pallas_call | solution.py:592
  8.4 0.0 collective-permute-done.near_ref
  8.4 0.0 collective-permute-done.1.far_ref
  8.4 0.0 copy-start
  8.4 1.3 %shard_map.148 = (bf16[128,256]{1,0:T(8,128)(2,1)S(1)}, bf16[256,1536]{1,0:T(8,128)(2,1)S(1)}, bf16[8,72,128]{2,1,0:T(8,128)(2,1)S(1)}) custom-call(bf16[16,256]{1,0:T(8,128)(2,1)S(1)} %collective-permute-done.near_ref, bf16[64,256]{1,0:T(8,128)(2,1)S(1)} %collective-permute-done.1.far_ref, bf16[256,256]{1,0:T(8,128)(2,1)S(1)} %get-tuple-element.67.upright_ref, ...), custom_call_target="tpu_custom_call" | custom-call | bytes 4052992 | tf_op jit(solution)/shard_map/pallas_call | solution.py:592
  9.7 13.1 %all_to_all.15.mine_ref = bf16[8,72,128]{2,1,0:T(8,128)(2,1)S(1)} all-to-all(bf16[8,72,128]{2,1,0:T(8,128)(2,1)S(1)} %get-tuple-element.74), channel_id=1, replica_groups={{0,2,4,6,8,10,12,14},{1,3,5,7,9,11,13,15},{16,18,20,22,24,26,28,30},{17..., dimensions={0} | all-to-all | bytes 294912 | tf_op jit(solution)/shard_map/all_to_all | solution.py:638
  22.9 0.0 collective-permute-start.2
  22.9 0.0 copy-done
  22.9 0.4 shard_map.149
  23.3 0.9 %collective-permute-done.2.theirs_ref = bf16[8,72,128]{2,1,0:T(8,128)(2,1)S(1)} collective-permute-done((bf16[8,72,128]{2,1,0:T(8,128)(2,1)S(1)}, bf16[8,72,128]{2,1,0:T(8,128)(2,1)S(1)}, u32[]{:S(2)}, u32[]{:S(2)}) %collective-permute-start.2) | collective-permute-done | bytes 147488 | tf_op jit(solution)/shard_map/ppermute | solution.py:635
  24.2 2.5 %shard_map.150 = (bf16[432,256]{1,0:T(8,128)(2,1)S(1)}, bf16[400,256]{1,0:T(8,128)(2,1)S(1)}, bf16[256,256]{1,0:T(8,128)(2,1)S(1)}, bf16[256,256]{1,0:T(8,128)(2...) custom-call(bf16[8,72,128]{2,1,0:T(8,128)(2,1)S(1)} %all_to_all.15.m, ...), custom_call_target="tpu_custom_call" | custom-call | bytes 5605376 | tf_op jit(solution)/shard_map/pallas_call | solution.py:592
  26.8 0.2 collective-permute-start.3
  27.0 0.6 %shard_map.151 = (f32[3,256,256]{2,1,0:T(8,128)S(1)}, bf16[256,256]{1,0:T(8,128)(2,1)S(1)}) custom-call(bf16[256,256]{1,0:T(8,128)(2,1)S(1)} %get-tuple-element.84.coarse_ref, bf16[256,256]{1,0:T(8,128)(2,1)S(1)} %get-tuple-element.85.parent_ref, bf16[256,768]{1,0:T(8,128)(2,1)S(1)} %get-tuple-element.86.into2_ref, ...), custom_call_target="tpu_custom_call" | custom-call | flops 100663296 | bytes 2228224 | tf_op jit(solution)/shard_map/pallas_call | solution.py:592
  27.6 0.7 %collective-permute-done.3.came_ref = bf16[432,256]{1,0:T(8,128)(2,1)S(1)} collective-permute-done((bf16[432,256]{1,0:T(8,128)(2,1)S(1)}, bf16[432,256]{1,0:T(8,128)(2,1)S(1)}, u32[]{:S(2)}, u32[]{:S(2)}) %collective-permute-start.3) | collective-permute-done | bytes 221216 | tf_op jit(solution)/shard_map/ppermute | solution.py:635
  28.3 0.1 shard_map.152
  28.5 11.2 %all_to_all.16.blocks_ref = bf16[8,104,128]{2,1,0:T(8,128)(2,1)S(1)} all-to-all(bf16[8,104,128]{2,1,0:T(8,128)(2,1)S(1)} %shard_map.152), channel_id=1, replica_groups={{0,2,4,6,8,10,12,14},{1,3,5,7,9,11,13,15},{16,18,20,22,24,26,28,30},{17..., dimensions={0} | all-to-all | bytes 425984 | tf_op jit(solution)/shard_map/all_to_all | solution.py:638
  39.7 11.3 %all_to_all.17.mine_ref = bf16[8,104,128]{2,1,0:T(8,128)(2,1)S(1)} all-to-all(bf16[8,104,128]{2,1,0:T(8,128)(2,1)S(1)} %get-tuple-element.91), channel_id=1, replica_groups={{0,2,4,6,8,10,12,14},{1,3,5,7,9,11,13,15},{16,18,20,22,24,26,28,30},{17..., dimensions={0} | all-to-all | bytes 425984 | tf_op jit(solution)/shard_map/all_to_all | solution.py:638
  51.0 0.0 collective-permute-start.4
  51.0 1.1 %shard_map.154 = (f32[128,256]{1,0:T(8,128)S(1)}, f32[128,256]{1,0:T(8,128)S(1)}, f32[2,256]{1,0:T(2,128)S(1)}, f32[3,256,256]{2,1,0:T(8,128)}) custom-call(bf16[3,256,256]{2,1,0:T(8,128)(2,1)S(1)} %copy-done, bf16[3,256,256]{2,1,0:T(8,128)(2,1)S(1)} %get-tuple-element.60.weights_ref, bf16[256,256]{1,0:T(8,128)(2,1)S(1)} %get-tuple-element.84.coarse_ref, ...), custom_call_target="tpu_custom_call" | custom-call | flops 67108864 | bytes 3735680 | tf_op jit(solution)/shard_map/pallas_call | solution.py:592
  52.1 0.3 collective-permute-done.4.theirs_ref
  52.4 1.0 %shard_map.155 = (f32[768,256]{1,0:T(8,128)}, f32[128,256]{1,0:T(8,128)}, f32[128,256]{1,0:T(8,128)}, f32[2,256]{1,0:T(2,128)}) custom-call(bf16[8,104,128]{2,1,0:T(8,128)(2,1)S(1)} %all_to_all.17.mine_ref, bf16[8,104,128]{2,1,0:T(8,128)(2,1)S(1)} %collective-permute-done.4.theirs_ref, f32[128,256]{1,0:T(8,128)S(1)} %get-tuple-element.101.moved_ref, ...), custom_call_target="tpu_custom_call" | custom-call | bytes 1740800 | tf_op jit(solution)/shard_map/pallas_call | solution.py:592
  (1 shorter events, 0.0 us)
Async XLA Ops:
  1.8 6.6 %collective-permute-start.1 = (bf16[64,256]{1,0:T(8,128)(2,1)S(1)}, bf16[64,256]{1,0:T(8,128)(2,1)S(1)}, u32[]{:S(2)}, u32[]{:S(2)}) collective-permute-start(bf16[64,256]{1,0:T(8,128)(2,1)S(1)} %get-tuple-element.58), channel_id=1, source_target_pairs={{1,2},{3,4},{5,6},{7,8},{9,10},{11,12},{13,14},{2,1},{4,3},{6,5},{... | collective-permute-start | bytes 98312 | tf_op jit(solution)/shard_map/ppermute | solution.py:673
  2.5 5.9 %collective-permute-start = (bf16[16,256]{1,0:T(8,128)(2,1)S(1)}, bf16[16,256]{1,0:T(8,128)(2,1)S(1)}, u32[]{:S(2)}, u32[]{:S(2)}) collective-permute-start(bf16[16,256]{1,0:T(8,128)(2,1)S(1)} %get-tuple-element.57), channel_id=1, source_target_pairs={{0,1},{1,0},{2,3},{3,2},{4,5},{5,4},{6,7},{7,6},{8,9},{9,8},{10,11... | collective-permute-start | bytes 24584 | tf_op jit(solution)/shard_map/ppermute | solution.py:635
  8.4 14.5 %copy-start = (bf16[3,256,256]{2,1,0:T(8,128)(2,1)S(1)}, bf16[3,256,256]{2,1,0:T(8,128)(2,1)}, u32[]{:S(2)}) copy-start(bf16[3,256,256]{2,1,0:T(8,128)(2,1)} %coarse_weights_ref.5) | copy-start | bytes 1179652
  22.9 1.4 %collective-permute-start.2 = (bf16[8,72,128]{2,1,0:T(8,128)(2,1)S(1)}, bf16[8,72,128]{2,1,0:T(8,128)(2,1)S(1)}, u32[]{:S(2)}, u32[]{:S(2)}) collective-permute-start(bf16[8,72,128]{2,1,0:T(8,128)(2,1)S(1)} %all_to_all.15.mine_ref), channel_id=1, source_target_pairs={{0,1},{1,0},{2,3},{3,2},{4,5},{5,4},{6,7},{7,6},{8,9},{9,8},{10,11... | collective-permute-start | bytes 442376 | tf_op jit(solution)/shard_map/ppermute | solution.py:635
  26.8 1.5 %collective-permute-start.3 = (bf16[432,256]{1,0:T(8,128)(2,1)S(1)}, bf16[432,256]{1,0:T(8,128)(2,1)S(1)}, u32[]{:S(2)}, u32[]{:S(2)}) collective-permute-start(bf16[432,256]{1,0:T(8,128)(2,1)S(1)} %get-tuple-element.83), channel_id=1, source_target_pairs={{0,1},{1,0},{2,3},{3,2},{4,5},{5,4},{6,7},{7,6},{8,9},{9,8},{10,11... | collective-permute-start | bytes 663560 | tf_op jit(solution)/shard_map/ppermute | solution.py:635
  51.0 1.5 %collective-permute-start.4 = (bf16[8,104,128]{2,1,0:T(8,128)(2,1)S(1)}, bf16[8,104,128]{2,1,0:T(8,128)(2,1)S(1)}, u32[]{:S(2)}, u32[]{:S(2)}) collective-permute-start(bf16[8,104,128]{2,1,0:T(8,128)(2,1)S(1)} %all_to_all.17.mine_ref), channel_id=1, source_target_pairs={{0,1},{1,0},{2,3},{3,2},{4,5},{5,4},{6,7},{7,6},{8,9},{9,8},{10,11... | collective-permute-start | bytes 638984 | tf_op jit(solution)/shard_map/ppermute | solution.py:635

commit v8 on v7

--- a/solution.py
+++ b/solution.py
@@ -343,6 +343,10 @@
     grad_updated_near = grad_updated.astype(BF16)
     grad_dst = slopes_sum_ref[...] * dot_nt(grad_updated_near, weights_ref[2])
     grad_summed = dot_nt(weights_ref[2], grad_updated_near).astype(BF16)
+    bias1 = jnp.sum(grad_dst, 0, keepdims=True)
+    grad_dst = grad_dst.astype(BF16)
+    grads_ref[width : 2 * width, :] = dot_tn(nodes, grad_dst).astype(BF16)
+    grads_ref[2 * width : 3 * width, :] = dot_tn(summed_ref[...], grad_updated_near).astype(BF16)
     chunk = 2 * EDGE_BLOCK
     grad_src = jnp.zeros((outof_ref.shape[0], width), F32)
     for start in range(0, slots, chunk):
@@ -351,15 +355,11 @@
         edge = (dot(grad_summed, into_ref[:, span]) * slope).astype(BF16)
         grad_src = grad_src + dot_nt(outof_ref[:, span], edge)
     grad_src = grad_src.astype(BF16)
-    bias1 = jnp.sum(grad_dst, 0, keepdims=True)
-    grad_dst = grad_dst.astype(BF16)
     grad_src_ref[...] = grad_src
     grad_dst_ref[...] = grad_dst
     low = dot_nt(grad_src[:rim], weights_ref[0]).astype(BF16)
     high = dot_nt(grad_src[rim + node_count :], weights_ref[0]).astype(BF16)
     grads_ref[0:width, :] = dot_tn(extended, grad_src).astype(BF16)
-    grads_ref[width : 2 * width, :] = dot_tn(nodes, grad_dst).astype(BF16)
-    grads_ref[2 * width : 3 * width, :] = dot_tn(summed_ref[...], grad_updated_near).astype(BF16)
     if grads_ref.shape[0] > 3 * width:
         grads_ref[3 * width :, :] = jnp.zeros((grads_ref.shape[0] - 3 * width, width), BF16)
     half = grads_ref.shape[0] // 2
@@ -664,7 +664,7 @@
         coarse_ends,
     ) = call(
         pick_kernel,
-        [rim_rows, ((4 * rim, width), BF16)] + [(value.shape, value.dtype) for value in inputs],
+        [rim_rows, ((3 * rim, width), BF16)] + [(value.shape, value.dtype) for value in inputs],
         inputs,
         4,
         outside=range(len(inputs)),

time: 53.7 us -> 53.7 us (level)
  no operation moved by 1% of the time
where the time goes in v8:
time: 53.7 us; the launch traced here: 53.4 us
  blocking collectives  35.5 us (66%)
  Pallas kernels  9.26 us (17%)
  starting transfers between devices  5.27 us (10%)
  waiting for transfers between devices  2.01 us (4%)
  between operations  1.37 us (3%)
    all_to_all x3, blocking collectives, exchange(): return lax.all_to_all(value, 'dom', 0, 0, axis_index_groups=same_core)  35.5 us
    pallas_call x10, Pallas kernels, call(): pl.pallas_call(kernel, out_shape=[jax.ShapeDtypeStruct(shape, kind) for s...  9.26 us
    ppermute x4, starting transfers between devices, swap(): return lax.ppermute(value, 'dom', pairs)  4.61 us
    ppermute x4, waiting for transfers between devices, swap(): return lax.ppermute(value, 'dom', pairs)  2.01 us
  transfers between devices with their start and end apart: 5, of which 3 were waited for; matrix products, arithmetic and copies ran while one was open for 0% of the time, Pallas kernels for 6%

profile of v8, /device:TPU:0, one launch (start us, length us, event | category | flops | bytes accessed | tf_op | source)
XLA Modules:
  0.0 53.4 jit_solution(6231681711313998745)
XLA Ops:
  0.6 1.1 %shard_map.146 = (bf16[16,256]{1,0:T(8,128)(2,1)S(1)}, bf16[48,256]{1,0:T(8,128)(2,1)S(1)}, bf16[128,256]{1,0:T(8,128)(2,1)S(1)}, s32[2,16]{1,0:T(2,128)S(1)}, b...) custom-call(bf16[128,256]{1,0:T(8,128)(2,1)} %refs_0_.1, ...), custom_call_target="tpu_custom_call" | custom-call | bytes 1113088 | tf_op jit(solution)/shard_map/pallas_call | solution.py:592
  1.8 0.7 %collective-permute-start.1 = (bf16[48,256]{1,0:T(8,128)(2,1)S(1)}, bf16[48,256]{1,0:T(8,128)(2,1)S(1)}, u32[]{:S(2)}, u32[]{:S(2)}) collective-permute-start(bf16[48,256]{1,0:T(8,128)(2,1)S(1)} %get-tuple-element.58), channel_id=1, source_target_pairs={{1,2},{3,4},{5,6},{7,8},{9,10},{11,12},{13,14},{2,1},{4,3},{6,5},{... | collective-permute-start | bytes 73736 | tf_op jit(solution)/shard_map/ppermute | solution.py:673
  2.5 4.4 %collective-permute-start = (bf16[16,256]{1,0:T(8,128)(2,1)S(1)}, bf16[16,256]{1,0:T(8,128)(2,1)S(1)}, u32[]{:S(2)}, u32[]{:S(2)}) collective-permute-start(bf16[16,256]{1,0:T(8,128)(2,1)S(1)} %get-tuple-element.57), channel_id=1, source_target_pairs={{0,1},{1,0},{2,3},{3,2},{4,5},{5,4},{6,7},{7,6},{8,9},{9,8},{10,11... | collective-permute-start | bytes 24584 | tf_op jit(solution)/shard_map/ppermute | solution.py:635
  7.5 0.9 %shard_map.147 = (f32[256,1536]{1,0:T(8,128)S(1)}, bf16[160,1536]{1,0:T(8,128)(2,1)S(1)}, bf16[128,1536]{1,0:T(8,128)(2,1)S(1)}, bf16[128,16]{1,0:T(8,128)(2,1)S...) custom-call(bf16[128,256]{1,0:T(8,128)(2,1)S(1)} %get-tuple-element., ...), custom_call_target="tpu_custom_call" | custom-call | flops 226492416 | bytes 3163524 | tf_op jit(solution)/shard_map/pallas_call | solution.py:592
  8.4 0.0 collective-permute-done.near_ref
  8.4 0.0 collective-permute-done.1.far_ref
  8.4 0.0 copy-start
  8.4 1.3 %shard_map.148 = (bf16[128,256]{1,0:T(8,128)(2,1)S(1)}, bf16[256,1536]{1,0:T(8,128)(2,1)S(1)}, bf16[8,72,128]{2,1,0:T(8,128)(2,1)S(1)}) custom-call(bf16[16,256]{1,0:T(8,128)(2,1)S(1)} %collective-permute-done.near_ref, bf16[48,256]{1,0:T(8,128)(2,1)S(1)} %collective-permute-done.1.far_ref, bf16[256,256]{1,0:T(8,128)(2,1)S(1)} %get-tuple-element.67.upright_ref, ...), custom_call_target="tpu_custom_call" | custom-call | bytes 4044800 | tf_op jit(solution)/shard_map/pallas_call | solution.py:592
  9.7 13.0 %all_to_all.15.mine_ref = bf16[8,72,128]{2,1,0:T(8,128)(2,1)S(1)} all-to-all(bf16[8,72,128]{2,1,0:T(8,128)(2,1)S(1)} %get-tuple-element.74), channel_id=1, replica_groups={{0,2,4,6,8,10,12,14},{1,3,5,7,9,11,13,15},{16,18,20,22,24,26,28,30},{17..., dimensions={0} | all-to-all | bytes 294912 | tf_op jit(solution)/shard_map/all_to_all | solution.py:638
  22.8 0.0 collective-permute-start.2
  22.8 0.0 copy-done
  22.8 0.4 shard_map.149
  23.2 0.9 %collective-permute-done.2.theirs_ref = bf16[8,72,128]{2,1,0:T(8,128)(2,1)S(1)} collective-permute-done((bf16[8,72,128]{2,1,0:T(8,128)(2,1)S(1)}, bf16[8,72,128]{2,1,0:T(8,128)(2,1)S(1)}, u32[]{:S(2)}, u32[]{:S(2)}) %collective-permute-start.2) | collective-permute-done | bytes 147488 | tf_op jit(solution)/shard_map/ppermute | solution.py:635
  24.2 2.6 %shard_map.150 = (bf16[432,256]{1,0:T(8,128)(2,1)S(1)}, bf16[400,256]{1,0:T(8,128)(2,1)S(1)}, bf16[256,256]{1,0:T(8,128)(2,1)S(1)}, bf16[256,256]{1,0:T(8,128)(2...) custom-call(bf16[8,72,128]{2,1,0:T(8,128)(2,1)S(1)} %all_to_all.15.m, ...), custom_call_target="tpu_custom_call" | custom-call | bytes 5597184 | tf_op jit(solution)/shard_map/pallas_call | solution.py:592
  26.7 0.2 collective-permute-start.3
  27.0 0.6 %shard_map.151 = (f32[3,256,256]{2,1,0:T(8,128)S(1)}, bf16[256,256]{1,0:T(8,128)(2,1)S(1)}) custom-call(bf16[256,256]{1,0:T(8,128)(2,1)S(1)} %get-tuple-element.84.coarse_ref, bf16[256,256]{1,0:T(8,128)(2,1)S(1)} %get-tuple-element.85.parent_ref, bf16[256,768]{1,0:T(8,128)(2,1)S(1)} %get-tuple-element.86.into2_ref, ...), custom_call_target="tpu_custom_call" | custom-call | flops 100663296 | bytes 2228224 | tf_op jit(solution)/shard_map/pallas_call | solution.py:592
  27.6 0.7 %collective-permute-done.3.came_ref = bf16[432,256]{1,0:T(8,128)(2,1)S(1)} collective-permute-done((bf16[432,256]{1,0:T(8,128)(2,1)S(1)}, bf16[432,256]{1,0:T(8,128)(2,1)S(1)}, u32[]{:S(2)}, u32[]{:S(2)}) %collective-permute-start.3) | collective-permute-done | bytes 221216 | tf_op jit(solution)/shard_map/ppermute | solution.py:635
  28.3 0.1 shard_map.152
  28.4 11.2 %all_to_all.16.blocks_ref = bf16[8,104,128]{2,1,0:T(8,128)(2,1)S(1)} all-to-all(bf16[8,104,128]{2,1,0:T(8,128)(2,1)S(1)} %shard_map.152), channel_id=1, replica_groups={{0,2,4,6,8,10,12,14},{1,3,5,7,9,11,13,15},{16,18,20,22,24,26,28,30},{17..., dimensions={0} | all-to-all | bytes 425984 | tf_op jit(solution)/shard_map/all_to_all | solution.py:638
  39.7 11.3 %all_to_all.17.mine_ref = bf16[8,104,128]{2,1,0:T(8,128)(2,1)S(1)} all-to-all(bf16[8,104,128]{2,1,0:T(8,128)(2,1)S(1)} %get-tuple-element.91), channel_id=1, replica_groups={{0,2,4,6,8,10,12,14},{1,3,5,7,9,11,13,15},{16,18,20,22,24,26,28,30},{17..., dimensions={0} | all-to-all | bytes 425984 | tf_op jit(solution)/shard_map/all_to_all | solution.py:638
  50.9 0.0 collective-permute-start.4
  50.9 1.1 %shard_map.154 = (f32[128,256]{1,0:T(8,128)S(1)}, f32[128,256]{1,0:T(8,128)S(1)}, f32[2,256]{1,0:T(2,128)S(1)}, f32[3,256,256]{2,1,0:T(8,128)}) custom-call(bf16[3,256,256]{2,1,0:T(8,128)(2,1)S(1)} %copy-done, bf16[3,256,256]{2,1,0:T(8,128)(2,1)S(1)} %get-tuple-element.60.weights_ref, bf16[256,256]{1,0:T(8,128)(2,1)S(1)} %get-tuple-element.84.coarse_ref, ...), custom_call_target="tpu_custom_call" | custom-call | flops 67108864 | bytes 3735680 | tf_op jit(solution)/shard_map/pallas_call | solution.py:592
  52.0 0.3 collective-permute-done.4.theirs_ref
  52.4 1.0 %shard_map.155 = (f32[768,256]{1,0:T(8,128)}, f32[128,256]{1,0:T(8,128)}, f32[128,256]{1,0:T(8,128)}, f32[2,256]{1,0:T(2,128)}) custom-call(bf16[8,104,128]{2,1,0:T(8,128)(2,1)S(1)} %all_to_all.17.mine_ref, bf16[8,104,128]{2,1,0:T(8,128)(2,1)S(1)} %collective-permute-done.4.theirs_ref, f32[128,256]{1,0:T(8,128)S(1)} %get-tuple-element.101.moved_ref, ...), custom_call_target="tpu_custom_call" | custom-call | bytes 1740800 | tf_op jit(solution)/shard_map/pallas_call | solution.py:592
  (1 shorter events, 0.0 us)
Async XLA Ops:
  1.8 6.6 %collective-permute-start.1 = (bf16[48,256]{1,0:T(8,128)(2,1)S(1)}, bf16[48,256]{1,0:T(8,128)(2,1)S(1)}, u32[]{:S(2)}, u32[]{:S(2)}) collective-permute-start(bf16[48,256]{1,0:T(8,128)(2,1)S(1)} %get-tuple-element.58), channel_id=1, source_target_pairs={{1,2},{3,4},{5,6},{7,8},{9,10},{11,12},{13,14},{2,1},{4,3},{6,5},{... | collective-permute-start | bytes 73736 | tf_op jit(solution)/shard_map/ppermute | solution.py:673
  2.5 5.9 %collective-permute-start = (bf16[16,256]{1,0:T(8,128)(2,1)S(1)}, bf16[16,256]{1,0:T(8,128)(2,1)S(1)}, u32[]{:S(2)}, u32[]{:S(2)}) collective-permute-start(bf16[16,256]{1,0:T(8,128)(2,1)S(1)} %get-tuple-element.57), channel_id=1, source_target_pairs={{0,1},{1,0},{2,3},{3,2},{4,5},{5,4},{6,7},{7,6},{8,9},{9,8},{10,11... | collective-permute-start | bytes 24584 | tf_op jit(solution)/shard_map/ppermute | solution.py:635
  8.4 14.4 %copy-start = (bf16[3,256,256]{2,1,0:T(8,128)(2,1)S(1)}, bf16[3,256,256]{2,1,0:T(8,128)(2,1)}, u32[]{:S(2)}) copy-start(bf16[3,256,256]{2,1,0:T(8,128)(2,1)} %coarse_weights_ref.5) | copy-start | bytes 1179652
  22.8 1.4 %collective-permute-start.2 = (bf16[8,72,128]{2,1,0:T(8,128)(2,1)S(1)}, bf16[8,72,128]{2,1,0:T(8,128)(2,1)S(1)}, u32[]{:S(2)}, u32[]{:S(2)}) collective-permute-start(bf16[8,72,128]{2,1,0:T(8,128)(2,1)S(1)} %all_to_all.15.mine_ref), channel_id=1, source_target_pairs={{0,1},{1,0},{2,3},{3,2},{4,5},{5,4},{6,7},{7,6},{8,9},{9,8},{10,11... | collective-permute-start | bytes 442376 | tf_op jit(solution)/shard_map/ppermute | solution.py:635
  26.7 1.5 %collective-permute-start.3 = (bf16[432,256]{1,0:T(8,128)(2,1)S(1)}, bf16[432,256]{1,0:T(8,128)(2,1)S(1)}, u32[]{:S(2)}, u32[]{:S(2)}) collective-permute-start(bf16[432,256]{1,0:T(8,128)(2,1)S(1)} %get-tuple-element.83), channel_id=1, source_target_pairs={{0,1},{1,0},{2,3},{3,2},{4,5},{5,4},{6,7},{7,6},{8,9},{9,8},{10,11... | collective-permute-start | bytes 663560 | tf_op jit(solution)/shard_map/ppermute | solution.py:635
  50.9 1.5 %collective-permute-start.4 = (bf16[8,104,128]{2,1,0:T(8,128)(2,1)S(1)}, bf16[8,104,128]{2,1,0:T(8,128)(2,1)S(1)}, u32[]{:S(2)}, u32[]{:S(2)}) collective-permute-start(bf16[8,104,128]{2,1,0:T(8,128)(2,1)S(1)} %all_to_all.17.mine_ref), channel_id=1, source_target_pairs={{0,1},{1,0},{2,3},{3,2},{4,5},{5,4},{6,7},{7,6},{8,9},{9,8},{10,11... | collective-permute-start | bytes 638984 | tf_op jit(solution)/shard_map/ppermute | solution.py:635

commit v9 on v8

--- a/solution.py
+++ b/solution.py
@@ -317,8 +317,8 @@
         message2_ref[:, span] = message.astype(BF16)
         slope2_ref[:, span] = slope.astype(BF16)
         edge2_ref[:, span] = (dot(grad_agg2_near, into) * slope).astype(BF16)
+    grad_src2 = dot_nt(outof2_ref[...], edge2_ref[...])
     grad_dst2 = dot_nt(into2_ref[...], slope2_ref[...]) * grad_agg2
-    grad_src2 = dot_nt(outof2_ref[...], edge2_ref[...])
     bias2_ref[...] = jnp.sum(grad_dst2, 0, keepdims=True)
     grad_src2_ref[...] = grad_src2.astype(BF16)
     grad_dst2_ref[...] = grad_dst2.astype(BF16)

time: 53.7 us -> 53.7 us (level)
  no operation moved by 1% of the time
where the time goes in v9:
time: 53.7 us; the launch traced here: 53.4 us
  blocking collectives  35.5 us (66%)
  Pallas kernels  9.25 us (17%)
  starting transfers between devices  5.26 us (10%)
  waiting for transfers between devices  2.02 us (4%)
  between operations  1.37 us (3%)
    all_to_all x3, blocking collectives, exchange(): return lax.all_to_all(value, 'dom', 0, 0, axis_index_groups=same_core)  35.5 us
    pallas_call x10, Pallas kernels, call(): pl.pallas_call(kernel, out_shape=[jax.ShapeDtypeStruct(shape, kind) for s...  9.25 us
    ppermute x4, starting transfers between devices, swap(): return lax.ppermute(value, 'dom', pairs)  4.6 us
    ppermute x4, waiting for transfers between devices, swap(): return lax.ppermute(value, 'dom', pairs)  2.01 us
  transfers between devices with their start and end apart: 5, of which 3 were waited for; matrix products, arithmetic and copies ran while one was open for 0% of the time, Pallas kernels for 6%

profile of v9, /device:TPU:0, one launch (start us, length us, event | category | flops | bytes accessed | tf_op | source)
XLA Modules:
  0.0 53.4 jit_solution(13388346797342960776)
XLA Ops:
  0.6 1.1 %shard_map.146 = (bf16[16,256]{1,0:T(8,128)(2,1)S(1)}, bf16[48,256]{1,0:T(8,128)(2,1)S(1)}, bf16[128,256]{1,0:T(8,128)(2,1)S(1)}, s32[2,16]{1,0:T(2,128)S(1)}, b...) custom-call(bf16[128,256]{1,0:T(8,128)(2,1)} %refs_0_.1, ...), custom_call_target="tpu_custom_call" | custom-call | bytes 1113088 | tf_op jit(solution)/shard_map/pallas_call | solution.py:592
  1.8 0.7 %collective-permute-start.1 = (bf16[48,256]{1,0:T(8,128)(2,1)S(1)}, bf16[48,256]{1,0:T(8,128)(2,1)S(1)}, u32[]{:S(2)}, u32[]{:S(2)}) collective-permute-start(bf16[48,256]{1,0:T(8,128)(2,1)S(1)} %get-tuple-element.58), channel_id=1, source_target_pairs={{1,2},{3,4},{5,6},{7,8},{9,10},{11,12},{13,14},{2,1},{4,3},{6,5},{... | collective-permute-start | bytes 73736 | tf_op jit(solution)/shard_map/ppermute | solution.py:673
  2.5 4.4 %collective-permute-start = (bf16[16,256]{1,0:T(8,128)(2,1)S(1)}, bf16[16,256]{1,0:T(8,128)(2,1)S(1)}, u32[]{:S(2)}, u32[]{:S(2)}) collective-permute-start(bf16[16,256]{1,0:T(8,128)(2,1)S(1)} %get-tuple-element.57), channel_id=1, source_target_pairs={{0,1},{1,0},{2,3},{3,2},{4,5},{5,4},{6,7},{7,6},{8,9},{9,8},{10,11... | collective-permute-start | bytes 24584 | tf_op jit(solution)/shard_map/ppermute | solution.py:635
  7.5 0.9 %shard_map.147 = (f32[256,1536]{1,0:T(8,128)S(1)}, bf16[160,1536]{1,0:T(8,128)(2,1)S(1)}, bf16[128,1536]{1,0:T(8,128)(2,1)S(1)}, bf16[128,16]{1,0:T(8,128)(2,1)S...) custom-call(bf16[128,256]{1,0:T(8,128)(2,1)S(1)} %get-tuple-element., ...), custom_call_target="tpu_custom_call" | custom-call | flops 226492416 | bytes 3163524 | tf_op jit(solution)/shard_map/pallas_call | solution.py:592
  8.4 0.0 collective-permute-done.near_ref
  8.4 0.0 collective-permute-done.1.far_ref
  8.4 0.0 copy-start
  8.4 1.3 %shard_map.148 = (bf16[128,256]{1,0:T(8,128)(2,1)S(1)}, bf16[256,1536]{1,0:T(8,128)(2,1)S(1)}, bf16[8,72,128]{2,1,0:T(8,128)(2,1)S(1)}) custom-call(bf16[16,256]{1,0:T(8,128)(2,1)S(1)} %collective-permute-done.near_ref, bf16[48,256]{1,0:T(8,128)(2,1)S(1)} %collective-permute-done.1.far_ref, bf16[256,256]{1,0:T(8,128)(2,1)S(1)} %get-tuple-element.67.upright_ref, ...), custom_call_target="tpu_custom_call" | custom-call | bytes 4044800 | tf_op jit(solution)/shard_map/pallas_call | solution.py:592
  9.7 13.0 %all_to_all.15.mine_ref = bf16[8,72,128]{2,1,0:T(8,128)(2,1)S(1)} all-to-all(bf16[8,72,128]{2,1,0:T(8,128)(2,1)S(1)} %get-tuple-element.74), channel_id=1, replica_groups={{0,2,4,6,8,10,12,14},{1,3,5,7,9,11,13,15},{16,18,20,22,24,26,28,30},{17..., dimensions={0} | all-to-all | bytes 294912 | tf_op jit(solution)/shard_map/all_to_all | solution.py:638
  22.8 0.0 collective-permute-start.2
  22.8 0.0 copy-done
  22.8 0.4 shard_map.149
  23.2 0.9 %collective-permute-done.2.theirs_ref = bf16[8,72,128]{2,1,0:T(8,128)(2,1)S(1)} collective-permute-done((bf16[8,72,128]{2,1,0:T(8,128)(2,1)S(1)}, bf16[8,72,128]{2,1,0:T(8,128)(2,1)S(1)}, u32[]{:S(2)}, u32[]{:S(2)}) %collective-permute-start.2) | collective-permute-done | bytes 147488 | tf_op jit(solution)/shard_map/ppermute | solution.py:635
  24.2 2.6 %shard_map.150 = (bf16[432,256]{1,0:T(8,128)(2,1)S(1)}, bf16[400,256]{1,0:T(8,128)(2,1)S(1)}, bf16[256,256]{1,0:T(8,128)(2,1)S(1)}, bf16[256,256]{1,0:T(8,128)(2...) custom-call(bf16[8,72,128]{2,1,0:T(8,128)(2,1)S(1)} %all_to_all.15.m, ...), custom_call_target="tpu_custom_call" | custom-call | bytes 5597184 | tf_op jit(solution)/shard_map/pallas_call | solution.py:592
  26.7 0.2 collective-permute-start.3
  26.9 0.6 %shard_map.151 = (f32[3,256,256]{2,1,0:T(8,128)S(1)}, bf16[256,256]{1,0:T(8,128)(2,1)S(1)}) custom-call(bf16[256,256]{1,0:T(8,128)(2,1)S(1)} %get-tuple-element.84.coarse_ref, bf16[256,256]{1,0:T(8,128)(2,1)S(1)} %get-tuple-element.85.parent_ref, bf16[256,768]{1,0:T(8,128)(2,1)S(1)} %get-tuple-element.86.into2_ref, ...), custom_call_target="tpu_custom_call" | custom-call | flops 100663296 | bytes 2228224 | tf_op jit(solution)/shard_map/pallas_call | solution.py:592
  27.6 0.7 %collective-permute-done.3.came_ref = bf16[432,256]{1,0:T(8,128)(2,1)S(1)} collective-permute-done((bf16[432,256]{1,0:T(8,128)(2,1)S(1)}, bf16[432,256]{1,0:T(8,128)(2,1)S(1)}, u32[]{:S(2)}, u32[]{:S(2)}) %collective-permute-start.3) | collective-permute-done | bytes 221216 | tf_op jit(solution)/shard_map/ppermute | solution.py:635
  28.3 0.1 shard_map.152
  28.4 11.2 %all_to_all.16.blocks_ref = bf16[8,104,128]{2,1,0:T(8,128)(2,1)S(1)} all-to-all(bf16[8,104,128]{2,1,0:T(8,128)(2,1)S(1)} %shard_map.152), channel_id=1, replica_groups={{0,2,4,6,8,10,12,14},{1,3,5,7,9,11,13,15},{16,18,20,22,24,26,28,30},{17..., dimensions={0} | all-to-all | bytes 425984 | tf_op jit(solution)/shard_map/all_to_all | solution.py:638
  39.7 11.3 %all_to_all.17.mine_ref = bf16[8,104,128]{2,1,0:T(8,128)(2,1)S(1)} all-to-all(bf16[8,104,128]{2,1,0:T(8,128)(2,1)S(1)} %get-tuple-element.91), channel_id=1, replica_groups={{0,2,4,6,8,10,12,14},{1,3,5,7,9,11,13,15},{16,18,20,22,24,26,28,30},{17..., dimensions={0} | all-to-all | bytes 425984 | tf_op jit(solution)/shard_map/all_to_all | solution.py:638
  50.9 0.0 collective-permute-start.4
  50.9 1.1 %shard_map.154 = (f32[128,256]{1,0:T(8,128)S(1)}, f32[128,256]{1,0:T(8,128)S(1)}, f32[2,256]{1,0:T(2,128)S(1)}, f32[3,256,256]{2,1,0:T(8,128)}) custom-call(bf16[3,256,256]{2,1,0:T(8,128)(2,1)S(1)} %copy-done, bf16[3,256,256]{2,1,0:T(8,128)(2,1)S(1)} %get-tuple-element.60.weights_ref, bf16[256,256]{1,0:T(8,128)(2,1)S(1)} %get-tuple-element.84.coarse_ref, ...), custom_call_target="tpu_custom_call" | custom-call | flops 67108864 | bytes 3735680 | tf_op jit(solution)/shard_map/pallas_call | solution.py:592
  52.0 0.3 collective-permute-done.4.theirs_ref
  52.4 1.0 %shard_map.155 = (f32[768,256]{1,0:T(8,128)}, f32[128,256]{1,0:T(8,128)}, f32[128,256]{1,0:T(8,128)}, f32[2,256]{1,0:T(2,128)}) custom-call(bf16[8,104,128]{2,1,0:T(8,128)(2,1)S(1)} %all_to_all.17.mine_ref, bf16[8,104,128]{2,1,0:T(8,128)(2,1)S(1)} %collective-permute-done.4.theirs_ref, f32[128,256]{1,0:T(8,128)S(1)} %get-tuple-element.101.moved_ref, ...), custom_call_target="tpu_custom_call" | custom-call | bytes 1740800 | tf_op jit(solution)/shard_map/pallas_call | solution.py:592
  (1 shorter events, 0.0 us)
Async XLA Ops:
  1.8 6.6 %collective-permute-start.1 = (bf16[48,256]{1,0:T(8,128)(2,1)S(1)}, bf16[48,256]{1,0:T(8,128)(2,1)S(1)}, u32[]{:S(2)}, u32[]{:S(2)}) collective-permute-start(bf16[48,256]{1,0:T(8,128)(2,1)S(1)} %get-tuple-element.58), channel_id=1, source_target_pairs={{1,2},{3,4},{5,6},{7,8},{9,10},{11,12},{13,14},{2,1},{4,3},{6,5},{... | collective-permute-start | bytes 73736 | tf_op jit(solution)/shard_map/ppermute | solution.py:673
  2.5 5.9 %collective-permute-start = (bf16[16,256]{1,0:T(8,128)(2,1)S(1)}, bf16[16,256]{1,0:T(8,128)(2,1)S(1)}, u32[]{:S(2)}, u32[]{:S(2)}) collective-permute-start(bf16[16,256]{1,0:T(8,128)(2,1)S(1)} %get-tuple-element.57), channel_id=1, source_target_pairs={{0,1},{1,0},{2,3},{3,2},{4,5},{5,4},{6,7},{7,6},{8,9},{9,8},{10,11... | collective-permute-start | bytes 24584 | tf_op jit(solution)/shard_map/ppermute | solution.py:635
  8.4 14.4 %copy-start = (bf16[3,256,256]{2,1,0:T(8,128)(2,1)S(1)}, bf16[3,256,256]{2,1,0:T(8,128)(2,1)}, u32[]{:S(2)}) copy-start(bf16[3,256,256]{2,1,0:T(8,128)(2,1)} %coarse_weights_ref.5) | copy-start | bytes 1179652
  22.8 1.4 %collective-permute-start.2 = (bf16[8,72,128]{2,1,0:T(8,128)(2,1)S(1)}, bf16[8,72,128]{2,1,0:T(8,128)(2,1)S(1)}, u32[]{:S(2)}, u32[]{:S(2)}) collective-permute-start(bf16[8,72,128]{2,1,0:T(8,128)(2,1)S(1)} %all_to_all.15.mine_ref), channel_id=1, source_target_pairs={{0,1},{1,0},{2,3},{3,2},{4,5},{5,4},{6,7},{7,6},{8,9},{9,8},{10,11... | collective-permute-start | bytes 442376 | tf_op jit(solution)/shard_map/ppermute | solution.py:635
  26.7 1.5 %collective-permute-start.3 = (bf16[432,256]{1,0:T(8,128)(2,1)S(1)}, bf16[432,256]{1,0:T(8,128)(2,1)S(1)}, u32[]{:S(2)}, u32[]{:S(2)}) collective-permute-start(bf16[432,256]{1,0:T(8,128)(2,1)S(1)} %get-tuple-element.83), channel_id=1, source_target_pairs={{0,1},{1,0},{2,3},{3,2},{4,5},{5,4},{6,7},{7,6},{8,9},{9,8},{10,11... | collective-permute-start | bytes 663560 | tf_op jit(solution)/shard_map/ppermute | solution.py:635
  50.9 1.5 %collective-permute-start.4 = (bf16[8,104,128]{2,1,0:T(8,128)(2,1)S(1)}, bf16[8,104,128]{2,1,0:T(8,128)(2,1)S(1)}, u32[]{:S(2)}, u32[]{:S(2)}) collective-permute-start(bf16[8,104,128]{2,1,0:T(8,128)(2,1)S(1)} %all_to_all.17.mine_ref), channel_id=1, source_target_pairs={{0,1},{1,0},{2,3},{3,2},{4,5},{5,4},{6,7},{7,6},{8,9},{9,8},{10,11... | collective-permute-start | bytes 638984 | tf_op jit(solution)/shard_map/ppermute | solution.py:635
